TPU v7x, 128 devices: a whole 4x4x4 slice. The times are simulated.
128 devices in a mesh: fsdp: 32 (over x, z, core), tensor: 4 (over y).
Axes of the slice: x: 4, y: 4, z: 4, core: 2. Of those that a mesh axis runs over, the one named last changes fastest.
Arguments:
- tokens: bfloat16 [2, 2048, 2048], P(None, 'fsdp'), may hold values from -6 to 6
- segment: int32 [2, 2048], replicated, may hold values from 0 to 2, as said below
- routes: int32 [2, 2048, 6], P(None, 'fsdp'), may hold values from 0 to 7, all different within a row
- cotangent: bfloat16 [2, 2048, 2048], P(None, 'fsdp'), may hold values from -6 to 6
- gain_attn: bfloat16 [2048], P('fsdp'), may hold values from 0.5 to 1.5
- w_query: bfloat16 [2048, 3072], P('fsdp', 'tensor'), may hold values from -0.125 to 0.125
- w_compress: bfloat16 [2048, 576], P('fsdp'), may hold values from -0.125 to 0.125
- gain_latent: bfloat16 [512], P('fsdp'), may hold values from 0.5 to 1.5
- w_expand: bfloat16 [512, 4096], P('fsdp', 'tensor'), may hold values from -0.25 to 0.25
- w_output: bfloat16 [2048, 2048], P('fsdp', 'tensor'), may hold values from -2 to 2
- gain_ffn: bfloat16 [2048], P('fsdp'), may hold values from 0.5 to 1.5
- w_router: bfloat16 [2048, 8], P('fsdp'), may hold values from -0.0625 to 0.0625
- w_expert_in: bfloat16 [2048, 8, 2, 1408], P('fsdp', None, None, 'tensor'), may hold values from -0.125 to 0.125
- w_expert_out: bfloat16 [2048, 8, 1408], P('fsdp', None, 'tensor'), may hold values from -0.625 to 0.625
- w_shared_in: bfloat16 [2048, 2, 2816], P('fsdp', None, 'tensor'), may hold values from -0.125 to 0.125
- w_shared_out: bfloat16 [2048, 2816], P('fsdp', 'tensor'), may hold values from -0.15625 to 0.15625
Outputs:
- mixed: bfloat16 [2, 2048, 2048], P(None, 'fsdp')
- grad_tokens: bfloat16 [2, 2048, 2048], P(None, 'fsdp')
- grad_gain_attn: float32 [2048], P('fsdp')
- grad_w_query: float32 [2048, 3072], P('fsdp', 'tensor')
- grad_w_compress: float32 [2048, 576], P('fsdp')
- grad_gain_latent: float32 [512], P('fsdp')
- grad_w_expand: float32 [512, 4096], P('fsdp', 'tensor')
- grad_w_output: float32 [2048, 2048], P('fsdp', 'tensor')
- grad_gain_ffn: float32 [2048], P('fsdp')
- grad_w_router: float32 [2048, 8], P('fsdp')
- grad_w_expert_in: float32 [2048, 8, 2, 1408], P('fsdp', None, None, 'tensor')
- grad_w_expert_out: float32 [2048, 8, 1408], P('fsdp', None, 'tensor')
- grad_w_shared_in: float32 [2048, 2, 2816], P('fsdp', None, 'tensor')
- grad_w_shared_out: float32 [2048, 2816], P('fsdp', 'tensor')
Inputs may be any that keep to these rules, and one draw needn't show every extreme that they name: `segment`: along each micro-batch the document numbers never fall; document 1 begins within the first 64 tokens and ends within the last 64. `routes`: each token names 6 different experts.
All inputs are finite; a program needn't handle non-finite values.
Results may differ from a plain program's by a relative error of at most 0.03.
Values may be sent and summed in bfloat16 or wider, within the bound.
No kernel may reach another device: no remote copies, remote signals or barrier semaphores. Data moves between devices by JAX's collectives and lax.ppermute only.
A program may use at most 256 MiB of HBM per device.

v0:
```python
import jax
import jax.numpy as jnp
from jax import lax
from jax.sharding import PartitionSpec as P

NOPE = 128
ROPE = 64
VHEAD = 128
RANK = 512
EXPERTS = 8


epsilon = 1e-06


def as_sent(shard):

    def short(part):
        return part.astype(jnp.bfloat16) if part.dtype == jnp.float32 else part

    return jax.tree.map(short, shard)


def rotate_parts(values, position, inverse):
    half = values.shape[-1] // 2
    freq = jnp.exp(jnp.arange(half, dtype=jnp.float32) * (-jnp.log(10000.0) / half))
    angle = position.astype(jnp.float32)[:, None] * freq[None, :]
    cosine = jnp.cos(angle)
    sine = jnp.sin(angle)
    if inverse:
        sine = -sine
    if values.ndim == 3:
        cosine = cosine[:, None, :]
        sine = sine[:, None, :]
    first = values[..., :half]
    second = values[..., half:]
    return jnp.concatenate(
        [first * cosine - second * sine, second * cosine + first * sine], axis=-1
    )


def norm_forward(values, gain):
    factor = lax.rsqrt(jnp.mean(values * values, axis=-1, keepdims=True) + epsilon)
    return (values * factor * gain, factor)


def norm_backward(values, factor, gain, grad):
    scaled = grad * gain
    d_values = factor * scaled - values * (factor * factor * factor) * jnp.mean(
        values * scaled, axis=-1, keepdims=True
    )
    d_gain = jnp.sum(grad * values * factor, axis=0)
    return (d_values, d_gain)


def silu_parts(values):
    sigma = jax.nn.sigmoid(values)
    return (values * sigma, sigma + values * sigma * (1.0 - sigma))


def on_device(
    tokens,
    segment,
    routes,
    cotangent,
    gain_attn,
    w_query,
    w_compress,
    gain_latent,
    w_expand,
    w_output,
    gain_ffn,
    w_router,
    w_expert_in,
    w_expert_out,
    w_shared_in,
    w_shared_out,
):
    micro_count, tok_rows, width = tokens.shape
    shards = lax.axis_size("fsdp")
    heads_here = w_query.shape[1] // (NOPE + ROPE)
    first_row = lax.axis_index("fsdp") * tok_rows
    position = first_row + jnp.arange(tok_rows, dtype=jnp.int32)
    scale = (NOPE + ROPE) ** (-0.5)

    def fetch_attention():
        return (
            lax.all_gather(gain_attn, "fsdp", axis=0, tiled=True),
            lax.all_gather(w_query, "fsdp", axis=0, tiled=True),
            lax.all_gather(w_compress, "fsdp", axis=0, tiled=True),
            lax.all_gather(gain_latent, "fsdp", axis=0, tiled=True),
            lax.all_gather(w_expand, "fsdp", axis=0, tiled=True),
            lax.all_gather(w_output, "fsdp", axis=0, tiled=True),
        )

    def fetch_ffn():
        return (
            lax.all_gather(gain_ffn, "fsdp", axis=0, tiled=True),
            lax.all_gather(w_router, "fsdp", axis=0, tiled=True),
            lax.all_gather(w_expert_in, "fsdp", axis=0, tiled=True),
            lax.all_gather(w_expert_out, "fsdp", axis=0, tiled=True),
            lax.all_gather(w_shared_in, "fsdp", axis=0, tiled=True),
            lax.all_gather(w_shared_out, "fsdp", axis=0, tiled=True),
        )

    def zeros_whole(local):
        return tuple(
            (
                jnp.zeros((piece.shape[0] * shards,) + piece.shape[1:], jnp.float32)
                for piece in local
            )
        )

    attn_grads = zeros_whole((gain_attn, w_query, w_compress, gain_latent, w_expand, w_output))
    ffn_grads = zeros_whole(
        (gain_ffn, w_router, w_expert_in, w_expert_out, w_shared_in, w_shared_out)
    )
    mixed_rows = []
    grad_rows = []
    for batch_index in range(micro_count):
        attn_now = fetch_attention()
        ffn_now = fetch_ffn()
        gain_one, query_w, compress_w, latent_gain, expand_w, output_w = attn_now
        inputs = tokens[batch_index].astype(jnp.float32)
        segment_row = segment[batch_index]
        segment_here = lax.dynamic_slice_in_dim(segment_row, first_row, tok_rows)
        gain_first = gain_one.astype(jnp.float32)
        normed_full, factor_one = norm_forward(inputs, gain_first)
        normed = normed_full.astype(jnp.bfloat16)
        q_raw = jnp.dot(normed, query_w, preferred_element_type=jnp.float32).reshape(
            tok_rows, heads_here, NOPE + ROPE
        )
        query = jnp.concatenate(
            [q_raw[..., :NOPE], rotate_parts(q_raw[..., NOPE:], position, False)], axis=-1
        ).astype(jnp.bfloat16)
        compressed = jnp.dot(normed, compress_w, preferred_element_type=jnp.float32)
        latent_gain_full = latent_gain.astype(jnp.float32)
        latent_full, factor_latent = norm_forward(compressed[:, :RANK], latent_gain_full)
        latent = latent_full.astype(jnp.bfloat16)
        key_own = rotate_parts(compressed[:, RANK:], position, False).astype(jnp.bfloat16)
        packed = jnp.concatenate([latent, key_own], axis=1)
        expand_piece = lax.all_gather(packed, "fsdp", axis=0, tiled=True)
        kv_rows = jnp.dot(
            expand_piece[:, :RANK], expand_w, preferred_element_type=jnp.float32
        ).astype(jnp.bfloat16)
        gathered = jnp.concatenate([expand_piece, kv_rows], axis=1)
        key_total = gathered.shape[0]
        key_rot = gathered[:, RANK : RANK + ROPE]
        key_value = gathered[:, RANK + ROPE :].reshape(key_total, heads_here, NOPE + VHEAD)
        key_nope = key_value[..., :NOPE]
        values_all = key_value[..., NOPE:]
        key_place = jnp.arange(key_total, dtype=jnp.int32)
        allowed = (position[:, None] >= key_place[None, :]) & (
            segment_here[:, None] == segment_row[None, :]
        )
        score = (
            jnp.einsum(
                "thd,khd->htk", query[..., :NOPE], key_nope, preferred_element_type=jnp.float32
            )
            + jnp.einsum(
                "thd,kd->htk", query[..., NOPE:], key_rot, preferred_element_type=jnp.float32
            )
        ) * scale
        score = jnp.where(allowed[None], score, -1e30)
        prob = jax.nn.softmax(score, axis=-1)
        prob_low = prob.astype(jnp.bfloat16)
        attended = (
            jnp.einsum("htk,khd->thd", prob_low, values_all, preferred_element_type=jnp.float32)
            .astype(jnp.bfloat16)
            .reshape(tok_rows, heads_here * VHEAD)
        )
        branch = lax.psum(
            jnp.einsum("tv,dv->td", attended, output_w, preferred_element_type=jnp.float32),
            "tensor",
        )
        middle = inputs + branch
        gain_two, router_w, expert_in, expert_out, shared_in_w, shared_out_w = ffn_now
        gain_second = gain_two.astype(jnp.float32)
        normed_ffn_full, factor_two = norm_forward(middle, gain_second)
        normed_ffn = normed_ffn_full.astype(jnp.bfloat16)
        router = jax.nn.softmax(
            jnp.dot(normed_ffn, router_w, preferred_element_type=jnp.float32), axis=-1
        )
        chosen = jnp.sum(
            (
                routes[batch_index][:, :, None]
                == jnp.arange(EXPERTS, dtype=jnp.int32)[None, None, :]
            ).astype(jnp.float32),
            axis=1,
        )
        gate = router * chosen
        gate_up = jnp.einsum(
            "td,degf->tegf", normed_ffn, expert_in, preferred_element_type=jnp.float32
        )
        silu_gate, silu_slope = silu_parts(gate_up[:, :, 0])
        gate_upper = gate_up[:, :, 1]
        weighted = (gate[:, :, None] * silu_gate * gate_upper).astype(jnp.bfloat16)
        shared_gu = jnp.einsum(
            "td,dgf->tgf", normed_ffn, shared_in_w, preferred_element_type=jnp.float32
        )
        shared_silu, shared_slope = silu_parts(shared_gu[:, 0])
        shared_act = (shared_silu * shared_gu[:, 1]).astype(jnp.bfloat16)
        partial_out = jnp.einsum(
            "tef,def->td", weighted, expert_out, preferred_element_type=jnp.float32
        ) + jnp.einsum("tf,df->td", shared_act, shared_out_w, preferred_element_type=jnp.float32)
        ffn_out = lax.psum(partial_out.astype(jnp.bfloat16), "tensor").astype(jnp.float32)
        mixed_rows.append((middle + ffn_out).astype(jnp.bfloat16))
        gain_two, router_w, expert_in, expert_out, shared_in_w, shared_out_w = fetch_ffn()
        d_out = cotangent[batch_index]
        d_weighted = jnp.einsum(
            "td,def->tef", d_out, expert_out, preferred_element_type=jnp.float32
        )
        d_gate_part = jnp.sum(d_weighted * silu_gate * gate_upper, axis=2)
        d_act = d_weighted * gate[:, :, None]
        d_gate_up = jnp.stack([d_act * gate_upper * silu_slope, d_act * silu_gate], axis=2).astype(
            jnp.bfloat16
        )
        d_shared_act = jnp.einsum(
            "td,df->tf", d_out, shared_out_w, preferred_element_type=jnp.float32
        )
        d_shared_in = jnp.stack(
            [d_shared_act * shared_gu[:, 1] * shared_slope, d_shared_act * shared_silu], axis=1
        ).astype(jnp.bfloat16)
        d_normed_part = jnp.einsum(
            "tegf,degf->td", d_gate_up, expert_in, preferred_element_type=jnp.float32
        ) + jnp.einsum("tgf,dgf->td", d_shared_in, shared_in_w, preferred_element_type=jnp.float32)
        d_normed_sum, d_gate = (
            lax.psum(d_normed_part.astype(jnp.bfloat16), "tensor").astype(jnp.float32),
            lax.psum(d_gate_part.astype(jnp.bfloat16), "tensor").astype(jnp.float32),
        )
        d_chosen = d_gate * chosen
        d_logits = (
            router * (d_chosen - jnp.sum(router * d_chosen, axis=-1, keepdims=True))
        ).astype(jnp.bfloat16)
        d_normed_ffn = d_normed_sum + jnp.einsum(
            "te,de->td", d_logits, router_w, preferred_element_type=jnp.float32
        )
        d_middle_norm, d_gain_two = norm_backward(middle, factor_two, gain_second, d_normed_ffn)
        d_middle = d_out.astype(jnp.float32) + d_middle_norm
        ffn_terms = (
            d_gain_two,
            jnp.einsum("td,te->de", normed_ffn, d_logits, preferred_element_type=jnp.float32),
            jnp.einsum("td,tegf->degf", normed_ffn, d_gate_up, preferred_element_type=jnp.float32),
            jnp.einsum("td,tef->def", d_out, weighted, preferred_element_type=jnp.float32),
            jnp.einsum("td,tgf->dgf", normed_ffn, d_shared_in, preferred_element_type=jnp.float32),
            jnp.einsum("td,tf->df", d_out, shared_act, preferred_element_type=jnp.float32),
        )
        ffn_grads = tuple((total + term for total, term in zip(ffn_grads, ffn_terms)))
        gain_one, query_w, compress_w, latent_gain, expand_w, output_w = fetch_attention()
        d_branch = d_middle.astype(jnp.bfloat16)
        d_attended = (
            jnp.einsum("td,dv->tv", d_branch, output_w, preferred_element_type=jnp.float32)
            .astype(jnp.bfloat16)
            .reshape(tok_rows, heads_here, VHEAD)
        )
        d_prob = jnp.einsum(
            "thd,khd->htk", d_attended, values_all, preferred_element_type=jnp.float32
        )
        d_score = (prob * (d_prob - jnp.sum(prob * d_prob, axis=-1, keepdims=True))).astype(
            jnp.bfloat16
        )
        d_query_nope = (
            jnp.einsum("htk,khd->thd", d_score, key_nope, preferred_element_type=jnp.float32)
            * scale
        )
        d_query_rot = (
            jnp.einsum("htk,kd->thd", d_score, key_rot, preferred_element_type=jnp.float32) * scale
        )
        d_query = (
            jnp.concatenate([d_query_nope, rotate_parts(d_query_rot, position, True)], axis=-1)
            .astype(jnp.bfloat16)
            .reshape(tok_rows, heads_here * (NOPE + ROPE))
        )
        d_key_nope = (
            jnp.einsum(
                "htk,thd->khd", d_score, query[..., :NOPE], preferred_element_type=jnp.float32
            )
            * scale
        )
        d_key_rot = (
            jnp.einsum(
                "htk,thd->kd", d_score, query[..., NOPE:], preferred_element_type=jnp.float32
            )
            * scale
        )
        d_values = jnp.einsum(
            "htk,thd->khd", prob_low, d_attended, preferred_element_type=jnp.float32
        )
        key_terms = jnp.concatenate(
            [
                d_key_rot,
                jnp.concatenate([d_key_nope, d_values], axis=-1).reshape(
                    key_total, heads_here * (NOPE + VHEAD)
                ),
            ],
            axis=1,
        )
        own_terms = lax.psum_scatter(
            key_terms.astype(jnp.bfloat16), "fsdp", scatter_dimension=0, tiled=True
        ).astype(jnp.float32)
        d_expanded = own_terms[:, ROPE:].astype(jnp.bfloat16)
        d_latent_part = jnp.einsum(
            "tc,rc->tr", d_expanded, expand_w, preferred_element_type=jnp.float32
        )
        d_query_part = jnp.einsum("tq,dq->td", d_query, query_w, preferred_element_type=jnp.float32)
        d_normed_sum, d_latent, d_key_own = (
            lax.psum(d_query_part.astype(jnp.bfloat16), "tensor").astype(jnp.float32),
            lax.psum(d_latent_part.astype(jnp.bfloat16), "tensor").astype(jnp.float32),
            lax.psum(own_terms[:, :ROPE].astype(jnp.bfloat16), "tensor").astype(jnp.float32),
        )
        d_comp_latent, d_latent_gain = norm_backward(
            compressed[:, :RANK], factor_latent, latent_gain_full, d_latent
        )
        d_compressed = jnp.concatenate(
            [d_comp_latent, rotate_parts(d_key_own, position, True)], axis=1
        ).astype(jnp.bfloat16)
        d_normed = d_normed_sum + jnp.einsum(
            "tc,dc->td", d_compressed, compress_w, preferred_element_type=jnp.float32
        )
        d_inputs, d_gain_one = norm_backward(inputs, factor_one, gain_first, d_normed)
        grad_rows.append((d_middle + d_inputs).astype(jnp.bfloat16))
        attn_terms = (
            d_gain_one,
            jnp.einsum("td,tq->dq", normed, d_query, preferred_element_type=jnp.float32),
            jnp.einsum("td,tc->dc", normed, d_compressed, preferred_element_type=jnp.float32),
            d_latent_gain,
            jnp.einsum("tr,tc->rc", latent, d_expanded, preferred_element_type=jnp.float32),
            jnp.einsum("td,tv->dv", d_branch, attended, preferred_element_type=jnp.float32),
        )
        attn_grads = tuple((total + term for total, term in zip(attn_grads, attn_terms)))
    attn_owned = jax.tree.map(
        lambda part: part.astype(jnp.float32),
        lax.psum_scatter(as_sent(attn_grads), "fsdp", scatter_dimension=0, tiled=True),
    )
    ffn_owned = jax.tree.map(
        lambda part: part.astype(jnp.float32),
        lax.psum_scatter(as_sent(ffn_grads), "fsdp", scatter_dimension=0, tiled=True),
    )
    return (jnp.stack(mixed_rows), jnp.stack(grad_rows)) + tuple(attn_owned) + tuple(ffn_owned)


def solution(mesh):
    return jax.shard_map(
        on_device,
        mesh=mesh,
        in_specs=(
            P(None, "fsdp", None),
            P(),
            P(None, "fsdp", None),
            P(None, "fsdp", None),
            P("fsdp"),
            P("fsdp", "tensor"),
            P("fsdp", None),
            P("fsdp"),
            P("fsdp", "tensor"),
            P("fsdp", "tensor"),
            P("fsdp"),
            P("fsdp", None),
            P("fsdp", None, None, "tensor"),
            P("fsdp", None, "tensor"),
            P("fsdp", None, "tensor"),
            P("fsdp", "tensor"),
        ),
        out_specs=(
            P(None, "fsdp", None),
            P(None, "fsdp", None),
            P("fsdp"),
            P("fsdp", "tensor"),
            P("fsdp", None),
            P("fsdp"),
            P("fsdp", "tensor"),
            P("fsdp", "tensor"),
            P("fsdp"),
            P("fsdp", None),
            P("fsdp", None, None, "tensor"),
            P("fsdp", None, "tensor"),
            P("fsdp", None, "tensor"),
            P("fsdp", "tensor"),
        ),
        check_vma=False,
    )
```

profile of v0, /device:TPU:0, one launch (start us, length us, event | category | flops | bytes accessed | tf_op | source)
XLA Modules:
  0.0 1834.3 jit_solution(10623174751933198715)
XLA Ops:
  13.9 70.9 %all-reduce.8 = (bf16[2048]{0:T(1024)(128)(2,1)S(1)}, bf16[512]{0:T(512)(128)(2,1)S(1)}, bf16[2048]{0:T(1024)(128)(2,1)S(1)}) all-reduce(bf16[2048]{0:T(1024)(128)(2,1)S(1)} %dynamic-update-slice, bf16[512]{0:T(512)(128)(2,1)S(1)} %dynamic-update-slice.1, ...), channel_id=1, replica_groups=mesh['fsdp'=32,'tensor'=4] {'fsdp'}, use_global_device_ids=true, to_apply=%add | all-reduce | flops 4608 | bytes 18432
  96.2 7.9 all-gather.18.cloned.1.call-done
  104.1 4.8 copy.214
  108.9 3.2 fusion.189
  113.5 37.4 %all-gather.14.cloned.1.call-done = bf16[2048,576]{1,0:T(8,128)(2,1)} async-done(((bf16[64,576]{1,0:T(8,128)(2,1)}), bf16[2048,576]{1,0:T(8,128)(2,1)}) %all-gather.14.cloned.1.call-update) | async-done | bytes 2359312 | tf_op jit(solution)/shard_map/all_gather | solution.py:142
  152.4 42.8 %all-gather.16.cloned.1.call-done = bf16[512,1024]{1,0:T(8,128)(2,1)} async-done(((bf16[16,1024]{1,0:T(8,128)(2,1)}), bf16[512,1024]{1,0:T(8,128)(2,1)}) %all-gather.16.cloned.1.call-update) | async-done | bytes 1048592 | tf_op jit(solution)/shard_map/all_gather | solution.py:92
  195.2 4.3 convolution_convert_fusion.1
  204.5 3.9 fusion.66
  208.4 33.3 %all-gather.30.cloned.1.call-done = bf16[2048,576]{1,0:T(8,128)(2,1)} async-done(((bf16[64,576]{1,0:T(8,128)(2,1)}), bf16[2048,576]{1,0:T(8,128)(2,1)}) %all-gather.30.cloned.1.call-update) | async-done | bytes 2359312 | tf_op jit(solution)/shard_map/all_gather | solution.py:142
  243.3 4.0 convolution_convert_fusion
  254.4 32.7 %all-gather.20.cloned.1.call-done = bf16[2048,512]{1,0:T(8,128)(2,1)} async-done(((bf16[64,512]{1,0:T(8,128)(2,1)}), bf16[2048,512]{1,0:T(8,128)(2,1)}) %all-gather.20.cloned.1.call-update) | async-done | bytes 2097168 | tf_op jit(solution)/shard_map/all_gather | solution.py:93
  287.1 3.3 fusion.256
  295.9 23.5 %all-gather = bf16[32,64,8]{1,2,0:T(8,128)(2,1)S(1)} all-gather(bf16[1,64,8]{1,2,0:T(8,128)(2,1)S(1)} %bitcast.618), channel_id=1, replica_groups=mesh['fsdp'=32,'tensor'=4] {'fsdp'}, dimensions={0}, use_global_device_ids=true | all-gather | bytes 33792 | tf_op jit(solution)/shard_map/all_gather | solution.py:99
  319.6 17.7 all-reduce.17.cloned.1.call-done
  342.7 47.8 %all-gather.26.cloned.1.call-done = bf16[2048,2,704]{2,0,1:T(8,128)(2,1)} async-done(((bf16[64,2,704]{2,0,1:T(8,128)(2,1)}), bf16[2048,2,704]{2,0,1:T(8,128)(2,1)}) %all-gather.26.cloned.1.call-update) | async-done | bytes 5767184 | tf_op jit(solution)/shard_map/all_gather | solution.py:102
  390.6 4.0 fusion.187
  394.6 42.6 %all-gather.28.cloned.1.call-done = bf16[2048,704]{1,0:T(8,128)(2,1)} async-done(((bf16[64,704]{1,0:T(8,128)(2,1)}), bf16[2048,704]{1,0:T(8,128)(2,1)}) %all-gather.28.cloned.1.call-update) | async-done | bytes 2883600 | tf_op jit(solution)/shard_map/all_gather | solution.py:103
  437.2 3.2 fusion.248
  440.4 4.1 fusion.194
  446.6 85.1 %all-gather.22.cloned.1.call-done = bf16[2048,8,2,352]{3,0,2,1:T(8,128)(2,1)} async-done(((bf16[64,8,2,352]{3,0,2,1:T(8,128)(2,1)}), bf16[2048,8,2,352]{3,0,2,1:T(8,128)(2,1)}) %all-gather.22.cloned.1.call-update) | async-done | bytes 23068688 | tf_op jit(solution)/shard_map/all_gather | solution.py:100
  531.7 11.6 fusion.168
  543.3 11.9 fusion.171
  555.3 41.9 %all-gather.24.cloned.1.call-done = bf16[2048,8,352]{2,0,1:T(8,128)(2,1)} async-done(((bf16[64,8,352]{2,0,1:T(8,128)(2,1)}), bf16[2048,8,352]{2,0,1:T(8,128)(2,1)}) %all-gather.24.cloned.1.call-update) | async-done | bytes 11534352 | tf_op jit(solution)/shard_map/all_gather | solution.py:101
  597.1 9.0 fusion.152
  606.5 4.9 fusion.150
  611.4 11.6 all-reduce.10
  624.2 13.2 convolution_bitcast_fusion.7
  637.4 13.2 convolution_bitcast_fusion.9
  650.6 5.7 fusion.23
  656.4 5.5 fusion.22
  662.3 40.1 %all-reduce.21.cloned.1.call-done = (bf16[64,2048]{1,0:T(8,128)(2,1)}, bf16[64,2048]{1,0:T(8,128)(2,1)}) async-done(((bf16[64,2048]{1,0:T(8,128)(2,1)}, bf16[64,2048]{1,0:T(8,128)(2,1)}), (bf16[64,2048]{1,0:T(8,128)(2,1)}, bf16[64,2048]{1,0:T(8,128)(2,1)})) %all-reduce.21.cloned.1.call-update) | async-done | bytes 524304 | tf_op jit(solution)/shard_map/psum | solution.py:228
  708.7 4.4 fusion.7
  713.1 3.0 multiply_reduce_fusion
  719.2 2.6 pad_maximum_fusion.3
  721.8 6.4 copy.276
  730.2 7.1 pad_maximum_fusion.1
  739.9 4.4 fusion.6
  744.2 3.1 multiply_reduce_fusion.1
  750.3 2.6 pad_maximum_fusion.2
  753.0 6.5 copy.274
  763.8 7.3 pad_maximum_fusion
  771.8 9.2 convolution_bitcast_fusion.4
  782.8 9.0 convolution_bitcast_fusion.5
  800.7 21.2 %reduce-scatter.18.cloned.1.call-done = bf16[64,1088]{1,0:T(8,128)(2,1)} async-done(((bf16[2048,1088]{1,0:T(8,128)(2,1)}), bf16[64,1088]{1,0:T(8,128)(2,1)}) %reduce-scatter.18.cloned.1.call-update) | async-done | bytes 139280 | tf_op jit(solution)/shard_map/reduce_scatter | solution.py:298
  822.6 85.8 %reduce-scatter.16.cloned.1.call-done = bf16[64,1088]{1,0:T(8,128)(2,1)} async-done(((bf16[2048,1088]{1,0:T(8,128)(2,1)}), bf16[64,1088]{1,0:T(8,128)(2,1)}) %reduce-scatter.16.cloned.1.call-update) | async-done | bytes 139280 | tf_op jit(solution)/shard_map/reduce_scatter | solution.py:298
  909.2 17.1 all-reduce.9
  946.8 2.8 copy.279
  952.5 4.4 add_convert_fusion.2
  965.7 2.8 add_convert_fusion.3
  968.7 19.6 %all-reduce.19.cloned.1.call-done = (bf16[64,2048]{1,0:T(8,128)(2,1)}, bf16[64,2048]{1,0:T(8,128)(2,1)}, bf16[64,2048]{1,0:T(8,128)(2,1)}, bf16[64,512]{1,0:T(8,...) async-done(((bf16[64,2048]{1,0:T(8,128)(2,1)}, bf16[64,2048]{1,0:T(8,128)(2,1)}, bf16[64,2048]{1,0:T(8,128)(2,1)}, bf16[64,512]{1,0:T(8,128)(2,1)}, ...) | async-done | bytes 1179664 | tf_op jit(solution)/shard_map/psum | solution.py:206
  996.0 9.7 fusion.155
  1005.6 14.7 fusion.2
  1020.4 16.5 copy.255
  1038.0 19.7 %fusion.103 = f32[2048,8,2,352]{3,0,2,1:T(8,128)} fusion(bf16[64,2048]{1,0:T(8,128)(2,1)S(1)} %copy-done.24, bf16[64,8,1,352]{3,0,1,2:T(8,128)(2,1)S(1)} %copy-done.62, bf16[64,8,1,352]{3,0,1,2:T(8,128)(2,1)S(1)} %copy-done.61), kind=kOutput, calls=%fused_computation.154 | convolution fusion | flops 1476755456 | bytes 47120384 | tf_op jit(solution)/shard_map/td,tegf->degf/dot_general | solution.py:243
  1057.7 25.8 %add_convert_fusion = bf16[2048,8,2,352]{3,0,2,1:T(8,128)(2,1)} fusion(f32[2048,8,2,352]{3,0,2,1:T(8,128)} %fusion.103, bf16[64,2048]{1,0:T(8,128)(2,1)S(1)} %get-tuple-element.165, bf16[64,8,1,352]{3,0,1,2:T(8,128)(2,1)S(1)} %copy-done.60, bf16[64,8,1,352]{3,0,1,2:T(8,128)(2,1)S(1)} %copy-done.59), kind=kOutput, calls=%fused_computation.2 | convolution fusion | flops 1499824128 | bytes 70189056 | tf_op jit(solution)/shard_map/td,tegf->degf/dot_general | solution.py:243
  1087.0 76.0 %reduce-scatter.32.cloned.1.call-done = bf16[64,2,704]{2,0,1:T(8,128)(2,1)} async-done(((bf16[2048,2,704]{2,0,1:T(8,128)(2,1)}), bf16[64,2,704]{2,0,1:T(8,128)(2,1)}) %reduce-scatter.32.cloned.1.call-update) | async-done | bytes 180240 | tf_op jit(solution)/shard_map/reduce_scatter | solution.py:337
  1164.8 78.2 %reduce-scatter.34.cloned.1.call-done = bf16[64,8]{1,0:T(8,128)(2,1)} async-done(((bf16[2048,8]{1,0:T(8,128)(2,1)}), bf16[64,8]{1,0:T(8,128)(2,1)}) %reduce-scatter.34.cloned.1.call-update) | async-done | bytes 1040
  1247.0 78.2 %reduce-scatter.26.cloned.1.call-done = bf16[64,512]{1,0:T(8,128)(2,1)} async-done(((bf16[2048,512]{1,0:T(8,128)(2,1)}), bf16[64,512]{1,0:T(8,128)(2,1)}) %reduce-scatter.26.cloned.1.call-update) | async-done | bytes 65552 | tf_op jit(solution)/shard_map/reduce_scatter | solution.py:333
  1332.0 65.4 %all-reduce.7 = (bf16[2048]{0:T(1024)(128)(2,1)S(1)}, bf16[512]{0:T(512)(128)(2,1)S(1)}, bf16[2048]{0:T(1024)(128)(2,1)S(1)}) all-reduce(bf16[2048]{0:T(1024)(128)(2,1)S(1)} %add_convert_fusion.13, bf16[512]{0:T(512)(128)(2,1)S(1)} %copy-done.153, ...), channel_id=4, replica_groups=mesh['fsdp'=32,'tensor'=4] {'fsdp'}, use_global_device_ids=true, to_apply=%region_46.47.clone | all-reduce | flops 4608 | bytes 18432
  1407.3 82.0 %reduce-scatter.20.cloned.1.call-done = bf16[64,768]{1,0:T(8,128)(2,1)} async-done(((bf16[2048,768]{1,0:T(8,128)(2,1)}), bf16[64,768]{1,0:T(8,128)(2,1)}) %reduce-scatter.20.cloned.1.call-update) | async-done | bytes 98320 | tf_op jit(solution)/shard_map/reduce_scatter | solution.py:333
  1491.0 81.2 %reduce-scatter.22.cloned.1.call-done = bf16[64,576]{1,0:T(8,128)(2,1)} async-done(((bf16[2048,576]{1,0:T(8,128)(2,1)}), bf16[64,576]{1,0:T(8,128)(2,1)}) %reduce-scatter.22.cloned.1.call-update) | async-done | bytes 73744 | tf_op jit(solution)/shard_map/reduce_scatter | solution.py:333
  1573.7 106.0 %reduce-scatter.30.cloned.1.call-done = bf16[64,8,352]{2,1,0:T(8,128)(2,1)} async-done(((bf16[2048,8,352]{2,1,0:T(8,128)(2,1)}), bf16[64,8,352]{2,1,0:T(8,128)(2,1)}) %reduce-scatter.30.cloned.1.call-update) | async-done | bytes 360464 | tf_op jit(solution)/shard_map/reduce_scatter | solution.py:337
  1681.6 142.6 %reduce-scatter.28.cloned.1.call-done = bf16[64,8,2,352]{3,0,2,1:T(8,128)(2,1)} async-done(((bf16[2048,8,2,352]{3,0,2,1:T(8,128)(2,1)}), bf16[64,8,2,352]{3,0,2,1:T(8,128)(2,1)}) %reduce-scatter.28.cloned.1.call-update) | async-done | bytes 720912 | tf_op jit(solution)/shard_map/reduce_scatter | solution.py:337
  1824.2 3.1 copy.256
  (524 shorter events, 151.6 us)
Async XLA Ops:
  7.2 82.2 %copy-start.6 = (bf16[2,64,2048]{2,1,0:T(8,128)(2,1)S(1)}, bf16[2,64,2048]{2,1,0:T(8,128)(2,1)}, u32[]{:S(2)}) copy-start(bf16[2,64,2048]{2,1,0:T(8,128)(2,1)} %param.16) | copy-start | bytes 1572868
  7.2 79.5 %all-gather.12.cloned.1.call-start = ((), (), s32[]{:S(2)}) async-start(), calls=%async_computation.11 | async-start | bytes 2703360 | tf_op jit(solution)/shard_map/all_gather | solution.py:90
  7.9 96.2 %all-gather.18.cloned.1.call-start = ((), (), s32[]{:S(2)}) async-start(), calls=%async_computation.14 | async-start | bytes 3244032 | tf_op jit(solution)/shard_map/all_gather | solution.py:89
  8.7 142.2 %all-gather.14.cloned.1.call-start = ((), (), s32[]{:S(2)}) async-start(), calls=%async_computation.12 | async-start | bytes 2703360 | tf_op jit(solution)/shard_map/all_gather | solution.py:142
  92.9 102.2 %all-gather.16.cloned.1.call-start = ((), (), s32[]{:S(2)}) async-start(), calls=%async_computation.13 | async-start | bytes 1081344 | tf_op jit(solution)/shard_map/all_gather | solution.py:92
  93.5 148.2 %all-gather.30.cloned.1.call-start = ((), (), s32[]{:S(2)}) async-start(), calls=%async_computation.20 | async-start | bytes 2703360 | tf_op jit(solution)/shard_map/all_gather | solution.py:142
  94.3 192.8 %all-gather.20.cloned.1.call-start = ((), (), s32[]{:S(2)}) async-start(), calls=%async_computation.15 | async-start | bytes 2162688 | tf_op jit(solution)/shard_map/all_gather | solution.py:93
  94.9 242.4 %all-reduce.17.cloned.1.call-start = ((), (), s32[]{:S(2)}) async-start(), calls=%async_computation.32 | async-start | bytes 2097152 | tf_op jit(solution)/shard_map/psum | solution.py:172
  112.1 135.1 %copy-start.53 = (f32[64,4,192]{2,0,1:T(8,128)}, f32[64,4,192]{2,0,1:T(8,128)S(1)}, u32[]{:S(2)}) copy-start(f32[64,4,192]{2,0,1:T(8,128)S(1)} %fusion.189) | copy-start | bytes 589828
  113.3 86.2 %copy-start.51 = (f32[64,4,192]{2,0,1:T(8,128)}, f32[64,4,192]{2,0,1:T(8,128)S(1)}, u32[]{:S(2)}) copy-start(f32[64,4,192]{2,0,1:T(8,128)S(1)} %fusion.196) | copy-start | bytes 589828
  113.5 86.0 %copy-start.83 = (bf16[64,4,32]{2,0,1:T(8,128)(2,1)}, bf16[64,4,32]{2,0,1:T(8,128)(2,1)S(1)}, u32[]{:S(2)}) copy-start(bf16[64,4,32]{2,0,1:T(8,128)(2,1)S(1)} %get-tuple-element.154) | copy-start | bytes 49156
  113.5 86.0 %copy-start.85 = (bf16[64,4,32]{2,0,1:T(8,128)(2,1)}, bf16[64,4,32]{2,0,1:T(8,128)(2,1)S(1)}, u32[]{:S(2)}) copy-start(bf16[64,4,32]{2,0,1:T(8,128)(2,1)S(1)} %get-tuple-element.155) | copy-start | bytes 49156
  113.5 128.2 %copy-start.87 = (bf16[64,4,32]{2,0,1:T(8,128)(2,1)}, bf16[64,4,32]{2,0,1:T(8,128)(2,1)S(1)}, u32[]{:S(2)}) copy-start(bf16[64,4,32]{2,0,1:T(8,128)(2,1)S(1)} %get-tuple-element.140) | copy-start | bytes 49156
  113.5 128.2 %copy-start.89 = (bf16[64,4,32]{2,0,1:T(8,128)(2,1)}, bf16[64,4,32]{2,0,1:T(8,128)(2,1)S(1)}, u32[]{:S(2)}) copy-start(bf16[64,4,32]{2,0,1:T(8,128)(2,1)S(1)} %get-tuple-element.141) | copy-start | bytes 49156
  208.4 78.7 %copy-start.96 = (bf16[4,8,8,128]{3,2,1,0:T(8,128)(2,1)}, bf16[4,8,8,128]{3,2,1,0:T(8,128)(2,1)S(1)}, u32[]{:S(2)}) copy-start(bf16[4,8,8,128]{3,2,1,0:T(8,128)(2,1)S(1)} %fusion.66) | copy-start | bytes 196612
  208.4 34.8 %copy-start.46 = (bf16[512,1024]{1,0:T(8,128)(2,1)S(1)}, bf16[512,1024]{1,0:T(8,128)(2,1)}, u32[]{:S(2)}) copy-start(bf16[512,1024]{1,0:T(8,128)(2,1)} %all-gather.16.cloned.1.call-done) | copy-start | bytes 3145732
  254.4 37.6 %copy-start.98 = (bf16[4,8,8,128]{3,2,1,0:T(8,128)(2,1)}, bf16[4,8,8,128]{3,2,1,0:T(8,128)(2,1)S(1)}, u32[]{:S(2)}) copy-start(bf16[4,8,8,128]{3,2,1,0:T(8,128)(2,1)S(1)} %fusion.63) | copy-start | bytes 196612
  254.4 37.6 %copy-start.101 = (bf16[64,2,704]{2,1,0:T(2,128)(2,1)S(1)}, bf16[64,2,704]{2,1,0:T(2,128)(2,1)}, u32[]{:S(2)}) copy-start(bf16[64,2,704]{2,1,0:T(2,128)(2,1)} %param.30) | copy-start | bytes 540676
  292.0 27.5 %copy-start.144 = (s32[2,64,6]{1,0,2:T(2,128)S(1)}, s32[2,64,6]{1,0,2:T(2,128)}, u32[]{:S(2)}) copy-start(s32[2,64,6]{1,0,2:T(2,128)} %param.18) | copy-start | bytes 9220
  292.0 98.6 %all-gather.26.cloned.1.call-start = ((), (), s32[]{:S(2)}) async-start(), calls=%async_computation.18 | async-start | bytes 6488064 | tf_op jit(solution)/shard_map/all_gather | solution.py:102
  292.8 144.4 %all-gather.28.cloned.1.call-start = ((), (), s32[]{:S(2)}) async-start(), calls=%async_computation.19 | async-start | bytes 3244032 | tf_op jit(solution)/shard_map/all_gather | solution.py:103
  293.5 238.2 %all-gather.22.cloned.1.call-start = ((), (), s32[]{:S(2)}) async-start(), calls=%async_computation.16 | async-start | bytes 25952256 | tf_op jit(solution)/shard_map/all_gather | solution.py:100
  294.9 302.2 %all-gather.24.cloned.1.call-start = ((), (), s32[]{:S(2)}) async-start(), calls=%async_computation.17 | async-start | bytes 12976128 | tf_op jit(solution)/shard_map/all_gather | solution.py:101
  295.8 406.6 %all-reduce.21.cloned.1.call-start = ((), (), s32[]{:S(2)}) async-start(), calls=%async_computation.34 | async-start | bytes 1048576 | tf_op jit(solution)/shard_map/psum | solution.py:228
  319.5 75.0 %copy-start.110 = (f32[64,8]{0,1:T(8,128)}, f32[64,8]{0,1:T(8,128)S(1)}, u32[]{:S(2)}) copy-start(f32[64,8]{0,1:T(8,128)S(1)} %convert_reduce_fusion) | copy-start | bytes 6148
  319.6 75.0 %copy-start.108 = (f32[64,8]{0,1:T(8,128)}, f32[64,8]{0,1:T(8,128)S(1)}, u32[]{:S(2)}) copy-start(f32[64,8]{0,1:T(8,128)S(1)} %convert_reduce_fusion.1) | copy-start | bytes 6148
  340.8 53.8 %copy-start.132 = (f32[64]{0:T(128)}, f32[64]{0:T(128)S(1)}, u32[]{:S(2)}) copy-start(f32[64]{0:T(128)S(1)} %get-tuple-element.201) | copy-start | bytes 772
  340.8 53.7 %copy-start.140 = (f32[64]{0:T(128)}, f32[64]{0:T(128)S(1)}, u32[]{:S(2)}) copy-start(f32[64]{0:T(128)S(1)} %fusion.317) | copy-start | bytes 772
  341.5 53.1 %copy-start.130 = (f32[64]{0:T(128)}, f32[64]{0:T(128)S(1)}, u32[]{:S(2)}) copy-start(f32[64]{0:T(128)S(1)} %get-tuple-element.203) | copy-start | bytes 772
  341.5 53.0 %copy-start.138 = (f32[64]{0:T(128)}, f32[64]{0:T(128)S(1)}, u32[]{:S(2)}) copy-start(f32[64]{0:T(128)S(1)} %fusion.315) | copy-start | bytes 772
  342.7 94.4 %copy-start.25 = (bf16[2,64,2048]{2,1,0:T(8,128)(2,1)S(1)}, bf16[2,64,2048]{2,1,0:T(8,128)(2,1)}, u32[]{:S(2)}) copy-start(bf16[2,64,2048]{2,1,0:T(8,128)(2,1)} %param.19) | copy-start | bytes 1572868
  394.6 42.6 %copy-start.41 = (f32[64,2,704]{2,0,1:T(8,128)}, f32[64,2,704]{2,0,1:T(8,128)S(1)}, u32[]{:S(2)}) copy-start(f32[64,2,704]{2,0,1:T(8,128)S(1)} %fusion.187) | copy-start | bytes 1081348
  440.4 210.2 %copy-start.71 = (bf16[64,1,704]{2,0,1:T(8,128)(2,1)}, bf16[64,1,704]{2,0,1:T(8,128)(2,1)S(1)}, u32[]{:S(2)}) copy-start(bf16[64,1,704]{2,0,1:T(8,128)(2,1)S(1)} %get-tuple-element.132) | copy-start | bytes 270340
  656.4 47.4 %copy-start.150 = (f32[64]{0:T(128)S(1)}, f32[64]{0:T(128)}, u32[]{:S(2)}) copy-start(f32[64]{0:T(128)} %copy-done.149) | copy-start | bytes 772
  656.4 47.4 %copy-start.152 = (f32[64]{0:T(128)S(1)}, f32[64]{0:T(128)}, u32[]{:S(2)}) copy-start(f32[64]{0:T(128)} %copy-done.151) | copy-start | bytes 772
  661.9 44.4 %copy-start.164 = (f32[64]{0:T(128)S(1)}, f32[64]{0:T(128)}, u32[]{:S(2)}) copy-start(f32[64]{0:T(128)} %get-tuple-element.191) | copy-start | bytes 772
  661.9 44.4 %copy-start.165 = (f32[64]{0:T(128)S(1)}, f32[64]{0:T(128)}, u32[]{:S(2)}) copy-start(f32[64]{0:T(128)} %get-tuple-element.193) | copy-start | bytes 772
  661.9 160.0 %reduce-scatter.18.cloned.1.call-start = ((), (), s32[]{:S(2)}) async-start(), calls=%async_computation.22 | async-start | bytes 4866048 | tf_op jit(solution)/shard_map/reduce_scatter | solution.py:298
  662.3 45.1 %copy-start.124 = (bf16[64,8]{0,1:T(8,128)(2,1)}, bf16[64,8]{0,1:T(8,128)(2,1)S(1)}, u32[]{:S(2)}) copy-start(bf16[64,8]{0,1:T(8,128)(2,1)S(1)} %multiply_convert_fusion.16) | copy-start | bytes 3076
  662.3 45.1 %copy-start.126 = (bf16[64,8]{0,1:T(8,128)(2,1)}, bf16[64,8]{0,1:T(8,128)(2,1)S(1)}, u32[]{:S(2)}) copy-start(bf16[64,8]{0,1:T(8,128)(2,1)S(1)} %multiply_convert_fusion.17) | copy-start | bytes 3076
  737.3 171.2 %reduce-scatter.16.cloned.1.call-start = ((), (), s32[]{:S(2)}) async-start(), calls=%async_computation.21 | async-start | bytes 4866048 | tf_op jit(solution)/shard_map/reduce_scatter | solution.py:298
  771.1 217.2 %all-reduce.19.cloned.1.call-start = ((), (), s32[]{:S(2)}) async-start(), calls=%async_computation.33 | async-start | bytes 2359296 | tf_op jit(solution)/shard_map/psum | solution.py:206
  799.2 127.1 %copy-start.155 = (f32[32]{0:T(128)S(1)}, f32[32]{0:T(128)}, u32[]{:S(2)}) copy-start(f32[32]{0:T(128)} %copy-done.154) | copy-start | bytes 388
  799.2 127.1 %copy-start.157 = (f32[64]{0:T(128)S(1)}, f32[64]{0:T(128)}, u32[]{:S(2)}) copy-start(f32[64]{0:T(128)} %copy-done.156) | copy-start | bytes 772
  943.6 141.5 %reduce-scatter.36.cloned.1.call-start = ((), (), s32[]{:S(2)}) async-start(), calls=%async_computation.31 | async-start | bytes 3244032
  949.7 213.3 %reduce-scatter.32.cloned.1.call-start = ((), (), s32[]{:S(2)}) async-start(), calls=%async_computation.29 | async-start | bytes 6488064 | tf_op jit(solution)/shard_map/reduce_scatter | solution.py:337
  957.0 286.1 %reduce-scatter.34.cloned.1.call-start = ((), (), s32[]{:S(2)}) async-start(), calls=%async_computation.30 | async-start | bytes 540672
  958.9 366.3 %reduce-scatter.26.cloned.1.call-start = ((), (), s32[]{:S(2)}) async-start(), calls=%async_computation.26 | async-start | bytes 2162688 | tf_op jit(solution)/shard_map/reduce_scatter | solution.py:333
  962.1 443.9 %reduce-scatter.24.cloned.1.call-start = ((), (), s32[]{:S(2)}) async-start(), calls=%async_computation.25 | async-start | bytes 1081344 | tf_op jit(solution)/shard_map/reduce_scatter | solution.py:333
  964.6 524.8 %reduce-scatter.20.cloned.1.call-start = ((), (), s32[]{:S(2)}) async-start(), calls=%async_computation.23 | async-start | bytes 3244032 | tf_op jit(solution)/shard_map/reduce_scatter | solution.py:333
  968.7 603.4 %reduce-scatter.22.cloned.1.call-start = ((), (), s32[]{:S(2)}) async-start(), calls=%async_computation.24 | async-start | bytes 2703360 | tf_op jit(solution)/shard_map/reduce_scatter | solution.py:333
  994.5 685.2 %reduce-scatter.30.cloned.1.call-start = ((), (), s32[]{:S(2)}) async-start(), calls=%async_computation.28 | async-start | bytes 12976128 | tf_op jit(solution)/shard_map/reduce_scatter | solution.py:337
  1036.9 787.3 %reduce-scatter.28.cloned.1.call-start = ((), (), s32[]{:S(2)}) async-start(), calls=%async_computation.27 | async-start | bytes 25952256 | tf_op jit(solution)/shard_map/reduce_scatter | solution.py:337
  1083.5 162.2 %copy-start.117 = (f32[2048]{0:T(1024)S(1)}, f32[2048]{0:T(1024)}, u32[]{:S(2)}) copy-start(f32[2048]{0:T(1024)} %get-tuple-element.86) | copy-start | bytes 24580
  1083.5 244.5 %copy-start.3 = (bf16[2048,576]{1,0:T(8,128)(2,1)S(1)}, bf16[2048,576]{1,0:T(8,128)(2,1)}, u32[]{:S(2)}) copy-start(bf16[2048,576]{1,0:T(8,128)(2,1)} %all-gather.12.cloned.1.call-done) | copy-start | bytes 7077892
  1087.0 243.0 %copy-start.100 = (bf16[64,2048]{1,0:T(8,128)(2,1)S(1)}, bf16[64,2048]{1,0:T(8,128)(2,1)}, u32[]{:S(2)}) copy-start(bf16[64,2048]{1,0:T(8,128)(2,1)} %get-tuple-element.116) | copy-start | bytes 786436
  1247.0 82.9 %copy-start.120 = (f32[64]{0:T(128)S(1)}, f32[64]{0:T(128)}, u32[]{:S(2)}) copy-start(f32[64]{0:T(128)} %copy-done.118) | copy-start | bytes 772
  1247.0 83.0 %copy-start.123 = (f32[64]{0:T(128)S(1)}, f32[64]{0:T(128)}, u32[]{:S(2)}) copy-start(f32[64]{0:T(128)} %copy-done.121) | copy-start | bytes 772
  1331.9 70.4 %copy-start.35 = (f32[64,2048]{1,0:T(8,128)S(1)}, f32[64,2048]{1,0:T(8,128)}, u32[]{:S(2)}) copy-start(f32[64,2048]{1,0:T(8,128)} %get-tuple-element.136) | copy-start | bytes 1572868
  1331.9 70.4 %copy-start.38 = (f32[64,2048]{1,0:T(8,128)S(1)}, f32[64,2048]{1,0:T(8,128)}, u32[]{:S(2)}) copy-start(f32[64,2048]{1,0:T(8,128)} %copy-done.36) | copy-start | bytes 1572868
  1331.9 70.4 %copy-start.58 = (f32[64,2048]{1,0:T(8,128)S(1)}, f32[64,2048]{1,0:T(8,128)}, u32[]{:S(2)}) copy-start(f32[64,2048]{1,0:T(8,128)} %get-tuple-element.210) | copy-start | bytes 1572868
  1332.0 70.4 %copy-start.158 = (f32[64]{0:T(128)S(1)}, f32[64]{0:T(128)}, u32[]{:S(2)}) copy-start(f32[64]{0:T(128)} %get-tuple-element.185) | copy-start | bytes 772
  1332.0 70.4 %copy-start.159 = (f32[64]{0:T(128)S(1)}, f32[64]{0:T(128)}, u32[]{:S(2)}) copy-start(f32[64]{0:T(128)} %get-tuple-element.212) | copy-start | bytes 772
  1332.0 70.4 %copy-start.45 = (f32[64,2048]{1,0:T(8,128)S(1)}, f32[64,2048]{1,0:T(8,128)}, u32[]{:S(2)}) copy-start(f32[64,2048]{1,0:T(8,128)} %copy-done.44) | copy-start | bytes 1572868
  (126 other events, 738.1 us)
Sparse Core Ops, SparseCore 0:
  10.3 47.3 all-gather.11
  59.9 44.1 all-gather.17
  107.0 43.8 all-gather.13
  153.0 42.1 all-gather.15
  197.9 43.8 all-gather.29
  243.8 43.2 all-gather.19
  292.1 45.1 all-reduce.16
  340.4 50.0 all-gather.25
  393.1 44.0 all-gather.27
  440.1 91.5 all-gather.21
  534.8 62.2 all-gather.23
  662.0 40.3 all-reduce.20
  737.4 84.4 reduce-scatter.17
  825.5 82.9 reduce-scatter.15
  943.7 44.5 all-reduce.18
  992.3 81.3 reduce-scatter.35
  1077.3 85.6 reduce-scatter.31
  1166.7 76.3 reduce-scatter.33
  1247.0 78.1 reduce-scatter.25
  1329.0 76.9 reduce-scatter.23
  1409.6 79.7 reduce-scatter.19
  1493.4 78.7 reduce-scatter.21
  1576.0 103.6 reduce-scatter.29
  1684.0 140.1 reduce-scatter.27
where the time goes:
time: 1840 us; the launch traced here: 1830 us
  waiting for transfers between devices  1210 us (66%)
  matrix products  279 us (15%)
  blocking collectives  188 us (10%)
  local copies, waits for them, and re-layouts  77.8 us (4%)
  other arithmetic  61.6 us (3%)
  between operations  19.3 us (1%)
    reduce_scatter x3, waiting for transfers between devices, on_device(): lax.psum_scatter(as_sent(ffn_grads), 'fsdp', scatter_dimension=0, tiled=T...  325 us
    reduce_scatter x4, waiting for transfers between devices, on_device(): lax.psum_scatter(as_sent(attn_grads), 'fsdp', scatter_dimension=0, tiled=...  244 us
    unnamed x2, blocking collectives  136 us
    reduce_scatter x2, waiting for transfers between devices, on_device(): lax.psum_scatter(key_terms.astype(jnp.bfloat16), 'fsdp', scatter_dimensio...  107 us
    all_gather x1, waiting for transfers between devices, fetch_ffn(): lax.all_gather(w_expert_in, 'fsdp', axis=0, tiled=True)  85.1 us
    unnamed x26, waiting for transfers between devices  81.7 us
    all_gather x2, waiting for transfers between devices, on_device(): expand_piece = lax.all_gather(packed, 'fsdp', axis=0, tiled=True)  70.6 us
    all_gather x1, waiting for transfers between devices, fetch_ffn(): lax.all_gather(w_shared_in, 'fsdp', axis=0, tiled=True)  47.8 us
  transfers between devices with their start and end apart: 24, of which 22 were waited for; matrix products, arithmetic and copies ran while one was open for 16% of the time, Pallas kernels for 0%

commit v1 on v0

v1 whole, which is shorter than its diff:
```python
import jax
import jax.numpy as jnp
from jax import lax
from jax.experimental import pallas as pl
from jax.experimental.pallas import tpu as pltpu
from jax.sharding import Mesh
from jax.sharding import PartitionSpec as P

NOPE = 128
ROPE = 64
VHEAD = 128
RANK = 512
EXPERTS = 8

epsilon = 1e-06
bf16 = jnp.bfloat16
f32 = jnp.float32


def rotate_parts(values, position, inverse):
    half = values.shape[-1] // 2
    freq = jnp.exp(jnp.arange(half, dtype=f32) * (-jnp.log(10000.0) / half))
    angle = position.astype(f32)[:, None] * freq[None, :]
    cosine = jnp.cos(angle)
    sine = jnp.sin(angle)
    if inverse:
        sine = -sine
    if values.ndim == 3:
        cosine = cosine[:, None, :]
        sine = sine[:, None, :]
    first = values[..., :half]
    second = values[..., half:]
    return jnp.concatenate(
        [first * cosine - second * sine, second * cosine + first * sine], axis=-1
    )


def norm_forward(values, gain):
    factor = lax.rsqrt(jnp.mean(values * values, axis=-1, keepdims=True) + epsilon)
    return (values * factor * gain, factor)


def norm_backward(values, factor, gain, grad):
    scaled = grad * gain
    d_values = factor * scaled - values * (factor * factor * factor) * jnp.mean(
        values * scaled, axis=-1, keepdims=True
    )
    d_gain = jnp.sum(grad * values * factor, axis=0)
    return (d_values, d_gain)


def shift(value, axis, step):
    count = lax.axis_size(axis)
    return lax.ppermute(value, axis, [(i, (i + step) % count) for i in range(count)])


def pick(value, place, at):
    return lax.dynamic_index_in_dim(value, place, at, keepdims=False)


def gather_near(value, axis):
    return [value] + [shift(value, axis, s) for s in range(1, lax.axis_size(axis))]


def gather_at(value, axis):
    count = lax.axis_size(axis)
    me = lax.axis_index(axis)
    whole = jnp.zeros((count,) + value.shape, value.dtype)
    for s in range(count):
        part = value if s == 0 else shift(value, axis, s)
        whole = lax.dynamic_update_index_in_dim(whole, part, lax.rem(me - s + count, count), 0)
    return whole


def sum_near(parts, axis):
    total = parts[0].astype(f32)
    for s in range(1, len(parts)):
        total = total + shift(parts[s], axis, -s).astype(f32)
    return total


def sum_ahead(parts, axis):
    total = parts[0].astype(f32)
    for s in range(1, len(parts)):
        total = total + shift(parts[s], axis, s).astype(f32)
    return total


def sum_at(value, axis, at):
    count = lax.axis_size(axis)
    me = lax.axis_index(axis)
    return sum_ahead([pick(value, lax.rem(me + s, count), at) for s in range(count)], axis)


def exchange_at(value, axis):
    count = lax.axis_size(axis)
    me = lax.axis_index(axis)
    whole = jnp.zeros_like(value)
    for s in range(count):
        part = pick(value, lax.rem(me + s, count), 0)
        part = part if s == 0 else shift(part, axis, s)
        whole = lax.dynamic_update_index_in_dim(whole, part, lax.rem(me - s + count, count), 0)
    return whole


def to_far(value):
    rows = value.shape[0]
    return value.reshape(rows, 4, 4, 128).transpose(0, 2, 1, 3).reshape(rows, 2048)


def dot_nn(a, b):
    return jnp.dot(a, b, preferred_element_type=f32)


def dot_nt(a, b):
    return lax.dot_general(a, b, (((1,), (1,)), ((), ())), preferred_element_type=f32)


def dot_tn(a, b):
    return lax.dot_general(a, b, (((0,), (0,)), ((), ())), preferred_element_type=f32)


def whole(*shape):
    return pl.BlockSpec(shape, lambda h: (0,) * len(shape))


SCALARS = pl.BlockSpec(memory_space=pltpu.SMEM)
SCALE = (NOPE + ROPE) ** (-0.5)
MIB = 1024 * 1024


def attend_kernel(
    place, q, a0, a1, a2, a3, b0, b1, b2, b3, expand, out_w, where_q, where_k,
    prob, kv, attended, lat, r0, r1, r2, r3, key_rot, total,
):
    head = pl.program_id(0)

    @pl.when(head == 0)
    def _():
        for sx in range(4):
            lat[sx * 512 : sx * 512 + 512, 256:576] = (b0, b1, b2, b3)[sx][...]
            for sz in range(4):
                row = (sx * 4 + sz) * 128
                lat[row : row + 128, 0:256] = (a0, a1, a2, a3)[sz][sx * 128 : sx * 128 + 128, :]
        key_rot[...] = jnp.concatenate(
            [lat[:, RANK:576], jnp.zeros((2048, 64), bf16)], axis=1
        )
        total[...] = jnp.zeros_like(total)

    expand_h = expand[...].reshape(RANK, 256)
    kv_h = dot_nn(lat[:, :RANK], expand_h).astype(bf16)
    kv[...] = kv_h
    score = (dot_nt(q[:, :128], kv_h[:, :128]) + dot_nt(q[:, 128:], key_rot[...])) * SCALE
    allowed = (where_q[:, 0:1] >= where_k[0:1, :]) & (where_q[:, 1:2] == where_k[1:2, :])
    score = jnp.where(allowed, score, -1e30)
    power = jnp.exp(score - jnp.max(score, axis=1, keepdims=True))
    prob_h = power / jnp.sum(power, axis=1, keepdims=True)
    prob[0] = prob_h
    attended_h = dot_nn(prob_h.astype(bf16), kv_h[:, 128:]).astype(bf16)
    attended[...] = attended_h
    total[...] += dot_nt(attended_h, out_w[...])

    @pl.when(head == 3)
    def _():
        for s, out in enumerate((r0, r1, r2, r3)):
            row = pl.multiple_of(lax.rem(place[3] + s, 4) * 32, 32)
            out[...] = total[pl.ds(row, 32), :].astype(bf16)


def attend(place, q, parts_a, parts_b, attn_all, where_q, where_k):
    by_head = attn_all.reshape(32, 4, 16, 1536)
    return pl.pallas_call(
        attend_kernel,
        grid=(4,),
        in_specs=[SCALARS, pl.BlockSpec((128, 256), lambda h: (0, h))]
        + [whole(512, 256)] * 4
        + [whole(512, 320)] * 4
        + [
            pl.BlockSpec((32, 1, 16, 256), lambda h: (0, h, 0, 5)),
            pl.BlockSpec((2048, 128), lambda h: (0, 6 + h)),
            whole(128, 2),
            whole(2, 2048),
        ],
        out_specs=[
            pl.BlockSpec((1, 128, 2048), lambda h: (h, 0, 0)),
            pl.BlockSpec((2048, 256), lambda h: (0, h)),
            pl.BlockSpec((128, 128), lambda h: (0, h)),
            whole(2048, 576),
        ]
        + [whole(32, 2048)] * 4,
        out_shape=[
            jax.ShapeDtypeStruct((4, 128, 2048), f32),
            jax.ShapeDtypeStruct((2048, 1024), bf16),
            jax.ShapeDtypeStruct((128, 512), bf16),
            jax.ShapeDtypeStruct((2048, 576), bf16),
        ]
        + [jax.ShapeDtypeStruct((32, 2048), bf16)] * 4,
        scratch_shapes=[pltpu.VMEM((2048, 128), bf16), pltpu.VMEM((128, 2048), f32)],
        compiler_params=pltpu.CompilerParams(vmem_limit_bytes=48 * MIB),
        cost_estimate=pl.CostEstimate(
            flops=5 * 10**9, bytes_accessed=22 * 10**6, transcendentals=2**20
        ),
        name="attend",
    )(place, q, *parts_a, *parts_b, by_head, attn_all, where_q, where_k)


def attend_back_kernel(
    place, d0, d1, d2, d3, out_w, q, kv, prob, lat, expand, nope_w, rot_w, cosine, sine,
    d_q, d_rot, d_exp, d_branch, a0, a1, a2, a3, b0, b1, b2, b3, r0, r1, r2, r3,
    key_rot, lat_sum, rot_sum, rot_q, total,
):
    head = pl.program_id(0)

    @pl.when(head == 0)
    def _():
        for s, part in enumerate((d0, d1, d2, d3)):
            row = pl.multiple_of(lax.rem(place[3] - s + 4, 4) * 32, 32)
            d_branch[pl.ds(row, 32), :] = part[...]
        key_rot[...] = jnp.concatenate(
            [lat[:, RANK:576], jnp.zeros((2048, 64), bf16)], axis=1
        )
        lat_sum[...] = jnp.zeros_like(lat_sum)
        rot_sum[...] = jnp.zeros_like(rot_sum)
        total[...] = jnp.zeros_like(total)

    d_att = dot_nn(d_branch[...], out_w[...]).astype(bf16)
    prob_h = prob[0]
    d_prob = dot_nt(d_att, kv[:, 128:])
    row_sum = jnp.sum(prob_h * d_prob, axis=1, keepdims=True)
    d_score = (prob_h * (d_prob - row_sum)).astype(bf16)
    d_nope = (dot_nn(d_score, kv[:, :128]) * SCALE).astype(bf16)
    d_q[...] = d_nope
    rot_q[head] = dot_nn(d_score, key_rot[...]) * SCALE
    d_key = dot_tn(d_score, q[...]) * SCALE
    d_val = dot_tn(prob_h.astype(bf16), d_att)
    d_exp_h = jnp.concatenate([d_key[:, :128], d_val], axis=1).astype(bf16)
    d_exp[...] = d_exp_h
    rot_sum[...] += d_key[:, 128:]
    lat_sum[...] += dot_nt(d_exp_h, expand[...].reshape(RANK, 256))
    total[...] += dot_nt(d_nope, nope_w[...])

    @pl.when(head == 3)
    def _():
        rot = jnp.concatenate([rot_q[h][:, :64] for h in range(4)], axis=1)
        lane = lax.broadcasted_iota(jnp.int32, rot.shape, 1)
        partner = jnp.where(
            lane % 64 < 32, pltpu.roll(rot, 224, 1), pltpu.roll(rot, 32, 1)
        )
        rot = (rot * cosine[...] + partner * sine[...]).astype(bf16)
        d_rot[...] = rot
        summed = total[...] + dot_nt(rot, rot_w[...])
        total[...] = summed
        for s, out in enumerate((r0, r1, r2, r3)):
            row = pl.multiple_of(lax.rem(place[3] + s, 4) * 32, 32)
            out[...] = total[pl.ds(row, 32), :].astype(bf16)
        for sx in range(4):
            (a0, a1, a2, a3)[sx][...] = lat_sum[sx * 512 : sx * 512 + 512, :256].astype(bf16)
            for sz in range(4):
                row = (sx * 4 + sz) * 128
                out = (b0, b1, b2, b3)[sz]
                out[sx, :, :256] = lat_sum[row : row + 128, 256:].astype(bf16)
                out[sx, :, 256:] = rot_sum[row : row + 128, :64].astype(bf16)


def attend_back(place, parts, q, kv, prob, lat, attn_all, cosine, sine):
    by_head = attn_all.reshape(32, 4, 16, 1536)
    return pl.pallas_call(
        attend_back_kernel,
        grid=(4,),
        in_specs=[SCALARS]
        + [whole(32, 2048)] * 4
        + [
            pl.BlockSpec((2048, 128), lambda h: (0, 6 + h)),
            pl.BlockSpec((128, 256), lambda h: (0, h)),
            pl.BlockSpec((2048, 256), lambda h: (0, h)),
            pl.BlockSpec((1, 128, 2048), lambda h: (h, 0, 0)),
            whole(2048, 576),
            pl.BlockSpec((32, 1, 16, 256), lambda h: (0, h, 0, 5)),
            pl.BlockSpec((2048, 128), lambda h: (0, h)),
            pl.BlockSpec((2048, 256), lambda h: (0, 2)),
            whole(128, 256),
            whole(128, 256),
        ],
        out_specs=[
            pl.BlockSpec((128, 128), lambda h: (0, h)),
            whole(128, 256),
            pl.BlockSpec((2048, 256), lambda h: (0, h)),
            whole(128, 2048),
        ]
        + [whole(512, 256)] * 4
        + [whole(4, 128, 320)] * 4
        + [whole(32, 2048)] * 4,
        out_shape=[
            jax.ShapeDtypeStruct((128, 512), bf16),
            jax.ShapeDtypeStruct((128, 256), bf16),
            jax.ShapeDtypeStruct((2048, 1024), bf16),
            jax.ShapeDtypeStruct((128, 2048), bf16),
        ]
        + [jax.ShapeDtypeStruct((512, 256), bf16)] * 4
        + [jax.ShapeDtypeStruct((4, 128, 320), bf16)] * 4
        + [jax.ShapeDtypeStruct((32, 2048), bf16)] * 4,
        scratch_shapes=[
            pltpu.VMEM((2048, 128), bf16),
            pltpu.VMEM((2048, 512), f32),
            pltpu.VMEM((2048, 128), f32),
            pltpu.VMEM((4, 128, 128), f32),
            pltpu.VMEM((128, 2048), f32),
        ],
        compiler_params=pltpu.CompilerParams(vmem_limit_bytes=56 * MIB),
        cost_estimate=pl.CostEstimate(
            flops=8 * 10**9, bytes_accessed=30 * 10**6, transcendentals=0
        ),
        name="attend_back",
    )(place, *parts, attn_all, q, kv, prob, lat, by_head, attn_all, attn_all, cosine, sine)


def expert_kernel(
    place, far, spread, w0, w1, w2, w3, d_far, d_hidden, hidden, out, weight, sems
):
    @pl.when(pl.program_id(0) == 0)
    def _():
        copies = []
        for s, part in enumerate((w0, w1, w2, w3)):
            row = pl.multiple_of(lax.rem(place[1] - s + 4, 4) * 512, 512)
            copies.append(pltpu.make_async_copy(part, weight.at[pl.ds(row, 512)], sems.at[s]))
        for copy in copies:
            copy.start()
        for copy in copies:
            copy.wait()

    expert = 2 * place[0] + place[2]
    raw = dot_nn(far[...], weight[:, :896])
    d_weighted = dot_nn(spread[:, :2048], weight[:, 896:])
    rows = raw.shape[0]
    logits = raw[:, 880:888]
    power = jnp.exp(logits - jnp.max(logits, axis=1, keepdims=True))
    router = power / jnp.sum(power, axis=1, keepdims=True)
    is_mine = lax.broadcasted_iota(jnp.int32, (rows, 8), 1) == expert
    chosen = spread[:, 2048:2176][:, :8].astype(f32)
    gate = jnp.sum(jnp.where(is_mine, router * chosen, 0.0), axis=1, keepdims=True)
    routed = lax.broadcasted_iota(jnp.int32, (rows, 440), 1) < 352
    gate = jnp.where(routed, gate, 1.0)
    low, upper = raw[:, :440], raw[:, 440:880]
    sigma = 1.0 / (1.0 + jnp.exp(-low))
    silu = low * sigma
    slope = sigma + silu * (1.0 - sigma)
    act = silu * upper
    weighted = (gate * act).astype(bf16)
    d_gate = jnp.sum(jnp.where(routed, d_weighted * act, 0.0), axis=1, keepdims=True)
    d_act = d_weighted * gate
    d_up = jnp.concatenate(
        [d_act * upper * slope, d_act * silu, jnp.zeros((rows, 16), f32)], axis=1
    ).astype(bf16)
    d_hidden[...] = d_up
    hidden[...] = jnp.concatenate([weighted, jnp.zeros((rows, 72), bf16)], axis=1)
    d_far[:, :2048] = dot_nt(d_up, weight[:, :896]).astype(bf16)
    lane = lax.broadcasted_iota(jnp.int32, (rows, 128), 1)
    d_far[:, 2048:] = jnp.where(lane == expert, d_gate, 0.0).astype(bf16)
    out[...] = dot_nt(weighted, weight[:, 896:]).astype(bf16)


def run_expert(place, far, spread, pieces):
    rows = 256
    by_rows = lambda columns: pl.BlockSpec((rows, columns), lambda i: (i, 0))
    return pl.pallas_call(
        expert_kernel,
        grid=(512 // rows,),
        in_specs=[SCALARS, by_rows(2048), by_rows(2176)] + [pl.BlockSpec(memory_space=pl.ANY)] * 4,
        out_specs=[by_rows(2176), by_rows(896), by_rows(512), by_rows(2048)],
        out_shape=[
            jax.ShapeDtypeStruct((512, 2176), bf16),
            jax.ShapeDtypeStruct((512, 896), bf16),
            jax.ShapeDtypeStruct((512, 512), bf16),
            jax.ShapeDtypeStruct((512, 2048), bf16),
        ],
        scratch_shapes=[pltpu.VMEM((2048, 1336), bf16), pltpu.SemaphoreType.DMA((4,))],
        compiler_params=pltpu.CompilerParams(vmem_limit_bytes=48 * MIB),
        cost_estimate=pl.CostEstimate(
            flops=6 * 10**9, bytes_accessed=18 * 10**6, transcendentals=2**18
        ),
        name="expert",
    )(place, far, spread, *pieces)


def expert_grad_kernel(x0, x1, y0, y1, d0, d1, h0, h1, out):
    out[:, :896] = (dot_tn(x0[...], d0[...]) + dot_tn(x1[...], d1[...])).astype(bf16)
    down = dot_tn(y0[...], h0[...]) + dot_tn(y1[...], h1[...])
    out[:, 896:] = down[:, :440].astype(bf16)


def expert_grad(fars, spreads, d_hiddens, hiddens):
    block = 512
    columns = pl.BlockSpec((512, block), lambda i: (0, i))
    return pl.pallas_call(
        expert_grad_kernel,
        grid=(2048 // block,),
        in_specs=[columns] * 4 + [whole(512, 896)] * 2 + [whole(512, 512)] * 2,
        out_specs=pl.BlockSpec((block, 1336), lambda i: (i, 0)),
        out_shape=jax.ShapeDtypeStruct((2048, 1336), bf16),
        compiler_params=pltpu.CompilerParams(vmem_limit_bytes=48 * MIB),
        cost_estimate=pl.CostEstimate(
            flops=6 * 10**9, bytes_accessed=18 * 10**6, transcendentals=0
        ),
        name="expert_grad",
    )(*fars, *spreads, *d_hiddens, *hiddens)


def attn_grad_kernel(normed, d_q, d_rot, d_branch, attended, out):
    out[:, :512] = dot_tn(normed[...], d_q[...]).astype(bf16)
    out[:, 512:768] = dot_tn(normed[...], d_rot[...]).astype(bf16)
    out[:, 768:] = dot_tn(d_branch[...], attended[...]).astype(bf16)


def attn_grad(normed, d_q, d_rot, d_branch, attended):
    block = 512
    columns = pl.BlockSpec((128, block), lambda i: (0, i))
    return pl.pallas_call(
        attn_grad_kernel,
        grid=(2048 // block,),
        in_specs=[columns, whole(128, 512), whole(128, 256), columns, whole(128, 512)],
        out_specs=pl.BlockSpec((block, 1280), lambda i: (i, 0)),
        out_shape=jax.ShapeDtypeStruct((2048, 1280), bf16),
        compiler_params=pltpu.CompilerParams(vmem_limit_bytes=48 * MIB),
        cost_estimate=pl.CostEstimate(
            flops=7 * 10**8, bytes_accessed=7 * 10**6, transcendentals=0
        ),
        name="attn_grad",
    )(normed, d_q, d_rot, d_branch, attended)


def on_device(
    tokens,
    segment,
    routes,
    cotangent,
    gain_attn,
    w_query,
    w_compress,
    gain_latent,
    w_expand,
    w_output,
    gain_ffn,
    w_router,
    w_expert_in,
    w_expert_out,
    w_shared_in,
    w_shared_out,
):
    xi, zi, ci, yi = (lax.axis_index(a) for a in ("x", "z", "c", "y"))
    place = jnp.stack([xi, zi, ci, yi]).astype(jnp.int32)
    is_first = ci == 0
    heads = 4
    dim = 2048

    def enter(value):
        mine, other = pick(value, ci, 0), shift(pick(value, 1 - ci, 0), "c", 1)
        return jnp.concatenate(
            [jnp.where(is_first, mine, other), jnp.where(is_first, other, mine)], axis=0
        )

    def leave(value):
        halves = value.reshape((2, 64) + value.shape[1:])
        mine, other = pick(halves, ci, 0), shift(pick(halves, 1 - ci, 0), "c", 1)
        return jnp.stack([jnp.where(is_first, mine, other), jnp.where(is_first, other, mine)])

    small = jnp.concatenate(
        [
            w_compress,
            gain_attn[:, None],
            gain_ffn[:, None],
            w_router,
            jnp.pad(gain_latent, (0, 48))[:, None],
            jnp.zeros((64, 53), bf16),
        ],
        axis=1,
    )
    small_all = lax.all_gather(small, ("x", "z", "c"), axis=0, tiled=True)
    compress_w = small_all[:, :576]
    gain_first = small_all[:, 576].astype(f32)
    gain_second = small_all[:, 577].astype(f32)
    router_w = small_all[:, 578:586]
    latent_gain = small_all[:, 586].reshape(32, 64)[:, :16].reshape(RANK).astype(f32)

    by_head = w_query.reshape(64, heads, NOPE + ROPE)
    attn_all = lax.all_gather(
        jnp.concatenate(
            [
                by_head[:, :, :NOPE].reshape(64, 512),
                by_head[:, :, NOPE:].reshape(64, 256),
                w_output,
                w_expand.reshape(16, heads, 256).transpose(1, 0, 2).reshape(64, 256),
            ],
            axis=1,
        ),
        ("x", "z", "c"),
        axis=0,
        tiled=True,
    )

    packed_w = jnp.concatenate(
        [
            w_expert_in[:, :, 0],
            w_shared_in[:, 0].reshape(64, 8, 88),
            w_expert_in[:, :, 1],
            w_shared_in[:, 1].reshape(64, 8, 88),
            jnp.broadcast_to(w_router[:, None, :], (64, 8, 8)),
            jnp.zeros((64, 8, 8), bf16),
            w_expert_out,
            w_shared_out.reshape(64, 8, 88),
        ],
        axis=-1,
    )
    packed_w = packed_w.transpose(1, 0, 2).reshape(4, 2, 64, 1336)
    mine_w, other_w = pick(packed_w, ci, 1), shift(pick(packed_w, 1 - ci, 1), "c", 1)
    pair_w = jnp.concatenate(
        [jnp.where(is_first, mine_w, other_w), jnp.where(is_first, other_w, mine_w)], axis=1
    )
    pieces = gather_near(exchange_at(pair_w, "x").reshape(512, 1336), "z")

    inputs = enter(tokens).astype(f32)
    chosen = jnp.sum(
        (routes[..., None] == jnp.arange(EXPERTS, dtype=jnp.int32)).astype(f32), axis=2
    )
    spread = jnp.concatenate(
        [
            to_far(cotangent.reshape(128, dim)),
            chosen.reshape(128, 8).astype(bf16),
            jnp.zeros((128, 120), bf16),
        ],
        axis=1,
    )
    spread = enter(spread.reshape(2, 64, 2176))

    def own(value):
        return lax.dynamic_slice_in_dim(value, yi * 32, 32, 0)

    spread_own = own(spread)
    d_out_own = to_far(spread_own[:, :2048])
    chosen_own = spread_own[:, 2048:2056].astype(f32)
    inputs_own = own(inputs)
    spread = jnp.concatenate(
        [lax.dynamic_slice_in_dim(spread, lax.rem(yi - s + 4, 4) * 32, 32, 0) for s in range(4)]
    )
    spread = jnp.concatenate(gather_near(spread, "x"), axis=0)
    spread_other = shift(spread, "c", 1)

    position = (xi * 4 + zi) * 128 + jnp.arange(128, dtype=jnp.int32)
    segment_row = pick(segment, ci, 0)
    blocks = jnp.stack(
        [lax.rem(xi - sx + 4, 4) * 4 + lax.rem(zi - sz + 4, 4) for sx in range(4) for sz in range(4)]
    )
    segment_near = segment_row.reshape(16, 128)[blocks].reshape(2048)
    key_place = (blocks[:, None] * 128 + jnp.arange(128, dtype=jnp.int32)[None, :]).reshape(2048)
    where_k = jnp.stack([key_place, segment_near])
    where_q = jnp.stack(
        [position, lax.dynamic_slice_in_dim(segment_row, (xi * 4 + zi) * 128, 128)], axis=1
    )
    normed_full, factor_one = norm_forward(inputs, gain_first)
    normed = normed_full.astype(bf16)
    compressed = dot_nn(normed, compress_w)
    latent_full, factor_latent = norm_forward(compressed[:, :RANK], latent_gain)
    packed = jnp.concatenate(
        [latent_full, rotate_parts(compressed[:, RANK:], position, False)], axis=1
    ).astype(bf16)
    parts_a = gather_near(jnp.concatenate(gather_near(packed[:, :256], "x"), axis=0), "z")
    parts_b = gather_near(jnp.concatenate(gather_near(packed[:, 256:], "z"), axis=0), "x")

    q_raw = dot_nn(normed, attn_all[:, :768])
    rot = rotate_parts(q_raw[:, 512:].reshape(128, heads, ROPE), position, False)
    query = (
        jnp.concatenate(
            [q_raw[:, :512].reshape(128, heads, NOPE), rot, jnp.zeros((128, heads, 64), f32)],
            axis=-1,
        )
        .astype(bf16)
        .reshape(128, heads * 256)
    )
    prob, kv, attended, latent_all, *branch = attend(
        place, query, parts_a, parts_b, attn_all, where_q, where_k
    )
    middle = inputs_own + sum_ahead(branch, "y")

    normed_ffn_full, factor_two = norm_forward(middle, gain_second)
    normed_ffn = normed_ffn_full.astype(bf16)
    far = to_far(normed_ffn)
    far_a = jnp.stack(gather_near(jnp.concatenate(gather_near(far[:, :1024], "x")), "y"))
    far_b = jnp.stack(gather_near(jnp.concatenate(gather_near(far[:, 1024:], "y")), "x"))
    far_a = far_a.reshape(4, 4, 32, 1024).transpose(1, 0, 2, 3).reshape(512, 1024)
    far = jnp.concatenate([far_a, far_b.reshape(512, 1024)], axis=1)
    far_other = shift(far, "c", 1)
    d_far, d_hidden, hidden, out_far = run_expert(place, far, spread, pieces)
    d_far2, d_hidden2, hidden2, out_far2 = run_expert(place, far_other, spread_other, pieces)

    d_far = (d_far.astype(f32) + shift(d_far2, "c", 1).astype(f32)).astype(bf16)
    d_far = d_far.reshape(4, 4, 32, 2176)
    part_a = sum_near([d_far[s, :, :, :1024] for s in range(4)], "x").astype(bf16)
    part_b = sum_near([d_far[:, s, :, 1024:] for s in range(4)], "y").astype(bf16)
    d_own = jnp.concatenate(
        [
            sum_near([part_a[s] for s in range(4)], "y"),
            sum_near([part_b[s] for s in range(4)], "x"),
        ],
        axis=1,
    )

    out_far = (out_far.astype(f32) + shift(out_far2, "c", 1).astype(f32)).astype(bf16)
    out_far = out_far.reshape(4, 128, dim)
    out_far = sum_near([out_far[s] for s in range(4)], "x").astype(bf16).reshape(4, 32, dim)
    out_far = sum_near([out_far[s] for s in range(4)], "y")
    mixed = (middle + to_far(out_far)).astype(bf16)
    mixed = leave(gather_at(mixed, "y").reshape(128, dim))

    grad_ffn = expert_grad(
        (far, far_other), (spread, spread_other), (d_hidden, d_hidden2), (hidden, hidden2)
    )
    grad_ffn = lax.psum_scatter(grad_ffn, "z", scatter_dimension=0, tiled=True)
    grad_ffn = exchange_at(grad_ffn.reshape(4, 128, 1336), "x").reshape(4, 2, 64, 1336)
    mine_g, other_g = pick(grad_ffn, ci, 1), shift(pick(grad_ffn, 1 - ci, 1), "c", 1)
    grad_ffn = jnp.stack(
        [jnp.where(is_first, mine_g, other_g), jnp.where(is_first, other_g, mine_g)], axis=1
    )
    grad_ffn = grad_ffn.reshape(8, 64, 1336).transpose(1, 0, 2).astype(f32)
    g_expert_in = jnp.stack([grad_ffn[..., :352], grad_ffn[..., 440:792]], axis=2)
    g_shared_in = jnp.stack(
        [grad_ffn[..., 352:440].reshape(64, 704), grad_ffn[..., 792:880].reshape(64, 704)], axis=1
    )
    g_expert_out = grad_ffn[..., 896:1248]
    g_shared_out = grad_ffn[..., 1248:].reshape(64, 704)

    router = jax.nn.softmax(dot_nn(normed_ffn, router_w), axis=-1)
    d_chosen = d_own[:, 2048:2056] * chosen_own
    d_logits = (router * (d_chosen - jnp.sum(router * d_chosen, axis=-1, keepdims=True))).astype(bf16)
    d_normed_ffn = to_far(d_own[:, :2048]) + dot_nt(d_logits, router_w)
    d_middle_norm, d_gain_two = norm_backward(middle, factor_two, gain_second, d_normed_ffn)
    d_middle = d_out_own.astype(f32) + d_middle_norm
    g_router = dot_tn(normed_ffn, d_logits)

    half = ROPE // 2
    freq = jnp.exp(jnp.arange(half, dtype=f32) * (-jnp.log(10000.0) / half))
    angle = position.astype(f32)[:, None] * freq[None, :]
    cosine = jnp.tile(jnp.cos(angle), (1, 8))
    sine = jnp.tile(jnp.concatenate([jnp.sin(angle), -jnp.sin(angle)], axis=1), (1, 4))
    d_q, d_rot, d_expanded, d_branch, *rest = attend_back(
        place, gather_near(d_middle.astype(bf16), "y"), query, kv, prob, latent_all, attn_all,
        cosine, sine,
    )
    terms_a = sum_near(rest[0:4], "x").astype(bf16).reshape(4, 128, 256)
    terms_b = sum_near(rest[4:8], "z").astype(bf16)
    terms = jnp.concatenate(
        [
            sum_near([terms_a[s] for s in range(4)], "z"),
            sum_near([terms_b[s] for s in range(4)], "x"),
        ],
        axis=1,
    ).astype(bf16)
    terms = sum_at(terms.reshape(4, 32, 576), "y", 0)
    d_query_own = sum_ahead(rest[8:12], "y")

    d_comp_latent, d_latent_gain = norm_backward(
        own(compressed)[:, :RANK], own(factor_latent), latent_gain, terms[:, :RANK]
    )
    d_compressed = jnp.concatenate(
        [d_comp_latent, rotate_parts(terms[:, RANK:], own(position), True)], axis=1
    ).astype(bf16)
    d_normed = d_query_own + dot_nt(d_compressed, compress_w)
    d_inputs, d_gain_one = norm_backward(inputs_own, own(factor_one), gain_first, d_normed)
    grad_rows = (d_middle + d_inputs).astype(bf16)
    grad_rows = leave(gather_at(grad_rows, "y").reshape(128, dim))

    def fsdp_sum(value, first, second):
        value = value.reshape(4, 4, 2, 64, -1)
        value = sum_ahead([pick(value, ci, 2), pick(value, 1 - ci, 2)], "c").astype(bf16)
        value = sum_at(value, first, 0 if first == "x" else 1).astype(bf16)
        return sum_at(value, second, 0)

    g_attn = attn_grad(normed, d_q, d_rot, d_branch, attended)
    g_query = fsdp_sum(g_attn[:, :768], "x", "z")
    g_query = jnp.concatenate(
        [g_query[:, :512].reshape(64, heads, NOPE), g_query[:, 512:].reshape(64, heads, ROPE)],
        axis=-1,
    ).reshape(64, 768)
    g_expand = dot_tn(latent_all[:, :RANK], d_expanded)
    g_expand = (
        g_expand.astype(bf16)
        .reshape(32, 16, heads, 256)
        .transpose(0, 2, 1, 3)
        .reshape(2048, 256)
    )
    g_other = fsdp_sum(jnp.concatenate([g_attn[:, 768:], g_expand], axis=1), "z", "x")
    g_output = g_other[:, :512]
    g_expand = (
        g_other[:, 512:].reshape(heads, 16, 256).transpose(1, 0, 2).reshape(16, heads * 256)
    )

    d_compressed_all = gather_at(d_compressed, "y").reshape(128, 576)
    d_compressed_mine = jnp.concatenate(
        [
            lax.dynamic_slice_in_dim(d_compressed_all[:, :RANK], yi * 128, 128, 1),
            d_compressed_all[:, RANK:],
        ],
        axis=1,
    )
    g_compress = dot_tn(normed, d_compressed_mine)
    g_small = jnp.concatenate(
        [
            g_compress,
            d_gain_one[:, None],
            d_gain_two[:, None],
            g_router,
            jnp.pad(d_latent_gain.reshape(32, 16), ((0, 0), (0, 48))).reshape(dim, 1),
            jnp.zeros((dim, 53), f32),
        ],
        axis=1,
    ).astype(bf16)
    g_small = gather_at(fsdp_sum(g_small, "x", "z").astype(bf16), "y").astype(f32)
    g_compress = jnp.concatenate(
        [g_small[i, :, :128] for i in range(4)] + [g_small[0, :, 128:192]], axis=1
    )
    g_small = jnp.sum(g_small[:, :, 192:], axis=0)

    return (
        mixed,
        grad_rows,
        g_small[:, 0],
        g_query,
        g_compress,
        g_small[:16, 10],
        g_expand,
        g_output,
        g_small[:, 1],
        g_small[:, 2:10],
        g_expert_in,
        g_expert_out,
        g_shared_in,
        g_shared_out,
    )


def solution(mesh):
    fine = Mesh(mesh.devices.reshape(4, 4, 2, 4), ("x", "z", "c", "y"))
    rows = ("x", "z", "c")
    return jax.shard_map(
        on_device,
        mesh=fine,
        in_specs=(
            P(None, rows, None),
            P(),
            P(None, rows, None),
            P(None, rows, None),
            P(rows),
            P(rows, "y"),
            P(rows, None),
            P(rows),
            P(rows, "y"),
            P(rows, "y"),
            P(rows),
            P(rows, None),
            P(rows, None, None, "y"),
            P(rows, None, "y"),
            P(rows, None, "y"),
            P(rows, "y"),
        ),
        out_specs=(
            P(None, rows, None),
            P(None, rows, None),
            P(rows),
            P(rows, "y"),
            P(rows, None),
            P(rows),
            P(rows, "y"),
            P(rows, "y"),
            P(rows),
            P(rows, None),
            P(rows, None, None, "y"),
            P(rows, None, "y"),
            P(rows, None, "y"),
            P(rows, "y"),
        ),
        check_vma=False,
    )
```

time: 1840 us -> 683 us (0.37)
  waiting for transfers between devices: 1210 us -> 223 us
  matrix products: 279 us -> 14.7 us
  blocking collectives: 188 us -> 0 us
  starting transfers between devices: 2.72 us -> 172 us
  Pallas kernels: 0 us -> 70 us
  local copies, waits for them, and re-layouts: 77.8 us -> 125 us
    reduce_scatter x9 -> x1, waiting for transfers between devices: 675 us -> 0.02 us  [on_device(): grad_ffn = lax.psum_scatter(grad_ffn, 'z', scatter_dimension=0, tiled=True)]
    all_gather x10 -> x2, waiting for transfers between devices: 371 us -> 47.6 us  [the longest x1 28.2 us: on_device(): lax.all_gather(jnp.concatenate([by_head[:, :, :NOPE].reshape(64, 512), by...]
    dot_general x72 -> x8, matrix products: 279 us -> 14.7 us  [the longest x3 7.57 us: dot_nn(): return jnp.dot(a, b, preferred_element_type=f32)]
    ppermute x0 -> x121, waiting for transfers between devices: none -> 175 us  [shift(): lax.ppermute(value, axis, [(i, (i + step) % count) for i in range(count)])]
    ppermute x0 -> x121, starting transfers between devices: none -> 172 us  [shift(): lax.ppermute(value, axis, [(i, (i + step) % count) for i in range(count)])]
    unnamed x2 -> x0, blocking collectives: 136 us -> none
    unnamed x26 -> x3, waiting for transfers between devices: 81.7 us -> 0.05 us
    psum x3 -> x0, waiting for transfers between devices: 77.4 us -> none  [the longest x1 40.1 us: on_device(): lax.psum(d_normed_part.astype(jnp.bfloat16), 'tensor').astype(jnp.float32)]
  transfers between devices with their start and end apart: 24 -> 124, of which waited for: 22 -> 43; matrix products, arithmetic and copies ran while one was open for 16% -> 23% of each run, Pallas kernels for 0% -> 9%
where the time goes in v1:
time: 683 us; the launch traced here: 673 us
  waiting for transfers between devices  223 us (33%)
  starting transfers between devices  172 us (25%)
  local copies, waits for them, and re-layouts  125 us (18%)
  Pallas kernels  70 us (10%)
  other arithmetic  51.7 us (8%)
  between operations  16.2 us (2%)
  matrix products  14.7 us (2%)
    ppermute x121, waiting for transfers between devices, shift(): lax.ppermute(value, axis, [(i, (i + step) % count) for i in range(count)])  175 us
    ppermute x121, starting transfers between devices, shift(): lax.ppermute(value, axis, [(i, (i + step) % count) for i in range(count)])  172 us
    all_gather x1, waiting for transfers between devices, on_device(): lax.all_gather(jnp.concatenate([by_head[:, :, :NOPE].reshape(64, 512), by...  28.2 us
    pallas_call x2, Pallas kernels, run_expert(): pl.pallas_call(expert_kernel, grid=(512 // rows,), in_specs=[SCALARS, by_...  25.4 us
    unnamed x186, local copies, waits for them, and re-layouts  24.7 us
    all_gather x1, waiting for transfers between devices, on_device(): small_all = lax.all_gather(small, ('x', 'z', 'c'), axis=0, tiled=True)  19.3 us
    pallas_call x1, Pallas kernels, attend_back(): pl.pallas_call(attend_back_kernel, grid=(4,), in_specs=[SCALARS] + [whole...  16 us
    pallas_call x1, Pallas kernels, attend(): pl.pallas_call(attend_kernel, grid=(4,), in_specs=[SCALARS, pl.BlockSpec(...  14.4 us
  transfers between devices with their start and end apart: 124, of which 43 were waited for; matrix products, arithmetic and copies ran while one was open for 23% of the time, Pallas kernels for 9%

profile of v1, /device:TPU:0, one launch (start us, length us, event | category | flops | bytes accessed | tf_op | source)
XLA Modules:
  0.0 673.0 jit_solution(7380002306663944080)
XLA Ops:
  20.9 4.1 constant_dynamic-slice_fusion.2
  40.0 19.3 %all-gather.3.cloned.1.call-done = bf16[2048,640]{1,0:T(8,128)(2,1)} async-done(((bf16[64,640]{1,0:T(8,128)(2,1)}), bf16[2048,640]{1,0:T(8,128)(2,1)}) %all-gather.3.cloned.1.call-update) | async-done | bytes 2621456 | tf_op jit(solution)/shard_map/all_gather | solution.py:477
  60.9 2.7 convert_reduce_fusion
  67.7 2.7 collective-permute-start.2
  73.1 2.7 collective-permute-start.8
  79.9 2.5 collective-permute-start.6
  84.1 4.4 collective-permute-start.10
  88.5 28.2 %all-gather.5.cloned.1.call-done.out_w.nope_w.rot_w = bf16[2048,1536]{1,0:T(8,128)(2,1)} async-done(((bf16[64,1536]{1,0:T(8,128)(2,1)}), bf16[2048,1536]{1,0:T(8,128)(2,1)}) %all-gather.5.cloned.1.call-update) | async-done | bytes 6291472 | tf_op jit(solution)/shard_map/all_gather | solution.py:485
  137.9 14.4 %attend.1 = (f32[4,128,2048]{2,1,0:T(8,128)}, bf16[2048,1024]{1,0:T(8,128)(2,1)}, bf16[128,512]{1,0:T(8,128)(2,1)S(1)}, bf16[2048,576]{1,0:T(8,128)(2,1)}, bf16[...) custom-call(s32[4]{0:T(128)S(1)} %pad_add_fusion.2.place, ...), custom_call_target="tpu_custom_call" | custom-call | flops 5000000000 | bytes 22000000 | tf_op jit(solution)/shard_map/attend/pallas_call | solution.py:172
  153.9 2.7 collective-permute-start.14
  158.6 2.7 collective-permute-start.15
  166.1 3.0 collective-permute-start.17
  173.5 3.9 collective-permute-start.23
  181.5 2.6 collective-permute-start.21
  184.3 3.8 collective-permute-start.26
  191.7 2.6 collective-permute-start.35
  194.7 3.9 collective-permute-done.26
  202.9 6.8 %collective-permute-done.35 = bf16[128,1336]{1,0:T(8,128)(2,1)S(1)} collective-permute-done((bf16[128,1336]{1,0:T(8,128)(2,1)S(1)}, bf16[128,1336]{1,0:T(8,128)(2,1)S(1)}, u32[]{:S(2)}, u32[]{:S(2)}) %collective-permute-start.35) | collective-permute-done | bytes 342048 | tf_op jit(solution)/shard_map/ppermute | solution.py:54
  211.2 2.5 collective-permute-start.36
  213.8 4.1 collective-permute-start.37
  217.8 2.8 collective-permute-start.38
  221.9 22.8 %collective-permute-done.36 = bf16[512,1336]{0,1:T(8,128)(2,1)} collective-permute-done((bf16[512,1336]{0,1:T(8,128)(2,1)}, bf16[512,1336]{0,1:T(8,128)(2,1)}, u32[]{:S(2)}, u32[]{:S(2)}) %collective-permute-start.36) | collective-permute-done | bytes 1368096 | tf_op jit(solution)/shard_map/ppermute | solution.py:54
  246.6 26.9 %collective-permute-done.37 = bf16[512,1336]{0,1:T(8,128)(2,1)} collective-permute-done((bf16[512,1336]{0,1:T(8,128)(2,1)}, bf16[512,1336]{0,1:T(8,128)(2,1)}, u32[]{:S(2)}, u32[]{:S(2)}) %collective-permute-start.37) | collective-permute-done | bytes 1368096 | tf_op jit(solution)/shard_map/ppermute | solution.py:54
  279.9 12.6 %expert.3 = (bf16[512,2176]{1,0:T(8,128)(2,1)}, bf16[512,896]{1,0:T(8,128)(2,1)S(1)}, bf16[512,512]{1,0:T(8,128)(2,1)S(1)}, bf16[512,2048]{1,0:T(8,128)(2,1)}) custom-call(s32[4]{0:T(128)S(1)} %pad_add_fusion.2.place, bf16[512,2048]{1,0:T(8,128)(2,1)} %collective-permute-done.39.far.x1, bf16[512,2176]{1,0:T(8,128)(2,1)} %collective-permute-done.40.spread.y1, ...), custom_call_target="tpu_custom_call" | custom-call | flops 6000000000 | bytes 18000000 | tf_op jit(solution)/shard_map/expert/pallas_call | solution.py:365
  310.6 2.8 fusion.122
  318.1 12.8 %expert.2 = (bf16[512,2176]{1,0:T(8,128)(2,1)}, bf16[512,896]{1,0:T(8,128)(2,1)S(1)}, bf16[512,512]{1,0:T(8,128)(2,1)S(1)}, bf16[512,2048]{1,0:T(8,128)(2,1)}) custom-call(s32[4]{0:T(128)S(1)} %pad_add_fusion.2.place, bf16[512,2048]{1,0:T(8,128)(2,1)} %pad_maximum_fusion.far.x0, bf16[512,2176]{1,0:T(8,128)(2,1)} %constant_dynamic-update-slice_fusion.spread.y0, ...), custom_call_target="tpu_custom_call" | custom-call | flops 6000000000 | bytes 18000000 | tf_op jit(solution)/shard_map/expert/pallas_call | solution.py:365
  330.9 10.3 %expert_grad.1 = bf16[2048,1336]{1,0:T(8,128)(2,1)} custom-call(bf16[512,2048]{1,0:T(8,128)(2,1)} %pad_maximum_fusion.far.x0, bf16[512,2048]{1,0:T(8,128)(2,1)} %collective-permute-done.39.far.x1, bf16[512,2176]{1,0:T(8,128)(2,1)} %constant_dynamic-update-slice_fusion.spread.y0, bf16[512,2176]{1,0:T(8,128)(2,1)} %collective-permute-done.40.spread.y1, ...), custom_call_target="tpu_custom_call" | custom-call | flops 6000000000 | bytes 18000000 | tf_op jit(solution)/shard_map/expert_grad/pallas_call | solution.py:394
  341.3 3.0 add_convert_fusion.1
  345.5 3.8 collective-permute-start.42
  353.4 2.7 collective-permute-start.54
  357.5 25.8 %collective-permute-done.53 = bf16[4,32,1024]{2,1,0:T(8,128)(2,1)S(1)} collective-permute-done((bf16[4,32,1024]{2,1,0:T(8,128)(2,1)S(1)}, bf16[4,32,1024]{2,1,0:T(8,128)(2,1)S(1)}, u32[]{:S(2)}, u32[]{:S(2)}) %collective-permute-start.53) | collective-permute-done | bytes 262176 | tf_op jit(solution)/shard_map/ppermute | solution.py:54
  386.2 7.1 %collective-permute-done.59 = bf16[4,32,1152]{2,1,0:T(8,128)(2,1)S(1)} collective-permute-done((bf16[4,32,1152]{2,1,0:T(8,128)(2,1)S(1)}, bf16[4,32,1152]{2,1,0:T(8,128)(2,1)S(1)}, u32[]{:S(2)}, u32[]{:S(2)}) %collective-permute-start.59) | collective-permute-done | bytes 294944 | tf_op jit(solution)/shard_map/ppermute | solution.py:54
  395.5 3.5 collective-permute-start.57
  402.3 4.0 collective-permute-start.62
  409.9 2.7 collective-permute-done.63
  432.3 16.0 %attend_back.1 = (bf16[128,512]{1,0:T(8,128)(2,1)}, bf16[128,256]{1,0:T(8,128)(2,1)}, bf16[2048,1024]{1,0:T(8,128)(2,1)}, bf16[128,2048]{1,0:T(8,128)(2,1)}, bf1...) custom-call(s32[4]{0:T(128)} %copy-done.8, ...), custom_call_target="tpu_custom_call" | custom-call | flops 8000000000 | bytes 30000000 | tf_op jit(solution)/shard_map/attend_back/pallas_call | solution.py:267
  451.1 3.9 attn_grad.1
  455.0 3.9 slice.439
  471.9 2.8 dynamic-slice_bitcast_fusion
  474.7 3.5 collective-permute-done.48
  479.0 5.7 collective-permute-done.49
  486.5 3.2 collective-permute-done.50
  489.8 3.5 collective-permute-start.78
  496.0 5.7 collective-permute-done.77
  503.5 3.5 collective-permute-start.75
  511.3 3.0 collective-permute-start.80
  517.5 2.9 collective-permute-done.81
  521.6 4.3 collective-permute-start.84
  546.0 2.7 collective-permute-start.88
  552.4 5.2 concatenate.178
  562.0 2.7 collective-permute-start.95
  565.6 6.3 collective-permute-done.94
  572.6 2.8 collective-permute-start.97
  583.4 2.6 collective-permute-start.102
  593.1 4.0 collective-permute-start.112
  601.1 3.4 collective-permute-start.105
  605.1 2.6 collective-permute-start.106
  607.8 3.6 collective-permute-done.112
  614.0 4.0 collective-permute-start.115
  622.3 5.8 collective-permute-done.117
  628.7 9.2 %collective-permute-done.118 = bf16[128,1336]{1,0:T(8,128)(2,1)S(1)} collective-permute-done((bf16[128,1336]{1,0:T(8,128)(2,1)S(1)}, bf16[128,1336]{1,0:T(8,128)(2,1)S(1)}, u32[]{:S(2)}, u32[]{:S(2)}) %collective-permute-start.118) | collective-permute-done | bytes 342048 | tf_op jit(solution)/shard_map/ppermute | solution.py:54
  645.4 2.7 collective-permute-done.108
  650.2 3.8 copy.399
  654.0 3.6 reshape.1306
  (641 shorter events, 266.4 us)
Async XLA Ops:
  7.2 52.1 %all-gather.3.cloned.1.call-start = ((), (), s32[]{:S(2)}) async-start(), calls=%async_computation.1 | async-start | bytes 2703360 | tf_op jit(solution)/shard_map/all_gather | solution.py:477
  12.1 104.6 %all-gather.5.cloned.1.call-start = ((), (), s32[]{:S(2)}) async-start(), calls=%async_computation.2 | async-start | bytes 6488064 | tf_op jit(solution)/shard_map/all_gather | solution.py:485
  15.7 595.9 %reduce-scatter.2.cloned.1.call-start = ((), (), s32[]{:S(2)}) async-start(), calls=%async_computation.3 | async-start | bytes 7208960 | tf_op jit(solution)/shard_map/reduce_scatter | solution.py:616
  25.1 12.5 %collective-permute-start.32 = (bf16[4,64,1336]{2,1,0:T(8,128)(2,1)S(1)}, bf16[4,64,1336]{2,1,0:T(8,128)(2,1)}, u32[]{:S(2)}, u32[]{:S(2)}) collective-permute-start(bf16[4,64,1336]{2,1,0:T(8,128)(2,1)S(1)} %bitcast.461), channel_id=1, source_target_pairs={{0,4},{4,0},{1,5},{5,1},{2,6},{6,2},{3,7},{7,3},{8,12},{12,8},{9,1... | collective-permute-start | bytes 2052104 | tf_op jit(solution)/shard_map/ppermute | solution.py:54
  77.8 44.5 %collective-permute-start.4 = (bf16[512,256]{1,0:T(8,128)(2,1)S(1)}, bf16[512,256]{1,0:T(8,128)(2,1)}, u32[]{:S(2)}, u32[]{:S(2)}) collective-permute-start(bf16[512,256]{1,0:T(8,128)(2,1)S(1)} %pad_maximum_fusion.10.a0), channel_id=1, source_target_pairs={{0,8},{8,16},{16,24},{24,0},{1,9},{9,17},{17,25},{25,1},{2,10},{10... | collective-permute-start | bytes 786440 | tf_op jit(solution)/shard_map/ppermute | solution.py:54
  78.6 52.1 %collective-permute-start.5 = (bf16[512,256]{1,0:T(8,128)(2,1)S(1)}, bf16[512,256]{1,0:T(8,128)(2,1)}, u32[]{:S(2)}, u32[]{:S(2)}) collective-permute-start(bf16[512,256]{1,0:T(8,128)(2,1)S(1)} %pad_maximum_fusion.10.a0), channel_id=1, source_target_pairs={{0,16},{8,24},{16,0},{24,8},{1,17},{9,25},{17,1},{25,9},{2,18},{10... | collective-permute-start | bytes 786440 | tf_op jit(solution)/shard_map/ppermute | solution.py:54
  79.9 52.8 %collective-permute-start.6 = (bf16[512,256]{1,0:T(8,128)(2,1)S(1)}, bf16[512,256]{1,0:T(8,128)(2,1)}, u32[]{:S(2)}, u32[]{:S(2)}) collective-permute-start(bf16[512,256]{1,0:T(8,128)(2,1)S(1)} %pad_maximum_fusion.10.a0), channel_id=1, source_target_pairs={{0,24},{8,0},{16,8},{24,16},{1,25},{9,1},{17,9},{25,17},{2,26},{10... | collective-permute-start | bytes 786440 | tf_op jit(solution)/shard_map/ppermute | solution.py:54
  84.1 50.4 %collective-permute-start.10 = (bf16[512,320]{1,0:T(8,128)(2,1)S(1)}, bf16[512,320]{1,0:T(8,128)(2,1)S(1)}, u32[]{:S(2)}, u32[]{:S(2)}) collective-permute-start(bf16[512,320]{1,0:T(8,128)(2,1)S(1)} %pad_maximum_fusion.7.b0), channel_id=1, source_target_pairs={{0,32},{32,64},{64,96},{96,0},{1,33},{33,65},{65,97},{97,1},{2,34}... | collective-permute-start | bytes 983048 | tf_op jit(solution)/shard_map/ppermute | solution.py:54
  88.5 47.7 %collective-permute-start.11 = (bf16[512,320]{1,0:T(8,128)(2,1)S(1)}, bf16[512,320]{1,0:T(8,128)(2,1)S(1)}, u32[]{:S(2)}, u32[]{:S(2)}) collective-permute-start(bf16[512,320]{1,0:T(8,128)(2,1)S(1)} %pad_maximum_fusion.7.b0), channel_id=1, source_target_pairs={{0,64},{32,96},{64,0},{96,32},{1,65},{33,97},{65,1},{97,33},{2,66}... | collective-permute-start | bytes 983048 | tf_op jit(solution)/shard_map/ppermute | solution.py:54
  122.3 14.6 %collective-permute-start.12 = (bf16[512,320]{1,0:T(8,128)(2,1)S(1)}, bf16[512,320]{1,0:T(8,128)(2,1)}, u32[]{:S(2)}, u32[]{:S(2)}) collective-permute-start(bf16[512,320]{1,0:T(8,128)(2,1)S(1)} %pad_maximum_fusion.7.b0), channel_id=1, source_target_pairs={{0,96},{32,0},{64,32},{96,64},{1,97},{33,1},{65,33},{97,65},{2,98}... | collective-permute-start | bytes 983048 | tf_op jit(solution)/shard_map/ppermute | solution.py:54
  130.7 27.9 %collective-permute-start.29 = (bf16[128,2176]{1,0:T(8,128)(2,1)}, bf16[128,2176]{1,0:T(8,128)(2,1)S(1)}, u32[]{:S(2)}, u32[]{:S(2)}) collective-permute-start(bf16[128,2176]{1,0:T(8,128)(2,1)} %pad_maximum_fusion.4), channel_id=1, source_target_pairs={{0,32},{32,64},{64,96},{96,0},{1,33},{33,65},{65,97},{97,1},{2,34}... | collective-permute-start | bytes 1671176 | tf_op jit(solution)/shard_map/ppermute | solution.py:54
  132.7 36.4 %collective-permute-start.30 = (bf16[128,2176]{1,0:T(8,128)(2,1)}, bf16[128,2176]{1,0:T(8,128)(2,1)}, u32[]{:S(2)}, u32[]{:S(2)}) collective-permute-start(bf16[128,2176]{1,0:T(8,128)(2,1)} %pad_maximum_fusion.4), channel_id=1, source_target_pairs={{0,64},{32,96},{64,0},{96,32},{1,65},{33,97},{65,1},{97,33},{2,66}... | collective-permute-start | bytes 1671176 | tf_op jit(solution)/shard_map/ppermute | solution.py:54
  134.4 43.3 %collective-permute-start.31 = (bf16[128,2176]{1,0:T(8,128)(2,1)}, bf16[128,2176]{1,0:T(8,128)(2,1)}, u32[]{:S(2)}, u32[]{:S(2)}) collective-permute-start(bf16[128,2176]{1,0:T(8,128)(2,1)} %pad_maximum_fusion.4), channel_id=1, source_target_pairs={{0,96},{32,0},{64,32},{96,64},{1,97},{33,1},{65,33},{97,65},{2,98}... | collective-permute-start | bytes 1671176 | tf_op jit(solution)/shard_map/ppermute | solution.py:54
  162.1 22.1 %collective-permute-start.33 = (bf16[128,1336]{1,0:T(8,128)(2,1)}, bf16[128,1336]{1,0:T(8,128)(2,1)S(1)}, u32[]{:S(2)}, u32[]{:S(2)}) collective-permute-start(bf16[128,1336]{1,0:T(8,128)(2,1)} %get-tuple-element.230), channel_id=1, source_target_pairs={{0,32},{32,64},{64,96},{96,0},{1,33},{33,65},{65,97},{97,1},{2,34}... | collective-permute-start | bytes 1026056 | tf_op jit(solution)/shard_map/ppermute | solution.py:54
  177.7 11.8 %collective-permute-start.19 = (bf16[128,1024]{1,0:T(8,128)(2,1)S(1)}, bf16[128,1024]{1,0:T(8,128)(2,1)S(1)}, u32[]{:S(2)}, u32[]{:S(2)}) collective-permute-start(bf16[128,1024]{1,0:T(8,128)(2,1)S(1)} %pad_maximum_fusion.11), channel_id=1, source_target_pairs={{0,1},{1,2},{2,3},{3,0},{4,5},{5,6},{6,7},{7,4},{8,9},{9,10},{10,1... | collective-permute-start | bytes 786440 | tf_op jit(solution)/shard_map/ppermute | solution.py:54
  184.3 14.4 %collective-permute-start.26 = (bf16[128,1024]{1,0:T(8,128)(2,1)S(1)}, bf16[128,1024]{1,0:T(8,128)(2,1)S(1)}, u32[]{:S(2)}, u32[]{:S(2)}) collective-permute-start(bf16[128,1024]{1,0:T(8,128)(2,1)S(1)} %get-tuple-element.272), channel_id=1, source_target_pairs={{0,64},{32,96},{64,0},{96,32},{1,65},{33,97},{65,1},{97,33},{2,66}... | collective-permute-start | bytes 786440 | tf_op jit(solution)/shard_map/ppermute | solution.py:54
  189.5 11.7 %collective-permute-start.27 = (bf16[128,1024]{1,0:T(8,128)(2,1)S(1)}, bf16[128,1024]{1,0:T(8,128)(2,1)S(1)}, u32[]{:S(2)}, u32[]{:S(2)}) collective-permute-start(bf16[128,1024]{1,0:T(8,128)(2,1)S(1)} %get-tuple-element.272), channel_id=1, source_target_pairs={{0,96},{32,0},{64,32},{96,64},{1,97},{33,1},{65,33},{97,65},{2,98}... | collective-permute-start | bytes 786440 | tf_op jit(solution)/shard_map/ppermute | solution.py:54
  190.3 12.6 %collective-permute-start.34 = (bf16[128,1336]{1,0:T(8,128)(2,1)S(1)}, bf16[128,1336]{1,0:T(8,128)(2,1)S(1)}, u32[]{:S(2)}, u32[]{:S(2)}) collective-permute-start(bf16[128,1336]{1,0:T(8,128)(2,1)S(1)} %copy-done.46), channel_id=1, source_target_pairs={{0,64},{32,96},{64,0},{96,32},{1,65},{33,97},{65,1},{97,33},{2,66}... | collective-permute-start | bytes 1026056 | tf_op jit(solution)/shard_map/ppermute | solution.py:54
  191.7 18.0 %collective-permute-start.35 = (bf16[128,1336]{1,0:T(8,128)(2,1)S(1)}, bf16[128,1336]{1,0:T(8,128)(2,1)S(1)}, u32[]{:S(2)}, u32[]{:S(2)}) collective-permute-start(bf16[128,1336]{1,0:T(8,128)(2,1)S(1)} %copy-done.45), channel_id=1, source_target_pairs={{0,96},{32,0},{64,32},{96,64},{1,97},{33,1},{65,33},{97,65},{2,98}... | collective-permute-start | bytes 1026056 | tf_op jit(solution)/shard_map/ppermute | solution.py:54
  194.7 83.8 %collective-permute-start.40 = (bf16[512,2176]{1,0:T(8,128)(2,1)}, bf16[512,2176]{1,0:T(8,128)(2,1)}, u32[]{:S(2)}, u32[]{:S(2)}) collective-permute-start(bf16[512,2176]{1,0:T(8,128)(2,1)} %constant_dynamic-update-slice_fusion.spread.y0), channel_id=1, source_target_pairs={{0,4},{4,0},{1,5},{5,1},{2,6},{6,2},{3,7},{7,3},{8,12},{12,8},{9,1... | collective-permute-start | bytes 6684680 | tf_op jit(solution)/shard_map/ppermute | solution.py:54
  202.8 75.6 %collective-permute-start.39 = (bf16[512,2048]{1,0:T(8,128)(2,1)}, bf16[512,2048]{1,0:T(8,128)(2,1)}, u32[]{:S(2)}, u32[]{:S(2)}) collective-permute-start(bf16[512,2048]{1,0:T(8,128)(2,1)} %pad_maximum_fusion.far.x0), channel_id=1, source_target_pairs={{0,4},{4,0},{1,5},{5,1},{2,6},{6,2},{3,7},{7,3},{8,12},{12,8},{9,1... | collective-permute-start | bytes 6291464 | tf_op jit(solution)/shard_map/ppermute | solution.py:54
  211.2 33.5 %collective-permute-start.36 = (bf16[512,1336]{0,1:T(8,128)(2,1)}, bf16[512,1336]{0,1:T(8,128)(2,1)}, u32[]{:S(2)}, u32[]{:S(2)}) collective-permute-start(bf16[512,1336]{0,1:T(8,128)(2,1)} %copy.367), channel_id=1, source_target_pairs={{0,8},{8,16},{16,24},{24,0},{1,9},{9,17},{17,25},{25,1},{2,10},{10... | collective-permute-start | bytes 4104200 | tf_op jit(solution)/shard_map/ppermute | solution.py:54
  213.8 59.7 %collective-permute-start.37 = (bf16[512,1336]{0,1:T(8,128)(2,1)}, bf16[512,1336]{0,1:T(8,128)(2,1)}, u32[]{:S(2)}, u32[]{:S(2)}) collective-permute-start(bf16[512,1336]{0,1:T(8,128)(2,1)} %copy.367), channel_id=1, source_target_pairs={{0,16},{8,24},{16,0},{24,8},{1,17},{9,25},{17,1},{25,9},{2,18},{10... | collective-permute-start | bytes 4104200 | tf_op jit(solution)/shard_map/ppermute | solution.py:54
  217.8 58.1 %collective-permute-start.38 = (bf16[512,1336]{0,1:T(8,128)(2,1)}, bf16[512,1336]{0,1:T(8,128)(2,1)}, u32[]{:S(2)}, u32[]{:S(2)}) collective-permute-start(bf16[512,1336]{0,1:T(8,128)(2,1)} %copy.367), channel_id=1, source_target_pairs={{0,24},{8,0},{16,8},{24,16},{1,25},{9,1},{17,9},{25,17},{2,26},{10... | collective-permute-start | bytes 4104200 | tf_op jit(solution)/shard_map/ppermute | solution.py:54
  294.2 47.0 %collective-permute-start.41 = (bf16[512,2048]{1,0:T(8,128)(2,1)}, bf16[512,2048]{1,0:T(8,128)(2,1)}, u32[]{:S(2)}, u32[]{:S(2)}) collective-permute-start(bf16[512,2048]{1,0:T(8,128)(2,1)} %get-tuple-element.51), channel_id=1, source_target_pairs={{0,4},{4,0},{1,5},{5,1},{2,6},{6,2},{3,7},{7,3},{8,12},{12,8},{9,1... | collective-permute-start | bytes 6291464 | tf_op jit(solution)/shard_map/ppermute | solution.py:54
  316.2 33.3 %collective-permute-start.52 = (bf16[512,2176]{1,0:T(8,128)(2,1)}, bf16[512,2176]{1,0:T(8,128)(2,1)}, u32[]{:S(2)}, u32[]{:S(2)}) collective-permute-start(bf16[512,2176]{1,0:T(8,128)(2,1)} %get-tuple-element.53), channel_id=1, source_target_pairs={{0,4},{4,0},{1,5},{5,1},{2,6},{6,2},{3,7},{7,3},{8,12},{12,8},{9,1... | collective-permute-start | bytes 6684680 | tf_op jit(solution)/shard_map/ppermute | solution.py:54
  345.5 78.1 %collective-permute-start.42 = (bf16[128,2048]{1,0:T(8,128)(2,1)}, bf16[128,2048]{1,0:T(8,128)(2,1)S(1)}, u32[]{:S(2)}, u32[]{:S(2)}) collective-permute-start(bf16[128,2048]{1,0:T(8,128)(2,1)} %get-tuple-element.215), channel_id=1, source_target_pairs={{0,96},{32,0},{64,32},{96,64},{1,97},{33,1},{65,33},{97,65},{2,98}... | collective-permute-start | bytes 1572872 | tf_op jit(solution)/shard_map/ppermute | solution.py:54
  349.3 75.3 %collective-permute-start.43 = (bf16[128,2048]{1,0:T(8,128)(2,1)}, bf16[128,2048]{1,0:T(8,128)(2,1)S(1)}, u32[]{:S(2)}, u32[]{:S(2)}) collective-permute-start(bf16[128,2048]{1,0:T(8,128)(2,1)} %get-tuple-element.217), channel_id=1, source_target_pairs={{0,64},{32,96},{64,0},{96,32},{1,65},{33,97},{65,1},{97,33},{2,66}... | collective-permute-start | bytes 1572872 | tf_op jit(solution)/shard_map/ppermute | solution.py:54
  352.2 31.2 %collective-permute-start.53 = (bf16[4,32,1024]{2,1,0:T(8,128)(2,1)S(1)}, bf16[4,32,1024]{2,1,0:T(8,128)(2,1)S(1)}, u32[]{:S(2)}, u32[]{:S(2)}) collective-permute-start(bf16[4,32,1024]{2,1,0:T(8,128)(2,1)S(1)} %get-tuple-element.205), channel_id=1, source_target_pairs={{0,96},{32,0},{64,32},{96,64},{1,97},{33,1},{65,33},{97,65},{2,98}... | collective-permute-start | bytes 786440 | tf_op jit(solution)/shard_map/ppermute | solution.py:54
  353.4 30.6 %collective-permute-start.54 = (bf16[4,32,1024]{2,1,0:T(8,128)(2,1)S(1)}, bf16[4,32,1024]{2,1,0:T(8,128)(2,1)S(1)}, u32[]{:S(2)}, u32[]{:S(2)}) collective-permute-start(bf16[4,32,1024]{2,1,0:T(8,128)(2,1)S(1)} %get-tuple-element.207), channel_id=1, source_target_pairs={{0,64},{32,96},{64,0},{96,32},{1,65},{33,97},{65,1},{97,33},{2,66}... | collective-permute-start | bytes 786440 | tf_op jit(solution)/shard_map/ppermute | solution.py:54
  356.1 29.8 %collective-permute-start.55 = (bf16[4,32,1024]{2,1,0:T(8,128)(2,1)S(1)}, bf16[4,32,1024]{2,1,0:T(8,128)(2,1)S(1)}, u32[]{:S(2)}, u32[]{:S(2)}) collective-permute-start(bf16[4,32,1024]{2,1,0:T(8,128)(2,1)S(1)} %get-tuple-element.206), channel_id=1, source_target_pairs={{0,32},{32,64},{64,96},{96,0},{1,33},{33,65},{65,97},{97,1},{2,34}... | collective-permute-start | bytes 786440 | tf_op jit(solution)/shard_map/ppermute | solution.py:54
  384.0 11.5 %collective-permute-start.60 = (bf16[4,32,1152]{2,1,0:T(8,128)(2,1)S(1)}, bf16[4,32,1152]{2,1,0:T(8,128)(2,1)S(1)}, u32[]{:S(2)}, u32[]{:S(2)}) collective-permute-start(bf16[4,32,1152]{2,1,0:T(8,128)(2,1)S(1)} %get-tuple-element.210), channel_id=1, source_target_pairs={{0,2},{1,3},{2,0},{3,1},{4,6},{5,7},{6,4},{7,5},{8,10},{9,11},{10,... | collective-permute-start | bytes 884744 | tf_op jit(solution)/shard_map/ppermute | solution.py:54
  385.9 14.3 %collective-permute-start.61 = (bf16[4,32,1152]{2,1,0:T(8,128)(2,1)S(1)}, bf16[4,32,1152]{2,1,0:T(8,128)(2,1)S(1)}, u32[]{:S(2)}, u32[]{:S(2)}) collective-permute-start(bf16[4,32,1152]{2,1,0:T(8,128)(2,1)S(1)} %get-tuple-element.209), channel_id=1, source_target_pairs={{0,1},{1,2},{2,3},{3,0},{4,5},{5,6},{6,7},{7,4},{8,9},{9,10},{10,1... | collective-permute-start | bytes 884744 | tf_op jit(solution)/shard_map/ppermute | solution.py:54
  409.0 15.6 %collective-permute-start.44 = (bf16[128,2048]{1,0:T(8,128)(2,1)}, bf16[128,2048]{1,0:T(8,128)(2,1)}, u32[]{:S(2)}, u32[]{:S(2)}) collective-permute-start(bf16[128,2048]{1,0:T(8,128)(2,1)} %get-tuple-element.216), channel_id=1, source_target_pairs={{0,32},{32,64},{64,96},{96,0},{1,33},{33,65},{65,97},{97,1},{2,34}... | collective-permute-start | bytes 1572872 | tf_op jit(solution)/shard_map/ppermute | solution.py:54
  417.4 12.7 %collective-permute-start.65 = (bf16[32,2048]{1,0:T(8,128)(2,1)S(1)}, bf16[32,2048]{1,0:T(8,128)(2,1)S(1)}, u32[]{:S(2)}, u32[]{:S(2)}) collective-permute-start(bf16[32,2048]{1,0:T(8,128)(2,1)S(1)} %get-tuple-element.183.d0), channel_id=1, source_target_pairs={{0,1},{1,2},{2,3},{3,0},{4,5},{5,6},{6,7},{7,4},{8,9},{9,10},{10,1... | collective-permute-start | bytes 393224 | tf_op jit(solution)/shard_map/ppermute | solution.py:54
  417.4 14.2 %collective-permute-start.66 = (bf16[32,2048]{1,0:T(8,128)(2,1)S(1)}, bf16[32,2048]{1,0:T(8,128)(2,1)S(1)}, u32[]{:S(2)}, u32[]{:S(2)}) collective-permute-start(bf16[32,2048]{1,0:T(8,128)(2,1)S(1)} %get-tuple-element.183.d0), channel_id=1, source_target_pairs={{0,2},{1,3},{2,0},{3,1},{4,6},{5,7},{6,4},{7,5},{8,10},{9,11},{10,... | collective-permute-start | bytes 393224 | tf_op jit(solution)/shard_map/ppermute | solution.py:54
  427.0 40.6 %collective-permute-start.45 = (bf16[32,2048]{1,0:T(8,128)(2,1)}, bf16[32,2048]{1,0:T(8,128)(2,1)S(1)}, u32[]{:S(2)}, u32[]{:S(2)}) collective-permute-start(bf16[32,2048]{1,0:T(8,128)(2,1)} %get-tuple-element.248), channel_id=1, source_target_pairs={{0,3},{1,0},{2,1},{3,2},{4,7},{5,4},{6,5},{7,6},{8,11},{9,8},{10,9... | collective-permute-start | bytes 393224 | tf_op jit(solution)/shard_map/ppermute | solution.py:54
  428.0 41.7 %collective-permute-start.46 = (bf16[32,2048]{1,0:T(8,128)(2,1)}, bf16[32,2048]{1,0:T(8,128)(2,1)}, u32[]{:S(2)}, u32[]{:S(2)}) collective-permute-start(bf16[32,2048]{1,0:T(8,128)(2,1)} %get-tuple-element.250), channel_id=1, source_target_pairs={{0,2},{1,3},{2,0},{3,1},{4,6},{5,7},{6,4},{7,5},{8,10},{9,11},{10,... | collective-permute-start | bytes 393224 | tf_op jit(solution)/shard_map/ppermute | solution.py:54
  430.0 39.7 %collective-permute-start.47 = (bf16[32,2048]{1,0:T(8,128)(2,1)}, bf16[32,2048]{1,0:T(8,128)(2,1)}, u32[]{:S(2)}, u32[]{:S(2)}) collective-permute-start(bf16[32,2048]{1,0:T(8,128)(2,1)} %get-tuple-element.249), channel_id=1, source_target_pairs={{0,1},{1,2},{2,3},{3,0},{4,5},{5,6},{6,7},{7,4},{8,9},{9,10},{10,1... | collective-permute-start | bytes 393224 | tf_op jit(solution)/shard_map/ppermute | solution.py:54
  466.3 124.1 %collective-permute-start.110 = (bf16[4,4,64,768]{3,2,0,1:T(8,128)(2,1)}, bf16[4,4,64,768]{3,2,0,1:T(8,128)(2,1)}, u32[]{:S(2)}, u32[]{:S(2)}) collective-permute-start(bf16[4,4,64,768]{3,2,0,1:T(8,128)(2,1)} %bitcast.419), channel_id=1, source_target_pairs={{0,4},{4,0},{1,5},{5,1},{2,6},{6,2},{3,7},{7,3},{8,12},{12,8},{9,1... | collective-permute-start | bytes 4718600 | tf_op jit(solution)/shard_map/ppermute | solution.py:54
  466.3 23.4 %collective-permute-start.71 = (bf16[512,256]{1,0:T(8,128)(2,1)}, bf16[512,256]{1,0:T(8,128)(2,1)S(1)}, u32[]{:S(2)}, u32[]{:S(2)}) collective-permute-start(bf16[512,256]{1,0:T(8,128)(2,1)} %get-tuple-element.62), channel_id=1, source_target_pairs={{0,96},{32,0},{64,32},{96,64},{1,97},{33,1},{65,33},{97,65},{2,98}... | collective-permute-start | bytes 786440 | tf_op jit(solution)/shard_map/ppermute | solution.py:54
  467.6 25.7 %collective-permute-start.72 = (bf16[512,256]{1,0:T(8,128)(2,1)}, bf16[512,256]{1,0:T(8,128)(2,1)}, u32[]{:S(2)}, u32[]{:S(2)}) collective-permute-start(bf16[512,256]{1,0:T(8,128)(2,1)} %get-tuple-element.63), channel_id=1, source_target_pairs={{0,64},{32,96},{64,0},{96,32},{1,65},{33,97},{65,1},{97,33},{2,66}... | collective-permute-start | bytes 786440 | tf_op jit(solution)/shard_map/ppermute | solution.py:54
  469.7 25.0 %collective-permute-start.73 = (bf16[512,256]{1,0:T(8,128)(2,1)}, bf16[512,256]{1,0:T(8,128)(2,1)}, u32[]{:S(2)}, u32[]{:S(2)}) collective-permute-start(bf16[512,256]{1,0:T(8,128)(2,1)} %get-tuple-element.64), channel_id=1, source_target_pairs={{0,32},{32,64},{64,96},{96,0},{1,33},{33,65},{65,97},{97,1},{2,34}... | collective-permute-start | bytes 786440 | tf_op jit(solution)/shard_map/ppermute | solution.py:54
  489.7 12.1 %collective-permute-start.77 = (bf16[4,128,320]{2,1,0:T(8,128)(2,1)S(1)}, bf16[4,128,320]{2,1,0:T(8,128)(2,1)S(1)}, u32[]{:S(2)}, u32[]{:S(2)}) collective-permute-start(bf16[4,128,320]{2,1,0:T(8,128)(2,1)S(1)} %copy-done.82), channel_id=1, source_target_pairs={{0,24},{8,0},{16,8},{24,16},{1,25},{9,1},{17,9},{25,17},{2,26},{10... | collective-permute-start | bytes 983048 | tf_op jit(solution)/shard_map/ppermute | solution.py:54
  489.8 13.7 %collective-permute-start.78 = (bf16[4,128,320]{2,1,0:T(8,128)(2,1)S(1)}, bf16[4,128,320]{2,1,0:T(8,128)(2,1)S(1)}, u32[]{:S(2)}, u32[]{:S(2)}) collective-permute-start(bf16[4,128,320]{2,1,0:T(8,128)(2,1)S(1)} %copy-done.81), channel_id=1, source_target_pairs={{0,16},{8,24},{16,0},{24,8},{1,17},{9,25},{17,1},{25,9},{2,18},{10... | collective-permute-start | bytes 983048 | tf_op jit(solution)/shard_map/ppermute | solution.py:54
  493.3 15.6 %collective-permute-start.79 = (bf16[4,128,320]{2,1,0:T(8,128)(2,1)S(1)}, bf16[4,128,320]{2,1,0:T(8,128)(2,1)S(1)}, u32[]{:S(2)}, u32[]{:S(2)}) collective-permute-start(bf16[4,128,320]{2,1,0:T(8,128)(2,1)S(1)} %copy-done.80), channel_id=1, source_target_pairs={{0,8},{8,16},{16,24},{24,0},{1,9},{9,17},{17,25},{25,1},{2,10},{10... | collective-permute-start | bytes 983048 | tf_op jit(solution)/shard_map/ppermute | solution.py:54
  494.7 39.2 %collective-permute-start.68 = (bf16[32,2048]{1,0:T(8,128)(2,1)S(1)}, bf16[32,2048]{1,0:T(8,128)(2,1)S(1)}, u32[]{:S(2)}, u32[]{:S(2)}) collective-permute-start(bf16[32,2048]{1,0:T(8,128)(2,1)S(1)} %copy-done.85), channel_id=1, source_target_pairs={{0,1},{1,2},{2,3},{3,0},{4,5},{5,6},{6,7},{7,4},{8,9},{9,10},{10,1... | collective-permute-start | bytes 393224 | tf_op jit(solution)/shard_map/ppermute | solution.py:54
  503.5 10.8 %collective-permute-start.75 = (bf16[128,256]{1,0:T(8,128)(2,1)S(1)}, bf16[128,256]{1,0:T(8,128)(2,1)S(1)}, u32[]{:S(2)}, u32[]{:S(2)}) collective-permute-start(bf16[128,256]{1,0:T(8,128)(2,1)S(1)} %get-tuple-element.267), channel_id=1, source_target_pairs={{0,16},{8,24},{16,0},{24,8},{1,17},{9,25},{17,1},{25,9},{2,18},{10... | collective-permute-start | bytes 196616 | tf_op jit(solution)/shard_map/ppermute | solution.py:54
  531.6 65.9 %collective-permute-start.103 = (bf16[4,4,64,768]{3,2,1,0:T(8,128)(2,1)}, bf16[4,4,64,768]{3,2,1,0:T(8,128)(2,1)}, u32[]{:S(2)}, u32[]{:S(2)}) collective-permute-start(bf16[4,4,64,768]{3,2,1,0:T(8,128)(2,1)} %dynamic-slice_bitcast_fusion), channel_id=1, source_target_pairs={{0,4},{4,0},{1,5},{5,1},{2,6},{6,2},{3,7},{7,3},{8,12},{12,8},{9,1... | collective-permute-start | bytes 4718600 | tf_op jit(solution)/shard_map/ppermute | solution.py:54
  544.0 14.8 %collective-permute-start.86 = (bf16[32,2048]{1,0:T(8,128)(2,1)}, bf16[32,2048]{1,0:T(8,128)(2,1)}, u32[]{:S(2)}, u32[]{:S(2)}) collective-permute-start(bf16[32,2048]{1,0:T(8,128)(2,1)} %get-tuple-element.177), channel_id=1, source_target_pairs={{0,1},{1,2},{2,3},{3,0},{4,5},{5,6},{6,7},{7,4},{8,9},{9,10},{10,1... | collective-permute-start | bytes 393224 | tf_op jit(solution)/shard_map/ppermute | solution.py:54
  544.0 15.8 %collective-permute-start.87 = (bf16[32,2048]{1,0:T(8,128)(2,1)}, bf16[32,2048]{1,0:T(8,128)(2,1)}, u32[]{:S(2)}, u32[]{:S(2)}) collective-permute-start(bf16[32,2048]{1,0:T(8,128)(2,1)} %get-tuple-element.177), channel_id=1, source_target_pairs={{0,2},{1,3},{2,0},{3,1},{4,6},{5,7},{6,4},{7,5},{8,10},{9,11},{10,... | collective-permute-start | bytes 393224 | tf_op jit(solution)/shard_map/ppermute | solution.py:54
  546.0 14.8 %collective-permute-start.88 = (bf16[32,2048]{1,0:T(8,128)(2,1)}, bf16[32,2048]{1,0:T(8,128)(2,1)}, u32[]{:S(2)}, u32[]{:S(2)}) collective-permute-start(bf16[32,2048]{1,0:T(8,128)(2,1)} %get-tuple-element.177), channel_id=1, source_target_pairs={{0,3},{1,0},{2,1},{3,2},{4,7},{5,4},{6,5},{7,6},{8,11},{9,8},{10,9... | collective-permute-start | bytes 393224 | tf_op jit(solution)/shard_map/ppermute | solution.py:54
  592.6 12.6 %collective-permute-start.111 = (bf16[4,64,768]{2,1,0:T(8,128)(2,1)S(1)}, bf16[4,64,768]{2,1,0:T(8,128)(2,1)S(1)}, u32[]{:S(2)}, u32[]{:S(2)}) collective-permute-start(bf16[4,64,768]{2,1,0:T(8,128)(2,1)S(1)} %get-tuple-element.218), channel_id=1, source_target_pairs={{0,8},{8,16},{16,24},{24,0},{1,9},{9,17},{17,25},{25,1},{2,10},{10... | collective-permute-start | bytes 1179656 | tf_op jit(solution)/shard_map/ppermute | solution.py:54
  593.1 18.2 %collective-permute-start.112 = (bf16[4,64,768]{2,1,0:T(8,128)(2,1)S(1)}, bf16[4,64,768]{2,1,0:T(8,128)(2,1)S(1)}, u32[]{:S(2)}, u32[]{:S(2)}) collective-permute-start(bf16[4,64,768]{2,1,0:T(8,128)(2,1)S(1)} %get-tuple-element.220), channel_id=1, source_target_pairs={{0,16},{8,24},{16,0},{24,8},{1,17},{9,25},{17,1},{25,9},{2,18},{10... | collective-permute-start | bytes 1179656 | tf_op jit(solution)/shard_map/ppermute | solution.py:54
  597.2 14.2 %collective-permute-start.113 = (bf16[4,64,768]{2,1,0:T(8,128)(2,1)S(1)}, bf16[4,64,768]{2,1,0:T(8,128)(2,1)S(1)}, u32[]{:S(2)}, u32[]{:S(2)}) collective-permute-start(bf16[4,64,768]{2,1,0:T(8,128)(2,1)S(1)} %get-tuple-element.219), channel_id=1, source_target_pairs={{0,24},{8,0},{16,8},{24,16},{1,25},{9,1},{17,9},{25,17},{2,26},{10... | collective-permute-start | bytes 1179656 | tf_op jit(solution)/shard_map/ppermute | solution.py:54
  600.4 13.5 %collective-permute-start.104 = (bf16[4,64,768]{2,1,0:T(8,128)(2,1)}, bf16[4,64,768]{2,1,0:T(8,128)(2,1)}, u32[]{:S(2)}, u32[]{:S(2)}) collective-permute-start(bf16[4,64,768]{2,1,0:T(8,128)(2,1)} %get-tuple-element.221), channel_id=1, source_target_pairs={{0,32},{32,64},{64,96},{96,0},{1,33},{33,65},{65,97},{97,1},{2,34}... | collective-permute-start | bytes 1179656 | tf_op jit(solution)/shard_map/ppermute | solution.py:54
  601.1 19.4 %collective-permute-start.105 = (bf16[4,64,768]{2,1,0:T(8,128)(2,1)}, bf16[4,64,768]{2,1,0:T(8,128)(2,1)}, u32[]{:S(2)}, u32[]{:S(2)}) collective-permute-start(bf16[4,64,768]{2,1,0:T(8,128)(2,1)} %get-tuple-element.223), channel_id=1, source_target_pairs={{0,64},{32,96},{64,0},{96,32},{1,65},{33,97},{65,1},{97,33},{2,66}... | collective-permute-start | bytes 1179656 | tf_op jit(solution)/shard_map/ppermute | solution.py:54
  605.1 15.3 %collective-permute-start.106 = (bf16[4,64,768]{2,1,0:T(8,128)(2,1)}, bf16[4,64,768]{2,1,0:T(8,128)(2,1)}, u32[]{:S(2)}, u32[]{:S(2)}) collective-permute-start(bf16[4,64,768]{2,1,0:T(8,128)(2,1)} %get-tuple-element.222), channel_id=1, source_target_pairs={{0,96},{32,0},{64,32},{96,64},{1,97},{33,1},{65,33},{97,65},{2,98}... | collective-permute-start | bytes 1179656 | tf_op jit(solution)/shard_map/ppermute | solution.py:54
  613.1 15.0 %collective-permute-start.117 = (bf16[128,1336]{1,0:T(8,128)(2,1)S(1)}, bf16[128,1336]{1,0:T(8,128)(2,1)S(1)}, u32[]{:S(2)}, u32[]{:S(2)}) collective-permute-start(bf16[128,1336]{1,0:T(8,128)(2,1)S(1)} %get-tuple-element.226), channel_id=1, source_target_pairs={{0,32},{32,64},{64,96},{96,0},{1,33},{33,65},{65,97},{97,1},{2,34}... | collective-permute-start | bytes 1026056 | tf_op jit(solution)/shard_map/ppermute | solution.py:54
  613.9 26.8 %collective-permute-start.114 = (bf16[64,768]{1,0:T(8,128)(2,1)S(1)}, bf16[64,768]{1,0:T(8,128)(2,1)S(1)}, u32[]{:S(2)}, u32[]{:S(2)}) collective-permute-start(bf16[64,768]{1,0:T(8,128)(2,1)S(1)} %get-tuple-element.251), channel_id=1, source_target_pairs={{0,32},{32,64},{64,96},{96,0},{1,33},{33,65},{65,97},{97,1},{2,34}... | collective-permute-start | bytes 294920 | tf_op jit(solution)/shard_map/ppermute | solution.py:54
  614.0 28.8 %collective-permute-start.115 = (bf16[64,768]{1,0:T(8,128)(2,1)S(1)}, bf16[64,768]{1,0:T(8,128)(2,1)S(1)}, u32[]{:S(2)}, u32[]{:S(2)}) collective-permute-start(bf16[64,768]{1,0:T(8,128)(2,1)S(1)} %get-tuple-element.253), channel_id=1, source_target_pairs={{0,64},{32,96},{64,0},{96,32},{1,65},{33,97},{65,1},{97,33},{2,66}... | collective-permute-start | bytes 294920 | tf_op jit(solution)/shard_map/ppermute | solution.py:54
  620.5 23.2 %collective-permute-start.116 = (bf16[64,768]{1,0:T(8,128)(2,1)S(1)}, bf16[64,768]{1,0:T(8,128)(2,1)S(1)}, u32[]{:S(2)}, u32[]{:S(2)}) collective-permute-start(bf16[64,768]{1,0:T(8,128)(2,1)S(1)} %get-tuple-element.252), channel_id=1, source_target_pairs={{0,96},{32,0},{64,32},{96,64},{1,97},{33,1},{65,33},{97,65},{2,98}... | collective-permute-start | bytes 294920 | tf_op jit(solution)/shard_map/ppermute | solution.py:54
  621.9 15.9 %collective-permute-start.118 = (bf16[128,1336]{1,0:T(8,128)(2,1)S(1)}, bf16[128,1336]{1,0:T(8,128)(2,1)S(1)}, u32[]{:S(2)}, u32[]{:S(2)}) collective-permute-start(bf16[128,1336]{1,0:T(8,128)(2,1)S(1)} %get-tuple-element.225), channel_id=1, source_target_pairs={{0,64},{32,96},{64,0},{96,32},{1,65},{33,97},{65,1},{97,33},{2,66}... | collective-permute-start | bytes 1026056 | tf_op jit(solution)/shard_map/ppermute | solution.py:54
  638.9 11.0 %collective-permute-start.120 = (bf16[4,64,1336]{2,1,0:T(8,128)(2,1)}, bf16[4,64,1336]{2,1,0:T(8,128)(2,1)S(1)}, u32[]{:S(2)}, u32[]{:S(2)}) collective-permute-start(bf16[4,64,1336]{2,1,0:T(8,128)(2,1)} %dynamic-slice_bitcast_fusion.1), channel_id=1, source_target_pairs={{0,4},{4,0},{1,5},{5,1},{2,6},{6,2},{3,7},{7,3},{8,12},{12,8},{9,1... | collective-permute-start | bytes 2052104 | tf_op jit(solution)/shard_map/ppermute | solution.py:54
  (147 other events, 1740.2 us)
Sparse Core Ops, SparseCore 0:
  12.2 47.0 all-gather.2
  62.1 54.5 all-gather.4
  341.4 60.5 reduce-scatter.1

commit v2 on v1

v2 whole, which is shorter than its diff:
```python
import jax
import jax.numpy as jnp
from jax import lax
from jax.experimental import pallas as pl
from jax.experimental.pallas import tpu as pltpu
from jax.sharding import Mesh
from jax.sharding import PartitionSpec as P

NOPE = 128
ROPE = 64
VHEAD = 128
RANK = 512
EXPERTS = 8

epsilon = 1e-06
bf16 = jnp.bfloat16
f32 = jnp.float32


def rotate_parts(values, position, inverse):
    half = values.shape[-1] // 2
    freq = jnp.exp(jnp.arange(half, dtype=f32) * (-jnp.log(10000.0) / half))
    angle = position.astype(f32)[:, None] * freq[None, :]
    cosine = jnp.cos(angle)
    sine = jnp.sin(angle)
    if inverse:
        sine = -sine
    if values.ndim == 3:
        cosine = cosine[:, None, :]
        sine = sine[:, None, :]
    first = values[..., :half]
    second = values[..., half:]
    return jnp.concatenate(
        [first * cosine - second * sine, second * cosine + first * sine], axis=-1
    )


def norm_forward(values, gain):
    factor = lax.rsqrt(jnp.mean(values * values, axis=-1, keepdims=True) + epsilon)
    return (values * factor * gain, factor)


def norm_backward(values, factor, gain, grad):
    scaled = grad * gain
    d_values = factor * scaled - values * (factor * factor * factor) * jnp.mean(
        values * scaled, axis=-1, keepdims=True
    )
    d_gain = jnp.sum(grad * values * factor, axis=0)
    return (d_values, d_gain)


def shift(value, axis, step):
    count = lax.axis_size(axis)
    return lax.ppermute(value, axis, [(i, (i + step) % count) for i in range(count)])


def pick(value, place, at):
    return lax.dynamic_index_in_dim(value, place, at, keepdims=False)


def gather_near(value, axis):
    return [value] + [shift(value, axis, s) for s in range(1, lax.axis_size(axis))]


def gather_at(value, axis):
    count = lax.axis_size(axis)
    me = lax.axis_index(axis)
    whole = jnp.zeros((count,) + value.shape, value.dtype)
    for s in range(count):
        part = value if s == 0 else shift(value, axis, s)
        whole = lax.dynamic_update_index_in_dim(whole, part, lax.rem(me - s + count, count), 0)
    return whole


def sum_near(parts, axis):
    total = parts[0].astype(f32)
    for s in range(1, len(parts)):
        total = total + shift(parts[s], axis, -s).astype(f32)
    return total


def sum_ahead(parts, axis):
    total = parts[0].astype(f32)
    for s in range(1, len(parts)):
        total = total + shift(parts[s], axis, s).astype(f32)
    return total


def sum_at(value, axis, at):
    count = lax.axis_size(axis)
    me = lax.axis_index(axis)
    return sum_ahead([pick(value, lax.rem(me + s, count), at) for s in range(count)], axis)


def exchange_at(value, axis):
    count = lax.axis_size(axis)
    me = lax.axis_index(axis)
    whole = jnp.zeros_like(value)
    for s in range(count):
        part = pick(value, lax.rem(me + s, count), 0)
        part = part if s == 0 else shift(part, axis, s)
        whole = lax.dynamic_update_index_in_dim(whole, part, lax.rem(me - s + count, count), 0)
    return whole


def to_far(value):
    rows = value.shape[0]
    return value.reshape(rows, 4, 4, 128).transpose(0, 2, 1, 3).reshape(rows, 2048)


def dot_nn(a, b):
    return jnp.dot(a, b, preferred_element_type=f32)


def dot_nt(a, b):
    return lax.dot_general(a, b, (((1,), (1,)), ((), ())), preferred_element_type=f32)


def dot_tn(a, b):
    return lax.dot_general(a, b, (((0,), (0,)), ((), ())), preferred_element_type=f32)


def whole(*shape):
    return pl.BlockSpec(shape, lambda h: (0,) * len(shape))


SCALARS = pl.BlockSpec(memory_space=pltpu.SMEM)
SCALE = (NOPE + ROPE) ** (-0.5)
MIB = 1024 * 1024


def front_kernel(
    place, tok, mine, other, cosine, sine, normed, packed, compressed, weight, gains
):
    for sx in range(4):
        for sz in range(4):
            block = lax.rem(place[0] - sx + 4, 4) * 4 + lax.rem(place[1] - sz + 4, 4)
            for part, core in ((mine, place[2]), (other, 1 - place[2])):
                row = pl.multiple_of(block * 128 + core * 64, 64)
                src = (sz * 4 + sx) * 64
                weight[pl.ds(row, 64), :] = part[src : src + 64, :]
    turned = weight[:, 512:640].astype(f32).T
    gains[0:2, :] = turned[64:66, :]
    latent_gain = jnp.concatenate(
        [turned[74:75, 64 * i : 64 * i + 16] for i in range(32)], axis=1
    )
    gains[2:3, :RANK] = latent_gain
    values = tok[...].astype(f32)
    factor = lax.rsqrt(jnp.mean(values * values, axis=1, keepdims=True) + epsilon)
    low = (values * factor * turned[64:65, :]).astype(bf16)
    normed[...] = low
    raw = dot_nn(low, weight[:, :576])
    compressed[...] = raw
    main = raw[:, :RANK]
    factor = lax.rsqrt(jnp.mean(main * main, axis=1, keepdims=True) + epsilon)
    latent = (main * factor * latent_gain).astype(bf16)
    first, second = raw[:, RANK : RANK + 32], raw[:, RANK + 32 :]
    cos, sin = cosine[:, :32], sine[:, :32]
    rot = jnp.concatenate([first * cos - second * sin, second * cos + first * sin], axis=1)
    packed[:, :RANK] = latent
    packed[:, RANK:] = jnp.concatenate([rot, jnp.zeros((128, 64), f32)], axis=1).astype(bf16)


def front(place, tok, mine, other, cosine, sine):
    return pl.pallas_call(
        front_kernel,
        in_specs=[SCALARS] + [pl.BlockSpec(memory_space=pltpu.VMEM)] * 5,
        out_specs=[pl.BlockSpec(memory_space=pltpu.VMEM)] * 5,
        out_shape=[
            jax.ShapeDtypeStruct((128, 2048), bf16),
            jax.ShapeDtypeStruct((128, 640), bf16),
            jax.ShapeDtypeStruct((128, 576), f32),
            jax.ShapeDtypeStruct((2048, 640), bf16),
            jax.ShapeDtypeStruct((8, 2048), f32),
        ],
        compiler_params=pltpu.CompilerParams(vmem_limit_bytes=32 * MIB),
        cost_estimate=pl.CostEstimate(
            flops=10**9, bytes_accessed=9 * 10**6, transcendentals=0
        ),
        name="front",
    )(place, tok, mine, other, cosine, sine)


def attend_kernel(
    place, normed, nope_w, rot_w, cosine, sine, l0, l1, l2, l3, expand, out_w,
    where_q, where_k, prob, kv, attended, lat, q, r0, r1, r2, r3, rot_q, total,
):
    head = pl.program_id(0)

    @pl.when(head == 0)
    def _():
        for sx in range(4):
            lat[sx * 512 : sx * 512 + 512, :] = (l0, l1, l2, l3)[sx][...]
        total[...] = jnp.zeros_like(total)
        rot = dot_nn(normed[...], rot_w[...])
        lane = lax.broadcasted_iota(jnp.int32, rot.shape, 1)
        partner = jnp.where(
            lane % 64 < 32, pltpu.roll(rot, 224, 1), pltpu.roll(rot, 32, 1)
        )
        rot = (rot * cosine[...] - partner * sine[...]).astype(bf16)
        for h in range(4):
            rot_q[h] = jnp.concatenate(
                [rot[:, 64 * h : 64 * h + 64], jnp.zeros((128, 64), bf16)], axis=1
            )

    nope = dot_nn(normed[...], nope_w[...]).astype(bf16)
    rot_h = rot_q[head]
    q[:, :128] = nope
    q[:, 128:] = rot_h
    expand_h = expand[...].reshape(RANK, 256)
    kv_h = dot_nn(lat[:, :RANK], expand_h).astype(bf16)
    kv[...] = kv_h
    score = (dot_nt(nope, kv_h[:, :128]) + dot_nt(rot_h, lat[:, RANK:])) * SCALE
    allowed = (where_q[:, 0:1] >= where_k[0:1, :]) & (where_q[:, 1:2] == where_k[1:2, :])
    score = jnp.where(allowed, score, -1e30)
    power = jnp.exp(score - jnp.max(score, axis=1, keepdims=True))
    prob_h = power / jnp.sum(power, axis=1, keepdims=True)
    prob[0] = prob_h
    attended_h = dot_nn(prob_h.astype(bf16), kv_h[:, 128:]).astype(bf16)
    attended[...] = attended_h
    total[...] += dot_nt(attended_h, out_w[...])

    @pl.when(head == 3)
    def _():
        for s, out in enumerate((r0, r1, r2, r3)):
            row = pl.multiple_of(lax.rem(place[3] + s, 4) * 32, 32)
            out[...] = total[pl.ds(row, 32), :].astype(bf16)


LOOSE = pl.BlockSpec(memory_space=pl.ANY)


def attend(place, normed, parts, attn_all, cosine, sine, where_q, where_k):
    by_head = attn_all.reshape(32, 4, 16, 1536)
    return pl.pallas_call(
        attend_kernel,
        grid=(4,),
        in_specs=[
            SCALARS,
            whole(128, 2048),
            pl.BlockSpec((2048, 128), lambda h: (0, h)),
            pl.BlockSpec((2048, 256), lambda h: (0, 2)),
            whole(128, 256),
            whole(128, 256),
        ]
        + [whole(512, 640)] * 4
        + [
            pl.BlockSpec((32, 1, 16, 256), lambda h: (0, h, 0, 5)),
            pl.BlockSpec((2048, 128), lambda h: (0, 6 + h)),
            whole(128, 2),
            whole(2, 2048),
        ],
        out_specs=[
            pl.BlockSpec((1, 128, 2048), lambda h: (h, 0, 0)),
            pl.BlockSpec((2048, 256), lambda h: (0, h)),
            pl.BlockSpec((128, 128), lambda h: (0, h)),
            whole(2048, 640),
            pl.BlockSpec((128, 256), lambda h: (0, h)),
        ]
        + [whole(32, 2048)] * 4,
        out_shape=[
            jax.ShapeDtypeStruct((4, 128, 2048), f32),
            jax.ShapeDtypeStruct((2048, 1024), bf16),
            jax.ShapeDtypeStruct((128, 512), bf16),
            jax.ShapeDtypeStruct((2048, 640), bf16),
            jax.ShapeDtypeStruct((128, 1024), bf16),
        ]
        + [jax.ShapeDtypeStruct((32, 2048), bf16)] * 4,
        scratch_shapes=[
            pltpu.VMEM((4, 128, 128), bf16),
            pltpu.VMEM((128, 2048), f32),
        ],
        compiler_params=pltpu.CompilerParams(vmem_limit_bytes=48 * MIB),
        cost_estimate=pl.CostEstimate(
            flops=5 * 10**9, bytes_accessed=26 * 10**6, transcendentals=2**20
        ),
        name="attend",
    )(
        place, normed, attn_all, attn_all, cosine, sine, *parts, by_head, attn_all,
        where_q, where_k,
    )


def far_block(b):
    return (b % 4) * 4 + b // 4


def middle_kernel(place, r0, r1, r2, r3, tok, gains, tie, middle, far):
    row = pl.multiple_of(place[3] * 32, 32)
    values = tok[pl.ds(row, 32), :].astype(f32)
    for part in (r0, r1, r2, r3):
        values = values + part[...].astype(f32)
    middle[...] = values
    factor = lax.rsqrt(jnp.mean(values * values, axis=1, keepdims=True) + epsilon)
    low = (values * factor * gains[1:2, :]).astype(bf16)
    for b in range(16):
        at = far_block(b)
        far[:, at * 128 : at * 128 + 128] = low[:, b * 128 : b * 128 + 128]


def run_middle(place, parts, tok, gains, tie):
    vmem = pl.BlockSpec(memory_space=pltpu.VMEM)
    return pl.pallas_call(
        middle_kernel,
        in_specs=[SCALARS] + [vmem] * 6 + [LOOSE],
        out_specs=[vmem] * 2,
        out_shape=[
            jax.ShapeDtypeStruct((32, 2048), f32),
            jax.ShapeDtypeStruct((32, 2048), bf16),
        ],
        cost_estimate=pl.CostEstimate(flops=10**6, bytes_accessed=2 * 10**6, transcendentals=0),
        name="middle",
    )(place, *parts, tok, gains, tie)


def middle_back_kernel(
    place, a0, a1, a2, a3, spread, middle, gains, weight, tie, d_mid, d_low, small
):
    row = pl.multiple_of(place[3] * 32, 32)
    total = a0[...].astype(f32)
    for part in (a1, a2, a3):
        total = total + part[...].astype(f32)
    near = lambda v: jnp.concatenate(
        [v[:, far_block(b) * 128 : far_block(b) * 128 + 128] for b in range(16)], axis=1
    )
    d_normed = near(total[:, :2048])
    d_gate = total[:, 2048:]
    mine = spread[pl.ds(row, 32), :]
    d_out = near(mine[:, :2048]).astype(f32)
    chosen = mine[:, 2048:].astype(f32)
    values = middle[...]
    gain = gains[1:2, :]
    factor = lax.rsqrt(jnp.mean(values * values, axis=1, keepdims=True) + epsilon)
    low = (values * factor * gain).astype(bf16)
    table = weight[:, 512:640]
    lane = lax.broadcasted_iota(jnp.int32, (32, 128), 1)
    is_expert = (lane >= 66) & (lane < 74)
    logits = jnp.where(is_expert, dot_nn(low, table), -1e30)
    power = jnp.exp(logits - jnp.max(logits, axis=1, keepdims=True))
    router = power / jnp.sum(power, axis=1, keepdims=True)
    d_chosen = d_gate * chosen
    d_logits = router * (d_chosen - jnp.sum(router * d_chosen, axis=1, keepdims=True))
    d_logits = d_logits.astype(bf16)
    d_normed = d_normed + dot_nt(d_logits, table)
    scaled = d_normed * gain
    d_norm = factor * scaled - values * (factor * factor * factor) * jnp.mean(
        values * scaled, axis=1, keepdims=True
    )
    d_values = d_out + d_norm
    d_mid[...] = d_values
    d_low[...] = d_values.astype(bf16)
    terms = (d_normed * values * factor).astype(bf16)
    small[...] = (
        dot_tn(low, d_logits) + dot_tn(terms, (lane == 65).astype(bf16))
    ).astype(bf16)


def middle_back(place, parts, spread, middle, gains, weight, tie):
    vmem = pl.BlockSpec(memory_space=pltpu.VMEM)
    return pl.pallas_call(
        middle_back_kernel,
        in_specs=[SCALARS] + [vmem] * 8 + [LOOSE],
        out_specs=[vmem] * 3,
        out_shape=[
            jax.ShapeDtypeStruct((32, 2048), f32),
            jax.ShapeDtypeStruct((32, 2048), bf16),
            jax.ShapeDtypeStruct((2048, 128), bf16),
        ],
        compiler_params=pltpu.CompilerParams(vmem_limit_bytes=32 * MIB),
        cost_estimate=pl.CostEstimate(
            flops=10**8, bytes_accessed=5 * 10**6, transcendentals=0
        ),
        name="middle_back",
    )(place, *parts, spread, middle, gains, weight, tie)


def latent_back_kernel(
    place, t0, t1, t2, t3, compressed, gains, cosine, sine, tie, d_comp, small
):
    row = pl.multiple_of(place[3] * 32, 32)
    terms = t0[...].astype(f32)
    for part in (t1, t2, t3):
        terms = terms + part[...].astype(f32)
    main = compressed[pl.ds(row, 32), :][:, :RANK]
    factor = lax.rsqrt(jnp.mean(main * main, axis=1, keepdims=True) + epsilon)
    grad_main = terms[:, :RANK]
    scaled = grad_main * gains[2:3, :RANK]
    d_main = factor * scaled - main * (factor * factor * factor) * jnp.mean(
        main * scaled, axis=1, keepdims=True
    )
    first, second = terms[:, RANK : RANK + 32], terms[:, RANK + 32 : RANK + 64]
    cos, sin = cosine[pl.ds(row, 32), :][:, :32], sine[pl.ds(row, 32), :][:, :32]
    rot = jnp.concatenate([first * cos + second * sin, second * cos - first * sin], axis=1)
    d_comp[:, :RANK] = d_main.astype(bf16)
    d_comp[:, RANK:] = jnp.concatenate([rot, jnp.zeros((32, 64), f32)], axis=1).astype(bf16)
    latent_terms = grad_main * main * factor
    gap = jnp.zeros((32, 48), f32)
    latent_terms = jnp.concatenate(
        [p for i in range(32) for p in (latent_terms[:, 16 * i : 16 * i + 16], gap)], axis=1
    )
    lane = lax.broadcasted_iota(jnp.int32, (32, 128), 1)
    small[...] = dot_tn(latent_terms.astype(bf16), (lane == 74).astype(bf16)).astype(bf16)


def latent_back(place, terms, compressed, gains, cosine, sine, tie):
    vmem = pl.BlockSpec(memory_space=pltpu.VMEM)
    return pl.pallas_call(
        latent_back_kernel,
        in_specs=[SCALARS] + [vmem] * 8 + [LOOSE],
        out_specs=[vmem] * 2,
        out_shape=[
            jax.ShapeDtypeStruct((32, 640), bf16),
            jax.ShapeDtypeStruct((2048, 128), bf16),
        ],
        compiler_params=pltpu.CompilerParams(vmem_limit_bytes=32 * MIB),
        cost_estimate=pl.CostEstimate(flops=10**7, bytes_accessed=10**6, transcendentals=0),
        name="latent_back",
    )(place, *terms, compressed, gains, cosine, sine, tie)


def token_back_kernel(place, d_comp, q0, q1, q2, q3, tok, gains, weight, d_mid, grad, small):
    row = pl.multiple_of(place[3] * 32, 32)
    d_normed = dot_nt(d_comp[...], weight[:, :640])
    for part in (q0, q1, q2, q3):
        d_normed = d_normed + part[...].astype(f32)
    values = tok[pl.ds(row, 32), :].astype(f32)
    factor = lax.rsqrt(jnp.mean(values * values, axis=1, keepdims=True) + epsilon)
    scaled = d_normed * gains[0:1, :]
    d_norm = factor * scaled - values * (factor * factor * factor) * jnp.mean(
        values * scaled, axis=1, keepdims=True
    )
    grad[...] = (d_mid[...] + d_norm).astype(bf16)
    lane = lax.broadcasted_iota(jnp.int32, (32, 128), 1)
    small[...] = dot_tn(
        (d_normed * values * factor).astype(bf16), (lane == 64).astype(bf16)
    ).astype(bf16)


def token_back(place, d_comp, d_queries, tok, gains, weight, d_mid):
    vmem = pl.BlockSpec(memory_space=pltpu.VMEM)
    return pl.pallas_call(
        token_back_kernel,
        in_specs=[SCALARS] + [vmem] * 9,
        out_specs=[vmem] * 2,
        out_shape=[
            jax.ShapeDtypeStruct((32, 2048), bf16),
            jax.ShapeDtypeStruct((2048, 128), bf16),
        ],
        compiler_params=pltpu.CompilerParams(vmem_limit_bytes=32 * MIB),
        cost_estimate=pl.CostEstimate(
            flops=10**8, bytes_accessed=4 * 10**6, transcendentals=0
        ),
        name="token_back",
    )(place, d_comp, *d_queries, tok, gains, weight, d_mid)


def compress_grad_kernel(place, c0, c1, c2, c3, normed, s0, s1, s2, *rest):
    mine, other, d_all = rest[-3:]
    for s, part in enumerate((c0, c1, c2, c3)):
        row = pl.multiple_of(lax.rem(place[3] - s + 4, 4) * 32, 32)
        d_all[pl.ds(row, 32), :] = part[...]
    column = pl.multiple_of(place[3] * 128, 128)
    own = d_all[:, pl.ds(column, 128)]
    rot = d_all[:, RANK:]
    main = dot_tn(normed[...], own).astype(bf16)
    rest = dot_tn(normed[...], rot)
    for part in (s0, s1, s2):
        rest = rest + part[...].astype(f32)
    rest = rest.astype(bf16)
    is_first = place[2] == 0
    for b in range(16):
        for columns, value in ((slice(0, 128), main), (slice(128, 256), rest)):
            low, high = value[b * 128 : b * 128 + 64], value[b * 128 + 64 : b * 128 + 128]
            mine[b * 64 : b * 64 + 64, columns] = jnp.where(is_first, low, high)
            other[b * 64 : b * 64 + 64, columns] = jnp.where(is_first, high, low)


def compress_grad(place, parts, normed, smalls, tie):
    vmem = pl.BlockSpec(memory_space=pltpu.VMEM)
    return pl.pallas_call(
        compress_grad_kernel,
        in_specs=[SCALARS] + [vmem] * 8 + [LOOSE] * len(tie),
        out_specs=[vmem] * 2,
        out_shape=[jax.ShapeDtypeStruct((1024, 256), bf16)] * 2,
        scratch_shapes=[pltpu.VMEM((128, 640), bf16)],
        compiler_params=pltpu.CompilerParams(vmem_limit_bytes=32 * MIB),
        cost_estimate=pl.CostEstimate(
            flops=2 * 10**8, bytes_accessed=3 * 10**6, transcendentals=0
        ),
        name="compress_grad",
    )(place, *parts, normed, *smalls, *tie)


def attend_back_kernel(
    place, d0, d1, d2, d3, out_w, q, kv, prob, lat, expand, nope_w, rot_w, cosine, sine, tie,
    d_q, d_rot, d_exp, d_branch, k0, k1, k2, k3, r0, r1, r2, r3,
    lat_sum, rot_sum, rot_q, total,
):
    head = pl.program_id(0)

    @pl.when(head == 0)
    def _():
        for s, part in enumerate((d0, d1, d2, d3)):
            row = pl.multiple_of(lax.rem(place[3] - s + 4, 4) * 32, 32)
            d_branch[pl.ds(row, 32), :] = part[...]
        lat_sum[...] = jnp.zeros_like(lat_sum)
        rot_sum[...] = jnp.zeros_like(rot_sum)
        total[...] = jnp.zeros_like(total)

    d_att = dot_nn(d_branch[...], out_w[...]).astype(bf16)
    prob_h = prob[0]
    d_prob = dot_nt(d_att, kv[:, 128:])
    row_sum = jnp.sum(prob_h * d_prob, axis=1, keepdims=True)
    d_score = (prob_h * (d_prob - row_sum)).astype(bf16)
    d_nope = (dot_nn(d_score, kv[:, :128]) * SCALE).astype(bf16)
    d_q[...] = d_nope
    rot_q[head] = dot_nn(d_score, lat[:, RANK:]) * SCALE
    d_key = dot_tn(d_score, q[...]) * SCALE
    d_val = dot_tn(prob_h.astype(bf16), d_att)
    d_exp_h = jnp.concatenate([d_key[:, :128], d_val], axis=1).astype(bf16)
    d_exp[...] = d_exp_h
    rot_sum[...] += d_key[:, 128:]
    lat_sum[...] += dot_nt(d_exp_h, expand[...].reshape(RANK, 256))
    total[...] += dot_nt(d_nope, nope_w[...])

    @pl.when(head == 3)
    def _():
        rot = jnp.concatenate([rot_q[h][:, :64] for h in range(4)], axis=1)
        lane = lax.broadcasted_iota(jnp.int32, rot.shape, 1)
        partner = jnp.where(
            lane % 64 < 32, pltpu.roll(rot, 224, 1), pltpu.roll(rot, 32, 1)
        )
        rot = (rot * cosine[...] + partner * sine[...]).astype(bf16)
        d_rot[...] = rot
        summed = total[...] + dot_nt(rot, rot_w[...])
        total[...] = summed
        for s, out in enumerate((r0, r1, r2, r3)):
            row = pl.multiple_of(lax.rem(place[3] + s, 4) * 32, 32)
            out[...] = total[pl.ds(row, 32), :].astype(bf16)
        for sx in range(4):
            rows = slice(sx * 512, sx * 512 + 512)
            out = (k0, k1, k2, k3)[sx]
            out[:, :RANK] = lat_sum[rows, :].astype(bf16)
            out[:, RANK:] = rot_sum[rows, :].astype(bf16)


def attend_back(place, parts, q, kv, prob, lat, attn_all, cosine, sine, tie):
    by_head = attn_all.reshape(32, 4, 16, 1536)
    return pl.pallas_call(
        attend_back_kernel,
        grid=(4,),
        in_specs=[SCALARS]
        + [whole(32, 2048)] * 4
        + [
            pl.BlockSpec((2048, 128), lambda h: (0, 6 + h)),
            pl.BlockSpec((128, 256), lambda h: (0, h)),
            pl.BlockSpec((2048, 256), lambda h: (0, h)),
            pl.BlockSpec((1, 128, 2048), lambda h: (h, 0, 0)),
            whole(2048, 640),
            pl.BlockSpec((32, 1, 16, 256), lambda h: (0, h, 0, 5)),
            pl.BlockSpec((2048, 128), lambda h: (0, h)),
            pl.BlockSpec((2048, 256), lambda h: (0, 2)),
            whole(128, 256),
            whole(128, 256),
            LOOSE,
        ],
        out_specs=[
            pl.BlockSpec((128, 128), lambda h: (0, h)),
            whole(128, 256),
            pl.BlockSpec((2048, 256), lambda h: (0, h)),
            whole(128, 2048),
        ]
        + [whole(512, 640)] * 4
        + [whole(32, 2048)] * 4,
        out_shape=[
            jax.ShapeDtypeStruct((128, 512), bf16),
            jax.ShapeDtypeStruct((128, 256), bf16),
            jax.ShapeDtypeStruct((2048, 1024), bf16),
            jax.ShapeDtypeStruct((128, 2048), bf16),
        ]
        + [jax.ShapeDtypeStruct((512, 640), bf16)] * 4
        + [jax.ShapeDtypeStruct((32, 2048), bf16)] * 4,
        scratch_shapes=[
            pltpu.VMEM((2048, 512), f32),
            pltpu.VMEM((2048, 128), f32),
            pltpu.VMEM((4, 128, 128), f32),
            pltpu.VMEM((128, 2048), f32),
        ],
        compiler_params=pltpu.CompilerParams(vmem_limit_bytes=56 * MIB),
        cost_estimate=pl.CostEstimate(
            flops=8 * 10**9, bytes_accessed=30 * 10**6, transcendentals=0
        ),
        name="attend_back",
    )(
        place, *parts, attn_all, q, kv, prob, lat, by_head, attn_all, attn_all, cosine, sine, tie
    )


def expert_kernel(place, far, spread, whole_w, d_far, d_hidden, hidden, out, weight, sem):
    @pl.when(pl.program_id(0) == 0)
    def _():
        copy = pltpu.make_async_copy(whole_w, weight, sem)
        copy.start()
        copy.wait()

    expert = 2 * place[0] + place[2]
    raw = dot_nn(far[...], weight[:, :896])
    d_weighted = dot_nn(spread[:, :2048], weight[:, 896:])
    rows = raw.shape[0]
    logits = raw[:, 880:888]
    power = jnp.exp(logits - jnp.max(logits, axis=1, keepdims=True))
    router = power / jnp.sum(power, axis=1, keepdims=True)
    is_mine = lax.broadcasted_iota(jnp.int32, (rows, 8), 1) == expert
    chosen = spread[:, 2048:2176][:, 66:74].astype(f32)
    gate = jnp.sum(jnp.where(is_mine, router * chosen, 0.0), axis=1, keepdims=True)
    routed = lax.broadcasted_iota(jnp.int32, (rows, 440), 1) < 352
    gate = jnp.where(routed, gate, 1.0)
    low, upper = raw[:, :440], raw[:, 440:880]
    sigma = 1.0 / (1.0 + jnp.exp(-low))
    silu = low * sigma
    slope = sigma + silu * (1.0 - sigma)
    act = silu * upper
    weighted = (gate * act).astype(bf16)
    d_gate = jnp.sum(jnp.where(routed, d_weighted * act, 0.0), axis=1, keepdims=True)
    d_act = d_weighted * gate
    d_up = jnp.concatenate(
        [d_act * upper * slope, d_act * silu, jnp.zeros((rows, 16), f32)], axis=1
    ).astype(bf16)
    d_hidden[...] = d_up
    hidden[...] = jnp.concatenate([weighted, jnp.zeros((rows, 72), bf16)], axis=1)
    d_far[:, :2048] = dot_nt(d_up, weight[:, :896]).astype(bf16)
    lane = lax.broadcasted_iota(jnp.int32, (rows, 128), 1)
    d_far[:, 2048:] = jnp.where(lane == expert + 66, d_gate, 0.0).astype(bf16)
    out[...] = dot_nt(weighted, weight[:, 896:]).astype(bf16)


def run_expert(place, far, spread, weight):
    rows = 256
    by_rows = lambda columns: pl.BlockSpec((rows, columns), lambda i: (i, 0))
    return pl.pallas_call(
        expert_kernel,
        grid=(512 // rows,),
        in_specs=[SCALARS, by_rows(2048), by_rows(2176), LOOSE],
        out_specs=[by_rows(2176), by_rows(896), by_rows(512), by_rows(2048)],
        out_shape=[
            jax.ShapeDtypeStruct((512, 2176), bf16),
            jax.ShapeDtypeStruct((512, 896), bf16),
            jax.ShapeDtypeStruct((512, 512), bf16),
            jax.ShapeDtypeStruct((512, 2048), bf16),
        ],
        scratch_shapes=[pltpu.VMEM((2048, 1336), bf16), pltpu.SemaphoreType.DMA],
        compiler_params=pltpu.CompilerParams(vmem_limit_bytes=48 * MIB),
        cost_estimate=pl.CostEstimate(
            flops=6 * 10**9, bytes_accessed=18 * 10**6, transcendentals=2**18
        ),
        name="expert",
    )(place, far, spread, weight)


def expert_grad_kernel(x0, x1, y0, y1, d0, d1, h0, h1, t1, t2, t3, out):
    out[:, :896] = (dot_tn(x0[...], d0[...]) + dot_tn(x1[...], d1[...])).astype(bf16)
    down = dot_tn(y0[...], h0[...]) + dot_tn(y1[...], h1[...])
    out[:, 896:] = down[:, :440].astype(bf16)


def expert_grad(fars, spreads, d_hiddens, hiddens, tie):
    block = 512
    columns = pl.BlockSpec((512, block), lambda i: (0, i))
    return pl.pallas_call(
        expert_grad_kernel,
        grid=(2048 // block,),
        in_specs=[columns] * 4 + [whole(512, 896)] * 2 + [whole(512, 512)] * 2 + [LOOSE] * 3,
        out_specs=pl.BlockSpec((block, 1336), lambda i: (i, 0)),
        out_shape=jax.ShapeDtypeStruct((2048, 1336), bf16),
        compiler_params=pltpu.CompilerParams(vmem_limit_bytes=48 * MIB),
        cost_estimate=pl.CostEstimate(
            flops=6 * 10**9, bytes_accessed=18 * 10**6, transcendentals=0
        ),
        name="expert_grad",
    )(*fars, *spreads, *d_hiddens, *hiddens, *tie)


def attn_grad_kernel(normed, d_q, d_rot, d_branch, attended, lat, d_exp, *rest):
    out, g_exp = rest[-2:]
    step = pl.program_id(0)

    @pl.when(step == 0)
    def _():
        g_exp[...] = dot_tn(lat[:, :RANK], d_exp[...]).astype(bf16)

    out[:, :512] = dot_tn(normed[...], d_q[...]).astype(bf16)
    out[:, 512:768] = dot_tn(normed[...], d_rot[...]).astype(bf16)
    out[:, 768:1280] = dot_tn(d_branch[...], attended[...]).astype(bf16)
    for d in range(8):
        for h in range(4):
            row = pl.multiple_of((step * 8 + d) * 16, 16)
            to = d * 64 + h * 16
            out[to : to + 16, 1280:] = g_exp[pl.ds(row, 16), h * 256 : h * 256 + 256]


def attn_grad(normed, d_q, d_rot, d_branch, attended, lat, d_exp, tie):
    columns = pl.BlockSpec((128, 512), lambda i: (0, i))
    return pl.pallas_call(
        attn_grad_kernel,
        grid=(4,),
        in_specs=[
            columns,
            whole(128, 512),
            whole(128, 256),
            columns,
            whole(128, 512),
            whole(2048, 640),
            whole(2048, 1024),
        ]
        + [LOOSE] * len(tie),
        out_specs=pl.BlockSpec((512, 1536), lambda i: (i, 0)),
        out_shape=jax.ShapeDtypeStruct((2048, 1536), bf16),
        scratch_shapes=[pltpu.VMEM((512, 1024), bf16)],
        compiler_params=pltpu.CompilerParams(vmem_limit_bytes=48 * MIB),
        cost_estimate=pl.CostEstimate(
            flops=4 * 10**9, bytes_accessed=15 * 10**6, transcendentals=0
        ),
        name="attn_grad",
    )(normed, d_q, d_rot, d_branch, attended, lat, d_exp, *tie)


def pair_kernel(place, mine, other, tie, p0, p1, p2, p3):
    is_first = place[2] == 0
    for s, out in enumerate((p0, p1, p2, p3)):
        to = lax.rem(place[0] + s, 4)
        a, b = mine[to], other[to]
        out[:64, :] = jnp.where(is_first, a, b)
        out[64:, :] = jnp.where(is_first, b, a)


def pair(place, mine, other, tie):
    vmem = pl.BlockSpec(memory_space=pltpu.VMEM)
    return pl.pallas_call(
        pair_kernel,
        in_specs=[SCALARS, vmem, vmem, LOOSE],
        out_specs=[vmem] * 4,
        out_shape=[jax.ShapeDtypeStruct((128, 1336), bf16)] * 4,
        cost_estimate=pl.CostEstimate(flops=10**6, bytes_accessed=3 * 10**6, transcendentals=0),
        name="pair",
    )(place, mine, other, tie)


def turn_kernel(place, value, tie, out):
    for s in range(4):
        row = pl.multiple_of(lax.rem(place[3] - s + 4, 4) * 32, 32)
        out[s * 32 : s * 32 + 32, :] = value[pl.ds(row, 32), :]


def turn(place, value, tie):
    vmem = pl.BlockSpec(memory_space=pltpu.VMEM)
    return pl.pallas_call(
        turn_kernel,
        in_specs=[SCALARS, vmem, LOOSE],
        out_specs=vmem,
        out_shape=jax.ShapeDtypeStruct(value.shape, bf16),
        cost_estimate=pl.CostEstimate(flops=10**6, bytes_accessed=10**6, transcendentals=0),
        name="turn",
    )(place, value, tie)


def out_parts_kernel(mine, other, middle, t1, t2, t3, p0, p1, p2, p3):
    for s, out in enumerate((p0, p1, p2, p3)):
        rows = slice(s * 128, s * 128 + 128)
        total = mine[rows, :].astype(f32) + other[rows, :].astype(f32)
        out[...] = total.astype(bf16)
        if s == 0:
            for b in range(16):
                at = far_block(b) * 128
                out[:32, at : at + 128] = (
                    total[:32, at : at + 128] + middle[:, b * 128 : b * 128 + 128]
                ).astype(bf16)


def out_parts(mine, other, middle, tie):
    vmem = pl.BlockSpec(memory_space=pltpu.VMEM)
    return pl.pallas_call(
        out_parts_kernel,
        in_specs=[vmem] * 3 + [LOOSE] * 3,
        out_specs=[vmem] * 4,
        out_shape=[jax.ShapeDtypeStruct((128, 2048), bf16)] * 4,
        compiler_params=pltpu.CompilerParams(vmem_limit_bytes=32 * MIB),
        cost_estimate=pl.CostEstimate(flops=10**6, bytes_accessed=6 * 10**6, transcendentals=0),
        name="out_parts",
    )(mine, other, middle, *tie)


def out_rows_kernel(place, p0, p1, p2, p3, out):
    for s in range(4):
        rows = slice(s * 32, s * 32 + 32)
        row = pl.multiple_of(lax.rem(place[3] - s + 4, 4) * 32, 32)
        total = p0[rows, :].astype(f32)
        for part in (p1, p2, p3):
            total = total + part[rows, :].astype(f32)
        for b in range(16):
            at = far_block(b) * 128
            out[pl.ds(row, 32), b * 128 : b * 128 + 128] = total[:, at : at + 128].astype(bf16)


def out_rows(place, parts):
    vmem = pl.BlockSpec(memory_space=pltpu.VMEM)
    return pl.pallas_call(
        out_rows_kernel,
        in_specs=[SCALARS] + [vmem] * 4,
        out_specs=vmem,
        out_shape=jax.ShapeDtypeStruct((128, 2048), bf16),
        cost_estimate=pl.CostEstimate(flops=10**6, bytes_accessed=3 * 10**6, transcendentals=0),
        name="out_rows",
    )(place, *parts)


def cut_kernel(place, value, tie, p0, p1, p2, p3):
    for s, out in enumerate((p0, p1, p2, p3)):
        row = pl.multiple_of(lax.rem(place[0] + s, 4) * 128, 128)
        out[...] = value[pl.ds(row, 128), :]


def cut(place, value, tie):
    vmem = pl.BlockSpec(memory_space=pltpu.VMEM)
    return pl.pallas_call(
        cut_kernel,
        in_specs=[SCALARS, vmem, LOOSE],
        out_specs=[vmem] * 4,
        out_shape=[jax.ShapeDtypeStruct((128, 1336), bf16)] * 4,
        cost_estimate=pl.CostEstimate(flops=10**6, bytes_accessed=3 * 10**6, transcendentals=0),
        name="cut",
    )(place, value, tie)


def by_core_kernel(place, p0, p1, p2, p3, mine, other):
    is_first = place[2] == 0
    for s, part in enumerate((p0, p1, p2, p3)):
        at = lax.rem(place[0] - s + 4, 4)
        low, high = part[:64, :], part[64:, :]
        mine[at] = jnp.where(is_first, low, high)
        other[at] = jnp.where(is_first, high, low)


def by_core(place, parts):
    vmem = pl.BlockSpec(memory_space=pltpu.VMEM)
    return pl.pallas_call(
        by_core_kernel,
        in_specs=[SCALARS] + [vmem] * 4,
        out_specs=[vmem] * 2,
        out_shape=[jax.ShapeDtypeStruct((4, 64, 1336), bf16)] * 2,
        cost_estimate=pl.CostEstimate(flops=10**6, bytes_accessed=3 * 10**6, transcendentals=0),
        name="by_core",
    )(place, *parts)


def unpack_kernel(place, mine, other, expert_in, expert_out, shared_in, shared_out):
    is_first = place[2] == 0
    ins, outs, downs = [], [], []
    for x in range(4):
        for core in range(2):
            a, b = (mine[x], other[x]) if core == 0 else (other[x], mine[x])
            value = jnp.where(is_first, a, b).astype(f32)
            expert = 2 * x + core
            expert_in[:, expert, 0, :] = value[:, :352]
            expert_in[:, expert, 1, :] = value[:, 440:792]
            expert_out[:, expert, :] = value[:, 896:1248]
            ins.append(value[:, 352:440])
            outs.append(value[:, 792:880])
            downs.append(value[:, 1248:])
    shared_in[:, 0, :] = jnp.concatenate(ins, axis=1)
    shared_in[:, 1, :] = jnp.concatenate(outs, axis=1)
    shared_out[...] = jnp.concatenate(downs, axis=1)


def unpack(place, mine, other):
    vmem = pl.BlockSpec(memory_space=pltpu.VMEM)
    return pl.pallas_call(
        unpack_kernel,
        in_specs=[SCALARS, vmem, vmem],
        out_specs=[vmem] * 4,
        out_shape=[
            jax.ShapeDtypeStruct((64, 8, 2, 352), f32),
            jax.ShapeDtypeStruct((64, 8, 352), f32),
            jax.ShapeDtypeStruct((64, 2, 704), f32),
            jax.ShapeDtypeStruct((64, 704), f32),
        ],
        compiler_params=pltpu.CompilerParams(vmem_limit_bytes=32 * MIB),
        cost_estimate=pl.CostEstimate(flops=10**6, bytes_accessed=6 * 10**6, transcendentals=0),
        name="unpack",
    )(place, mine, other)


def finish_kernel(total, *rest):
    query, output, expand = rest[-3:]
    value = total[...].astype(f32)
    query[...] = jnp.concatenate(
        [
            p
            for h in range(4)
            for p in (
                value[:, h * 128 : h * 128 + 128],
                value[:, 512 + h * 64 : 576 + h * 64],
            )
        ],
        axis=1,
    )
    output[...] = value[:, 768:1280]
    for h in range(4):
        expand[:, h * 256 : h * 256 + 256] = value[h * 16 : h * 16 + 16, 1280:]


def finish(total, tie):
    vmem = pl.BlockSpec(memory_space=pltpu.VMEM)
    return pl.pallas_call(
        finish_kernel,
        in_specs=[vmem] + [LOOSE] * len(tie),
        out_specs=[vmem] * 3,
        out_shape=[
            jax.ShapeDtypeStruct((64, 768), f32),
            jax.ShapeDtypeStruct((64, 512), f32),
            jax.ShapeDtypeStruct((16, 1024), f32),
        ],
        cost_estimate=pl.CostEstimate(flops=10**6, bytes_accessed=10**6, transcendentals=0),
        name="finish",
    )(total, *tie)


def on_device(
    tokens,
    segment,
    routes,
    cotangent,
    gain_attn,
    w_query,
    w_compress,
    gain_latent,
    w_expand,
    w_output,
    gain_ffn,
    w_router,
    w_expert_in,
    w_expert_out,
    w_shared_in,
    w_shared_out,
):
    xi, zi, ci, yi = (lax.axis_index(a) for a in ("x", "z", "c", "y"))
    place = jnp.stack([xi, zi, ci, yi]).astype(jnp.int32)
    is_first = ci == 0
    heads = 4
    dim = 2048

    def enter(value):
        mine, other = pick(value, ci, 0), shift(pick(value, 1 - ci, 0), "c", 1)
        return jnp.concatenate(
            [jnp.where(is_first, mine, other), jnp.where(is_first, other, mine)], axis=0
        )

    def leave(value):
        halves = value.reshape((2, 64) + value.shape[1:])
        mine, other = pick(halves, ci, 0), shift(pick(halves, 1 - ci, 0), "c", 1)
        return jnp.stack([jnp.where(is_first, mine, other), jnp.where(is_first, other, mine)])

    small = jnp.concatenate(
        [
            w_compress,
            gain_attn[:, None],
            gain_ffn[:, None],
            w_router,
            jnp.pad(gain_latent, (0, 48))[:, None],
            jnp.zeros((64, 53), bf16),
        ],
        axis=1,
    )
    small_mine = jnp.concatenate(gather_near(jnp.concatenate(gather_near(small, "x")), "z"))
    small_other = shift(small_mine, "c", 1)

    by_head = w_query.reshape(64, heads, NOPE + ROPE)
    attn_all = lax.all_gather(
        jnp.concatenate(
            [
                by_head[:, :, :NOPE].reshape(64, 512),
                by_head[:, :, NOPE:].reshape(64, 256),
                w_output,
                w_expand.reshape(16, heads, 256).transpose(1, 0, 2).reshape(64, 256),
            ],
            axis=1,
        ),
        ("x", "z", "c"),
        axis=0,
        tiled=True,
    )

    packed_w = jnp.concatenate(
        [
            w_expert_in[:, :, 0],
            w_shared_in[:, 0].reshape(64, 8, 88),
            w_expert_in[:, :, 1],
            w_shared_in[:, 1].reshape(64, 8, 88),
            jnp.broadcast_to(w_router[:, None, :], (64, 8, 8)),
            jnp.zeros((64, 8, 8), bf16),
            w_expert_out,
            w_shared_out.reshape(64, 8, 88),
        ],
        axis=-1,
    )
    packed_w = packed_w.transpose(1, 0, 2).reshape(4, 2, 64, 1336)
    mine_w, other_w = pick(packed_w, ci, 1), shift(pick(packed_w, 1 - ci, 1), "c", 1)
    mine_w, other_w = mine_w.reshape(4, 64, 1336), other_w.reshape(4, 64, 1336)
    tok = enter(tokens)
    chosen = jnp.sum(
        (routes[..., None] == jnp.arange(EXPERTS, dtype=jnp.int32)).astype(f32), axis=2
    )
    spread = jnp.concatenate(
        [
            to_far(cotangent.reshape(128, dim)),
            jnp.zeros((128, 66), bf16),
            chosen.reshape(128, 8).astype(bf16),
            jnp.zeros((128, 54), bf16),
        ],
        axis=1,
    )
    spread_here = enter(spread.reshape(2, 64, 2176))

    position = (xi * 4 + zi) * 128 + jnp.arange(128, dtype=jnp.int32)
    segment_row = pick(segment, ci, 0)
    blocks = jnp.stack(
        [lax.rem(xi - sx + 4, 4) * 4 + lax.rem(zi - sz + 4, 4) for sx in range(4) for sz in range(4)]
    )
    segment_near = segment_row.reshape(16, 128)[blocks].reshape(2048)
    key_place = (blocks[:, None] * 128 + jnp.arange(128, dtype=jnp.int32)[None, :]).reshape(2048)
    where_k = jnp.stack([key_place, segment_near])
    where_q = jnp.stack(
        [position, lax.dynamic_slice_in_dim(segment_row, (xi * 4 + zi) * 128, 128)], axis=1
    )
    lane = jnp.arange(256)[None, :]
    freq = jnp.exp((lane % 32).astype(f32) * (-jnp.log(10000.0) / 32))
    angle = position.astype(f32)[:, None] * freq
    cosine = jnp.cos(angle)
    sine = jnp.where(lane % 64 < 32, 1.0, -1.0) * jnp.sin(angle)

    normed, packed, compressed, weight, gains = front(
        place, tok, small_mine, small_other, cosine, sine
    )
    pair_w = pair(place, mine_w, other_w, small)
    pair_w = [pair_w[0]] + [shift(pair_w[s], "x", s) for s in range(1, 4)]
    expert_w = jnp.zeros((4, 128, 1336), bf16)
    for s in range(4):
        expert_w = lax.dynamic_update_index_in_dim(
            expert_w, pair_w[s], lax.rem(xi - s + 4, 4), 0
        )
    ffn_all = lax.all_gather(expert_w.reshape(512, 1336), "z", axis=0, tiled=True)
    latents = gather_near(jnp.concatenate(gather_near(packed, "z"), axis=0), "x")
    spread = turn(place, spread_here, latents[1])
    spread = jnp.concatenate(gather_near(spread, "x"), axis=0)
    spread_other = shift(spread, "c", 1)
    prob, kv, attended, latent_all, query, *branch = attend(
        place, normed, latents, attn_all, cosine, sine, where_q, where_k
    )
    branch = [branch[0]] + [shift(branch[s], "y", s) for s in range(1, 4)]
    middle, far = run_middle(place, branch, tok, gains, spread)

    far = jnp.concatenate(gather_near(jnp.concatenate(gather_near(far, "y")), "x"))
    far_other = shift(far, "c", 1)
    d_far, d_hidden, hidden, out_far = run_expert(place, far, spread, ffn_all)
    d_far2, d_hidden2, hidden2, out_far2 = run_expert(place, far_other, spread_other, ffn_all)

    d_far = (d_far.astype(f32) + shift(d_far2, "c", 1).astype(f32)).astype(bf16)
    d_far = [d_far[s * 128 : s * 128 + 128] for s in range(4)]
    d_far = [d_far[0]] + [shift(d_far[s], "x", -s) for s in range(1, 4)]
    tie = d_far[1:]
    d_far = sum(p.astype(f32) for p in d_far).astype(bf16)
    d_far = [d_far[s * 32 : s * 32 + 32] for s in range(4)]
    d_far = [d_far[0]] + [shift(d_far[s], "y", -s) for s in range(1, 4)]
    out_far = out_parts(out_far, shift(out_far2, "c", 1), middle, tie)
    d_mid, d_low, small_a = middle_back(
        place, d_far, spread_here, middle, gains, weight, out_far[0]
    )
    out_far = [out_far[0]] + [shift(out_far[s], "x", -s) for s in range(1, 4)]
    mixed = out_rows(place, out_far)
    mixed = [mixed] + [shift(mixed, "y", s) for s in range(1, 4)]
    d_low = gather_near(d_low, "y")

    grad_ffn = expert_grad(
        (far, far_other), (spread, spread_other), (d_hidden, d_hidden2), (hidden, hidden2), tie
    )
    grad_ffn = lax.psum_scatter(grad_ffn, "z", scatter_dimension=0, tiled=True)
    d_q, d_rot, d_expanded, d_branch, *rest = attend_back(
        place, d_low, query, kv, prob, latent_all, attn_all, cosine, sine, mixed[0]
    )
    terms = [rest[0]] + [shift(rest[s], "x", -s) for s in range(1, 4)]
    tie = terms[1:] + mixed[1:]
    terms = sum(p.astype(f32) for p in terms).astype(bf16)
    terms = [terms[s * 128 : s * 128 + 128] for s in range(4)]
    terms = [terms[0]] + [shift(terms[s], "z", -s) for s in range(1, 4)]
    late = terms[1]
    terms = sum(p.astype(f32) for p in terms).astype(bf16).reshape(4, 32, 640)
    terms = [pick(terms, lax.rem(yi + s, 4), 0) for s in range(4)]
    terms = [terms[0]] + [shift(terms[s], "y", s) for s in range(1, 4)]
    d_queries = [rest[4]] + [shift(rest[4 + s], "y", s) for s in range(1, 4)]
    grad_ffn = cut(place, grad_ffn, late)
    grad_ffn = [grad_ffn[0]] + [shift(grad_ffn[s], "x", s) for s in range(1, 4)]
    mine_g, other_g = by_core(place, grad_ffn)
    other_g = shift(other_g, "c", 1)
    d_comp, small_b = latent_back(place, terms, compressed, gains, cosine, sine, mine_g)
    g_expert_in, g_expert_out, g_shared_in, g_shared_out = unpack(place, mine_g, other_g)

    grad_rows, small_c = token_back(place, d_comp, d_queries, tok, gains, weight, d_mid)
    grad_rows = leave(gather_at(grad_rows, "y").reshape(128, dim))
    mixed = [m.astype(f32) for m in mixed]
    mixed = leave(((mixed[0] + mixed[2]) + (mixed[1] + mixed[3])).astype(bf16))

    def fsdp_sum(mine, other, cuts):
        value = (mine.astype(f32) + shift(other, "c", 1).astype(f32)).astype(bf16)
        value = value.reshape(4, 4, 64, -1)
        done = []
        for start, stop, first, second in cuts:
            part = sum_at(value[..., start:stop], first, 0 if first == "x" else 1).astype(bf16)
            done.append(sum_at(part, second, 0))
        return done

    g_attn = attn_grad(normed, d_q, d_rot, d_branch, attended, latent_all, d_expanded, tie)
    g_attn = lax.psum_scatter(g_attn, ("x", "z", "c"), scatter_dimension=0, tiled=True)
    g_mine, g_other = compress_grad(
        place,
        gather_near(d_comp, "y"),
        normed,
        (small_a, small_b, small_c),
        (g_expert_in, g_expert_out, g_shared_in, g_shared_out),
    )
    (g_small,) = fsdp_sum(g_mine, g_other, ((0, 256, "x", "z"),))
    g_small = g_small.astype(bf16)
    g_parts = gather_near(g_small, "y")
    g_query, g_output, g_expand = finish(g_attn, g_parts[1:])
    g_small = jnp.zeros((4, 64, 256), bf16)
    for s in range(4):
        g_small = lax.dynamic_update_index_in_dim(g_small, g_parts[s], lax.rem(yi - s + 4, 4), 0)
    g_small = g_small.astype(f32)
    g_compress = jnp.concatenate(
        [g_small[i, :, :128] for i in range(4)] + [g_small[0, :, 128:192]], axis=1
    )
    g_small = jnp.sum(g_small[:, :, 192:], axis=0)

    return (
        mixed,
        grad_rows,
        g_small[:, 0],
        g_query,
        g_compress,
        g_small[:16, 10],
        g_expand,
        g_output,
        g_small[:, 1],
        g_small[:, 2:10],
        g_expert_in,
        g_expert_out,
        g_shared_in,
        g_shared_out,
    )


def solution(mesh):
    fine = Mesh(mesh.devices.reshape(4, 4, 2, 4), ("x", "z", "c", "y"))
    rows = ("x", "z", "c")
    return jax.shard_map(
        on_device,
        mesh=fine,
        in_specs=(
            P(None, rows, None),
            P(),
            P(None, rows, None),
            P(None, rows, None),
            P(rows),
            P(rows, "y"),
            P(rows, None),
            P(rows),
            P(rows, "y"),
            P(rows, "y"),
            P(rows),
            P(rows, None),
            P(rows, None, None, "y"),
            P(rows, None, "y"),
            P(rows, None, "y"),
            P(rows, "y"),
        ),
        out_specs=(
            P(None, rows, None),
            P(None, rows, None),
            P(rows),
            P(rows, "y"),
            P(rows, None),
            P(rows),
            P(rows, "y"),
            P(rows, "y"),
            P(rows),
            P(rows, None),
            P(rows, None, None, "y"),
            P(rows, None, "y"),
            P(rows, None, "y"),
            P(rows, "y"),
        ),
        check_vma=False,
    )
```

time: 683 us -> 524 us (0.77)
  local copies, waits for them, and re-layouts: 125 us -> 70.5 us
  starting transfers between devices: 172 us -> 119 us
  waiting for transfers between devices: 223 us -> 183 us
  Pallas kernels: 70 us -> 103 us
  other arithmetic: 51.7 us -> 22 us
  matrix products: 14.7 us -> 0 us
    ppermute x121 -> x84, starting transfers between devices: 172 us -> 119 us  [shift(): lax.ppermute(value, axis, [(i, (i + step) % count) for i in range(count)])]
    pallas_call x2 -> x15, Pallas kernels: 18.3 us -> 51.9 us  [the longest x1 16.3 us: attend(): pl.pallas_call(attend_kernel, grid=(4,), in_specs=[SCALARS, whole(128, 20...]
    all_gather x1, waiting for transfers between devices: 28.2 us -> 0.01 us  [on_device(): lax.all_gather(jnp.concatenate([by_head[:, :, :NOPE].reshape(64, 512), by...]
    unnamed x186 -> x204, local copies, waits for them, and re-layouts: 24.7 us -> 45.3 us
    all_gather x1, waiting for transfers between devices: 19.3 us -> 0.01 us  [on_device(): lax.all_gather(expert_w.reshape(512, 1336), 'z', axis=0, tiled=True)]
    slice x20 -> x3, local copies, waits for them, and re-layouts: 16.1 us -> 0.21 us  [the longest x1 0.12 us: on_device(): d_far = [d_far[s * 128:s * 128 + 128] for s in range(4)]]
    convert_element_type x23 -> x8, other arithmetic: 19 us -> 3.83 us  [the longest x1 1.84 us: on_device(): mixed = leave((mixed[0] + mixed[2] + (mixed[1] + mixed[3])).astype(bf16))]
    dot_general x8 -> x0, matrix products: 14.7 us -> none  [the longest x3 7.57 us: dot_nn(): return jnp.dot(a, b, preferred_element_type=f32)]
  transfers between devices with their start and end apart: 124 -> 88, of which waited for: 43 -> 40; matrix products, arithmetic and copies ran while one was open for 23% -> 10% of each run, Pallas kernels for 9% -> 15%
where the time goes in v2:
time: 524 us; the launch traced here: 514 us
  waiting for transfers between devices  183 us (35%)
  starting transfers between devices  119 us (23%)
  Pallas kernels  103 us (20%)
  local copies, waits for them, and re-layouts  70.5 us (13%)
  other arithmetic  22 us (4%)
  between operations  15.6 us (3%)
    ppermute x84, waiting for transfers between devices, shift(): lax.ppermute(value, axis, [(i, (i + step) % count) for i in range(count)])  183 us
    ppermute x84, starting transfers between devices, shift(): lax.ppermute(value, axis, [(i, (i + step) % count) for i in range(count)])  119 us
    unnamed x204, local copies, waits for them, and re-layouts  45.3 us
    pallas_call x2, Pallas kernels, run_expert(): pl.pallas_call(expert_kernel, grid=(512 // rows,), in_specs=[SCALARS, by_...  25.5 us
    pallas_call x1, Pallas kernels, attend(): pl.pallas_call(attend_kernel, grid=(4,), in_specs=[SCALARS, whole(128, 20...  16.3 us
    pallas_call x1, Pallas kernels, attend_back(): pl.pallas_call(attend_back_kernel, grid=(4,), in_specs=[SCALARS] + [whole...  15.9 us
  transfers between devices with their start and end apart: 88, of which 40 were waited for; matrix products, arithmetic and copies ran while one was open for 10% of the time, Pallas kernels for 15%

profile of v2, /device:TPU:0, one launch (start us, length us, event | category | flops | bytes accessed | tf_op | source)
XLA Modules:
  0.0 513.7 jit_solution(2999206726162367601)
XLA Ops:
  16.7 2.7 collective-permute-start.2
  26.0 3.0 constant_dynamic-slice_fusion
  38.9 3.6 collective-permute-start.5
  44.9 2.3 pair.1
  47.2 4.4 collective-permute-done.4
  52.7 15.5 %collective-permute-done.5 = bf16[256,640]{1,0:T(8,128)(2,1)} collective-permute-done((bf16[256,640]{1,0:T(8,128)(2,1)}, bf16[256,640]{1,0:T(8,128)(2,1)}, u32[]{:S(2)}, u32[]{:S(2)}) %collective-permute-start.5) | collective-permute-done | bytes 327712 | tf_op jit(solution)/shard_map/ppermute | solution.py:54
  70.5 2.4 collective-permute-start.30
  73.6 9.1 %collective-permute-done.29 = bf16[128,1336]{1,0:T(8,128)(2,1)S(1)} collective-permute-done((bf16[128,1336]{1,0:T(8,128)(2,1)S(1)}, bf16[128,1336]{1,0:T(8,128)(2,1)S(1)}, u32[]{:S(2)}, u32[]{:S(2)}) %collective-permute-start.29) | collective-permute-done | bytes 342048 | tf_op jit(solution)/shard_map/ppermute | solution.py:54
  83.5 3.4 collective-permute-done.30
  93.8 2.4 collective-permute-start.9
  96.9 2.6 collective-permute-start.10
  99.5 4.9 collective-permute-done.8
  108.0 5.4 %collective-permute-start.11 = (bf16[512,640]{1,0:T(8,128)(2,1)}, bf16[512,640]{1,0:T(8,128)(2,1)}, u32[]{:S(2)}, u32[]{:S(2)}) collective-permute-start(bf16[512,640]{1,0:T(8,128)(2,1)} %constant_dynamic-update-slice_fusion.7.l0), channel_id=1, source_target_pairs={{0,32},{32,64},{64,96},{96,0},{1,33},{33,65},{65,97},{97,1},{2,34}... | collective-permute-start | bytes 1966088 | tf_op jit(solution)/shard_map/ppermute | solution.py:54
  113.5 2.7 collective-permute-start.13
  118.1 10.9 %collective-permute-done.11.l1.tie = bf16[512,640]{1,0:T(8,128)(2,1)} collective-permute-done((bf16[512,640]{1,0:T(8,128)(2,1)}, bf16[512,640]{1,0:T(8,128)(2,1)}, u32[]{:S(2)}, u32[]{:S(2)}) %collective-permute-start.11) | collective-permute-done | bytes 655392 | tf_op jit(solution)/shard_map/ppermute | solution.py:54
  130.9 2.5 collective-permute-start.18
  133.4 2.7 collective-permute-start.20
  136.2 6.8 %collective-permute-done.12.l2 = bf16[512,640]{1,0:T(8,128)(2,1)} collective-permute-done((bf16[512,640]{1,0:T(8,128)(2,1)}, bf16[512,640]{1,0:T(8,128)(2,1)}, u32[]{:S(2)}, u32[]{:S(2)}) %collective-permute-start.12) | collective-permute-done | bytes 655392 | tf_op jit(solution)/shard_map/ppermute | solution.py:54
  143.6 16.3 %attend.1 = (f32[4,128,2048]{2,1,0:T(8,128)}, bf16[2048,1024]{1,0:T(8,128)(2,1)}, bf16[128,512]{1,0:T(8,128)(2,1)S(1)}, bf16[2048,640]{1,0:T(8,128)(2,1)}, bf16[...) custom-call(s32[4]{0:T(128)S(1)} %copy-done.50, ...), custom_call_target="tpu_custom_call" | custom-call | flops 5000000000 | bytes 26000000 | tf_op jit(solution)/shard_map/attend/pallas_call | solution.py:235
  161.9 3.5 collective-permute-start.15
  166.4 3.0 pad_maximum_fusion.tie.spread.y0
  171.0 2.2 middle.1
  174.1 3.2 collective-permute-start.22
  183.2 9.1 %collective-permute-start.24 = (bf16[128,2048]{1,0:T(8,128)(2,1)S(1)}, bf16[128,2048]{1,0:T(8,128)(2,1)S(1)}, u32[]{:S(2)}, u32[]{:S(2)}) collective-permute-start(bf16[128,2048]{1,0:T(8,128)(2,1)S(1)} %get-tuple-element.234), channel_id=1, source_target_pairs={{0,32},{32,64},{64,96},{96,0},{1,33},{33,65},{65,97},{97,1},{2,34}... | collective-permute-start | bytes 1572872 | tf_op jit(solution)/shard_map/ppermute | solution.py:54
  192.2 2.7 collective-permute-start.26
  194.9 4.9 collective-permute-done.24
  200.6 9.9 %collective-permute-done.25 = bf16[128,2048]{1,0:T(8,128)(2,1)S(1)} collective-permute-done((bf16[128,2048]{1,0:T(8,128)(2,1)S(1)}, bf16[128,2048]{1,0:T(8,128)(2,1)S(1)}, u32[]{:S(2)}, u32[]{:S(2)}) %collective-permute-start.25) | collective-permute-done | bytes 524320 | tf_op jit(solution)/shard_map/ppermute | solution.py:54
  212.2 4.5 collective-permute-done.31.far.x1
  216.7 12.7 %expert.3 = (bf16[512,2176]{1,0:T(8,128)(2,1)}, bf16[512,896]{1,0:T(8,128)(2,1)S(1)}, bf16[512,512]{1,0:T(8,128)(2,1)S(1)}, bf16[512,2048]{1,0:T(8,128)(2,1)S(1)}) custom-call(s32[4]{0:T(128)S(1)} %copy-done.51, bf16[512,2048]{1,0:T(8,128)(2,1)} %collective-permute-done.31.far.x1, bf16[512,2176]{1,0:T(8,128)(2,1)} %collective-permute-done.32.spread.y1, ...), custom_call_target="tpu_custom_call" | custom-call | flops 6000000000 | bytes 18000000 | tf_op jit(solution)/shard_map/expert/pallas_call | solution.py:640
  230.9 12.7 %expert.2 = (bf16[512,2176]{1,0:T(8,128)(2,1)}, bf16[512,896]{1,0:T(8,128)(2,1)S(1)}, bf16[512,512]{1,0:T(8,128)(2,1)S(1)}, bf16[512,2048]{1,0:T(8,128)(2,1)S(1)}) custom-call(s32[4]{0:T(128)S(1)} %copy-done.51, bf16[512,2048]{1,0:T(8,128)(2,1)} %constant_dynamic-update-slice_fusion.15.far.x0, bf16[512,2176]{1,0:T(8,128)(2,1)} %pad_maximum_fusion.tie.spread.y0, ...), custom_call_target="tpu_custom_call" | custom-call | flops 6000000000 | bytes 18000000 | tf_op jit(solution)/shard_map/expert/pallas_call | solution.py:640
  243.6 2.9 add_convert_fusion
  250.2 13.2 %collective-permute-done.35.t1 = bf16[128,2176]{1,0:T(8,128)(2,1)S(1)} collective-permute-done((bf16[128,2176]{1,0:T(8,128)(2,1)S(1)}, bf16[128,2176]{1,0:T(8,128)(2,1)S(1)}, u32[]{:S(2)}, u32[]{:S(2)}) %collective-permute-start.35) | collective-permute-done | bytes 557088 | tf_op jit(solution)/shard_map/ppermute | solution.py:54
  263.3 2.8 collective-permute-done.36.t2
  266.2 11.0 %collective-permute-done.37.t3 = bf16[128,2176]{1,0:T(8,128)(2,1)S(1)} collective-permute-done((bf16[128,2176]{1,0:T(8,128)(2,1)S(1)}, bf16[128,2176]{1,0:T(8,128)(2,1)S(1)}, u32[]{:S(2)}, u32[]{:S(2)}) %collective-permute-start.37) | collective-permute-done | bytes 557088 | tf_op jit(solution)/shard_map/ppermute | solution.py:54
  277.2 10.2 %expert_grad.1 = bf16[2048,1336]{1,0:T(8,128)(2,1)} custom-call(bf16[512,2048]{1,0:T(8,128)(2,1)} %constant_dynamic-update-slice_fusion.15.far.x0, bf16[512,2048]{1,0:T(8,128)(2,1)} %collective-permute-done.31.far.x1, bf16[512,2176]{1,0:T(8,128)(2,1)} %pad_maximum_fusion.tie.spread.y0, bf16[512,2176]{1,0:T(8,128)(2,1)} %collective-permute-done.32.spread.y1, ...), custom_call_target="tpu_custom_call" | custom-call | flops 6000000000 | bytes 18000000 | tf_op jit(solution)/shard_map/expert_grad/pallas_call | solution.py:669
  290.0 4.3 collective-permute-done.33.other
  303.4 2.0 collective-permute-start.45
  307.2 3.9 collective-permute-done.45.a1
  311.1 2.1 collective-permute-start.47
  313.3 4.5 collective-permute-done.47.a3
  317.8 2.3 middle_back.1
  322.2 3.0 collective-permute-start.49
  326.9 2.6 out_rows.1.tie
  332.0 15.9 %attend_back.1 = (bf16[128,512]{1,0:T(8,128)(2,1)}, bf16[128,256]{1,0:T(8,128)(2,1)}, bf16[2048,1024]{1,0:T(8,128)(2,1)}, bf16[128,2048]{1,0:T(8,128)(2,1)}, bf1...) custom-call(s32[4]{0:T(128)} %copy-done.49, ...), custom_call_target="tpu_custom_call" | custom-call | flops 8000000000 | bytes 30000000 | tf_op jit(solution)/shard_map/attend_back/pallas_call | solution.py:549
  347.9 2.8 collective-permute-start.51
  353.3 3.4 collective-permute-start.43
  356.7 7.7 %collective-permute-done.42.rest_3_ = bf16[128,2048]{1,0:T(8,128)(2,1)S(1)} collective-permute-done((bf16[128,2048]{1,0:T(8,128)(2,1)S(1)}, bf16[128,2048]{1,0:T(8,128)(2,1)S(1)}, u32[]{:S(2)}, u32[]{:S(2)}) %collective-permute-start.42) | collective-permute-done | bytes 524320 | tf_op jit(solution)/shard_map/ppermute | solution.py:54
  365.8 4.2 collective-permute-done.52.rest_1_
  370.1 11.0 %collective-permute-done.53.rest_2_ = bf16[512,640]{1,0:T(8,128)(2,1)S(1)} collective-permute-done((bf16[512,640]{1,0:T(8,128)(2,1)}, bf16[512,640]{1,0:T(8,128)(2,1)S(1)}, u32[]{:S(2)}, u32[]{:S(2)}) %collective-permute-start.53) | collective-permute-done | bytes 655392 | tf_op jit(solution)/shard_map/ppermute | solution.py:54
  383.8 9.4 %attn_grad.1 = bf16[2048,1536]{1,0:T(8,128)(2,1)} custom-call(bf16[128,2048]{1,0:T(8,128)(2,1)S(1)} %get-tuple-element.80.normed, bf16[128,512]{1,0:T(8,128)(2,1)S(1)} %copy-done.46, bf16[128,256]{1,0:T(8,128)(2,1)S(1)} %copy-done.53, bf16[128,2048]{1,0:T(8,128)(2,1)S(1)} %copy-done.34, bf16[128,512]{1,0:T(8,128)(2,1)S(1)} %copy-done.45, ...), custom_call_target="tpu_custom_call" | custom-call | flops 4000000000 | bytes 15000000 | tf_op jit(solution)/shard_map/attn_grad/pallas_call | solution.py:703
  401.7 3.2 collective-permute-start.54
  406.6 4.4 collective-permute-done.54.tie
  416.3 2.6 cut.1
  420.1 2.3 collective-permute-start.62
  423.5 2.6 collective-permute-start.64
  426.2 11.7 %collective-permute-done.60.p1 = bf16[128,1336]{1,0:T(8,128)(2,1)S(1)} collective-permute-done((bf16[128,1336]{1,0:T(8,128)(2,1)}, bf16[128,1336]{1,0:T(8,128)(2,1)S(1)}, u32[]{:S(2)}, u32[]{:S(2)}) %collective-permute-start.60) | collective-permute-done | bytes 342048 | tf_op jit(solution)/shard_map/ppermute | solution.py:54
  443.4 2.5 by_core.1
  450.3 2.8 collective-permute-start.71
  454.2 2.3 token_back.1
  457.7 6.0 %collective-permute-done.66 = bf16[32,2048]{1,0:T(8,128)(2,1)S(1)} collective-permute-done((bf16[32,2048]{1,0:T(8,128)(2,1)S(1)}, bf16[32,2048]{1,0:T(8,128)(2,1)S(1)}, u32[]{:S(2)}, u32[]{:S(2)}) %collective-permute-start.66) | collective-permute-done | bytes 131104 | tf_op jit(solution)/shard_map/ppermute | solution.py:54
  464.2 2.4 collective-permute-start.68
  466.6 3.2 unpack.1
  481.0 6.6 %collective-permute-done.75 = bf16[4,64,256]{2,1,0:T(8,128)(2,1)S(1)} collective-permute-done((bf16[4,64,256]{2,1,0:T(8,128)(2,1)S(1)}, bf16[4,64,256]{2,1,0:T(8,128)(2,1)S(1)}, u32[]{:S(2)}, u32[]{:S(2)}) %collective-permute-start.75) | collective-permute-done | bytes 131104 | tf_op jit(solution)/shard_map/ppermute | solution.py:54
  495.8 2.9 collective-permute-start.82
  (439 shorter events, 151.0 us)
Async XLA Ops:
  7.2 136.3 %all-gather.3.cloned.1.call-start = ((), (), s32[]{:S(2)}) async-start(), calls=%async_computation.2 | async-start | bytes 6488064 | tf_op jit(solution)/shard_map/all_gather | solution.py:977
  10.9 201.2 %all-gather.5.cloned.1.call-start = ((), (), s32[]{:S(2)}) async-start(), calls=%async_computation.3 | async-start | bytes 7208960 | tf_op jit(solution)/shard_map/all_gather | solution.py:1050
  15.1 20.3 %collective-permute-start.1 = (bf16[64,640]{1,0:T(8,128)(2,1)S(1)}, bf16[64,640]{1,0:T(8,128)(2,1)S(1)}, u32[]{:S(2)}, u32[]{:S(2)}) collective-permute-start(bf16[64,640]{1,0:T(8,128)(2,1)S(1)} %concatenate.68), channel_id=1, source_target_pairs={{0,32},{32,64},{64,96},{96,0},{1,33},{33,65},{65,97},{97,1},{2,34}... | collective-permute-start | bytes 245768 | tf_op jit(solution)/shard_map/ppermute | solution.py:54
  16.7 18.6 %collective-permute-start.2 = (bf16[64,640]{1,0:T(8,128)(2,1)S(1)}, bf16[64,640]{1,0:T(8,128)(2,1)S(1)}, u32[]{:S(2)}, u32[]{:S(2)}) collective-permute-start(bf16[64,640]{1,0:T(8,128)(2,1)S(1)} %concatenate.68), channel_id=1, source_target_pairs={{0,64},{32,96},{64,0},{96,32},{1,65},{33,97},{65,1},{97,33},{2,66}... | collective-permute-start | bytes 245768 | tf_op jit(solution)/shard_map/ppermute | solution.py:54
  19.4 15.9 %collective-permute-start.3 = (bf16[64,640]{1,0:T(8,128)(2,1)S(1)}, bf16[64,640]{1,0:T(8,128)(2,1)}, u32[]{:S(2)}, u32[]{:S(2)}) collective-permute-start(bf16[64,640]{1,0:T(8,128)(2,1)S(1)} %concatenate.68), channel_id=1, source_target_pairs={{0,96},{32,0},{64,32},{96,64},{1,97},{33,1},{65,33},{97,65},{2,98}... | collective-permute-start | bytes 245768 | tf_op jit(solution)/shard_map/ppermute | solution.py:54
  29.9 14.6 %collective-permute-start.27 = (bf16[4,64,1336]{2,1,0:T(8,128)(2,1)}, bf16[4,64,1336]{2,1,0:T(8,128)(2,1)}, u32[]{:S(2)}, u32[]{:S(2)}) collective-permute-start(bf16[4,64,1336]{2,1,0:T(8,128)(2,1)} %bitcast.181), channel_id=1, source_target_pairs={{0,4},{4,0},{1,5},{5,1},{2,6},{6,2},{3,7},{7,3},{8,12},{12,8},{9,1... | collective-permute-start | bytes 2052104 | tf_op jit(solution)/shard_map/ppermute | solution.py:54
  30.9 57.5 %collective-permute-start = (bf16[64,2048]{1,0:T(8,128)(2,1)}, bf16[64,2048]{1,0:T(8,128)(2,1)}, u32[]{:S(2)}, u32[]{:S(2)}) collective-permute-start(bf16[64,2048]{1,0:T(8,128)(2,1)} %dynamic-slice_bitcast_fusion.3), channel_id=1, source_target_pairs={{0,4},{4,0},{1,5},{5,1},{2,6},{6,2},{3,7},{7,3},{8,12},{12,8},{9,1... | collective-permute-start | bytes 786440 | tf_op jit(solution)/shard_map/ppermute | solution.py:54
  37.0 14.7 %collective-permute-start.4 = (bf16[256,640]{1,0:T(8,128)(2,1)}, bf16[256,640]{1,0:T(8,128)(2,1)}, u32[]{:S(2)}, u32[]{:S(2)}) collective-permute-start(bf16[256,640]{1,0:T(8,128)(2,1)} %pad_maximum_fusion.5), channel_id=1, source_target_pairs={{0,8},{8,16},{16,24},{24,0},{1,9},{9,17},{17,25},{25,1},{2,10},{10... | collective-permute-start | bytes 983048 | tf_op jit(solution)/shard_map/ppermute | solution.py:54
  38.9 29.2 %collective-permute-start.5 = (bf16[256,640]{1,0:T(8,128)(2,1)}, bf16[256,640]{1,0:T(8,128)(2,1)}, u32[]{:S(2)}, u32[]{:S(2)}) collective-permute-start(bf16[256,640]{1,0:T(8,128)(2,1)} %pad_maximum_fusion.5), channel_id=1, source_target_pairs={{0,16},{8,24},{16,0},{24,8},{1,17},{9,25},{17,1},{25,9},{2,18},{10... | collective-permute-start | bytes 983048 | tf_op jit(solution)/shard_map/ppermute | solution.py:54
  42.5 26.7 %collective-permute-start.6 = (bf16[256,640]{1,0:T(8,128)(2,1)}, bf16[256,640]{1,0:T(8,128)(2,1)}, u32[]{:S(2)}, u32[]{:S(2)}) collective-permute-start(bf16[256,640]{1,0:T(8,128)(2,1)} %pad_maximum_fusion.5), channel_id=1, source_target_pairs={{0,24},{8,0},{16,8},{24,16},{1,25},{9,1},{17,9},{25,17},{2,26},{10... | collective-permute-start | bytes 983048 | tf_op jit(solution)/shard_map/ppermute | solution.py:54
  44.5 71.6 %collective-permute-start.17 = (bf16[64,2176]{1,0:T(8,128)(2,1)}, bf16[64,2176]{1,0:T(8,128)(2,1)}, u32[]{:S(2)}, u32[]{:S(2)}) collective-permute-start(bf16[64,2176]{1,0:T(8,128)(2,1)} %dynamic-slice_bitcast_fusion), channel_id=1, source_target_pairs={{0,4},{4,0},{1,5},{5,1},{2,6},{6,2},{3,7},{7,3},{8,12},{12,8},{9,1... | collective-permute-start | bytes 835592 | tf_op jit(solution)/shard_map/ppermute | solution.py:54
  51.7 18.8 %collective-permute-start.28 = (bf16[128,1336]{1,0:T(8,128)(2,1)}, bf16[128,1336]{1,0:T(8,128)(2,1)S(1)}, u32[]{:S(2)}, u32[]{:S(2)}) collective-permute-start(bf16[128,1336]{1,0:T(8,128)(2,1)} %get-tuple-element.191), channel_id=1, source_target_pairs={{0,32},{32,64},{64,96},{96,0},{1,33},{33,65},{65,97},{97,1},{2,34}... | collective-permute-start | bytes 1026056 | tf_op jit(solution)/shard_map/ppermute | solution.py:54
  70.3 19.3 %collective-permute-start.7 = (bf16[1024,640]{1,0:T(8,128)(2,1)S(1)}, bf16[1024,640]{1,0:T(8,128)(2,1)S(1)}, u32[]{:S(2)}, u32[]{:S(2)}) collective-permute-start(bf16[1024,640]{1,0:T(8,128)(2,1)S(1)} %constant_dynamic-update-slice_fusion.mine), channel_id=1, source_target_pairs={{0,4},{4,0},{1,5},{5,1},{2,6},{6,2},{3,7},{7,3},{8,12},{12,8},{9,1... | collective-permute-start | bytes 3932168 | tf_op jit(solution)/shard_map/ppermute | solution.py:54
  70.4 12.3 %collective-permute-start.29 = (bf16[128,1336]{1,0:T(8,128)(2,1)S(1)}, bf16[128,1336]{1,0:T(8,128)(2,1)S(1)}, u32[]{:S(2)}, u32[]{:S(2)}) collective-permute-start(bf16[128,1336]{1,0:T(8,128)(2,1)S(1)} %copy-done.77), channel_id=1, source_target_pairs={{0,64},{32,96},{64,0},{96,32},{1,65},{33,97},{65,1},{97,33},{2,66}... | collective-permute-start | bytes 1026056 | tf_op jit(solution)/shard_map/ppermute | solution.py:54
  70.5 16.4 %collective-permute-start.30 = (bf16[128,1336]{1,0:T(8,128)(2,1)S(1)}, bf16[128,1336]{1,0:T(8,128)(2,1)S(1)}, u32[]{:S(2)}, u32[]{:S(2)}) collective-permute-start(bf16[128,1336]{1,0:T(8,128)(2,1)S(1)} %get-tuple-element.195), channel_id=1, source_target_pairs={{0,96},{32,0},{64,32},{96,64},{1,97},{33,1},{65,33},{97,65},{2,98}... | collective-permute-start | bytes 1026056 | tf_op jit(solution)/shard_map/ppermute | solution.py:54
  87.7 328.6 %reduce-scatter.3.cloned.1.call-start = ((), (), s32[]{:S(2)}) async-start(), calls=%async_computation.4 | async-start | bytes 7208960 | tf_op jit(solution)/shard_map/reduce_scatter | solution.py:1085
  93.7 10.7 %collective-permute-start.8 = (bf16[128,640]{1,0:T(8,128)(2,1)S(1)}, bf16[128,640]{1,0:T(8,128)(2,1)S(1)}, u32[]{:S(2)}, u32[]{:S(2)}) collective-permute-start(bf16[128,640]{1,0:T(8,128)(2,1)S(1)} %get-tuple-element.81), channel_id=1, source_target_pairs={{0,8},{8,16},{16,24},{24,0},{1,9},{9,17},{17,25},{25,1},{2,10},{10... | collective-permute-start | bytes 491528 | tf_op jit(solution)/shard_map/ppermute | solution.py:54
  93.8 11.2 %collective-permute-start.9 = (bf16[128,640]{1,0:T(8,128)(2,1)S(1)}, bf16[128,640]{1,0:T(8,128)(2,1)S(1)}, u32[]{:S(2)}, u32[]{:S(2)}) collective-permute-start(bf16[128,640]{1,0:T(8,128)(2,1)S(1)} %get-tuple-element.81), channel_id=1, source_target_pairs={{0,16},{8,24},{16,0},{24,8},{1,17},{9,25},{17,1},{25,9},{2,18},{10... | collective-permute-start | bytes 491528 | tf_op jit(solution)/shard_map/ppermute | solution.py:54
  96.9 10.5 %collective-permute-start.10 = (bf16[128,640]{1,0:T(8,128)(2,1)S(1)}, bf16[128,640]{1,0:T(8,128)(2,1)S(1)}, u32[]{:S(2)}, u32[]{:S(2)}) collective-permute-start(bf16[128,640]{1,0:T(8,128)(2,1)S(1)} %get-tuple-element.81), channel_id=1, source_target_pairs={{0,24},{8,0},{16,8},{24,16},{1,25},{9,1},{17,9},{25,17},{2,26},{10... | collective-permute-start | bytes 491528 | tf_op jit(solution)/shard_map/ppermute | solution.py:54
  108.0 21.0 %collective-permute-start.11 = (bf16[512,640]{1,0:T(8,128)(2,1)}, bf16[512,640]{1,0:T(8,128)(2,1)}, u32[]{:S(2)}, u32[]{:S(2)}) collective-permute-start(bf16[512,640]{1,0:T(8,128)(2,1)} %constant_dynamic-update-slice_fusion.7.l0), channel_id=1, source_target_pairs={{0,32},{32,64},{64,96},{96,0},{1,33},{33,65},{65,97},{97,1},{2,34}... | collective-permute-start | bytes 1966088 | tf_op jit(solution)/shard_map/ppermute | solution.py:54
  113.5 29.6 %collective-permute-start.12 = (bf16[512,640]{1,0:T(8,128)(2,1)}, bf16[512,640]{1,0:T(8,128)(2,1)}, u32[]{:S(2)}, u32[]{:S(2)}) collective-permute-start(bf16[512,640]{1,0:T(8,128)(2,1)} %constant_dynamic-update-slice_fusion.7.l0), channel_id=1, source_target_pairs={{0,64},{32,96},{64,0},{96,32},{1,65},{33,97},{65,1},{97,33},{2,66}... | collective-permute-start | bytes 1966088 | tf_op jit(solution)/shard_map/ppermute | solution.py:54
  113.5 30.1 %collective-permute-start.13 = (bf16[512,640]{1,0:T(8,128)(2,1)}, bf16[512,640]{1,0:T(8,128)(2,1)}, u32[]{:S(2)}, u32[]{:S(2)}) collective-permute-start(bf16[512,640]{1,0:T(8,128)(2,1)} %constant_dynamic-update-slice_fusion.7.l0), channel_id=1, source_target_pairs={{0,96},{32,0},{64,32},{96,64},{1,97},{33,1},{65,33},{97,65},{2,98}... | collective-permute-start | bytes 1966088 | tf_op jit(solution)/shard_map/ppermute | solution.py:54
  130.9 34.4 %collective-permute-start.18 = (bf16[128,2176]{1,0:T(8,128)(2,1)}, bf16[128,2176]{1,0:T(8,128)(2,1)}, u32[]{:S(2)}, u32[]{:S(2)}) collective-permute-start(bf16[128,2176]{1,0:T(8,128)(2,1)} %turn.1), channel_id=1, source_target_pairs={{0,32},{32,64},{64,96},{96,0},{1,33},{33,65},{65,97},{97,1},{2,34}... | collective-permute-start | bytes 1671176 | tf_op jit(solution)/shard_map/ppermute | solution.py:54
  133.4 33.0 %collective-permute-start.19 = (bf16[128,2176]{1,0:T(8,128)(2,1)}, bf16[128,2176]{1,0:T(8,128)(2,1)}, u32[]{:S(2)}, u32[]{:S(2)}) collective-permute-start(bf16[128,2176]{1,0:T(8,128)(2,1)} %turn.1), channel_id=1, source_target_pairs={{0,64},{32,96},{64,0},{96,32},{1,65},{33,97},{65,1},{97,33},{2,66}... | collective-permute-start | bytes 1671176 | tf_op jit(solution)/shard_map/ppermute | solution.py:54
  133.4 33.0 %collective-permute-start.20 = (bf16[128,2176]{1,0:T(8,128)(2,1)}, bf16[128,2176]{1,0:T(8,128)(2,1)}, u32[]{:S(2)}, u32[]{:S(2)}) collective-permute-start(bf16[128,2176]{1,0:T(8,128)(2,1)} %turn.1), channel_id=1, source_target_pairs={{0,96},{32,0},{64,32},{96,64},{1,97},{33,1},{65,33},{97,65},{2,98}... | collective-permute-start | bytes 1671176 | tf_op jit(solution)/shard_map/ppermute | solution.py:54
  159.9 9.5 %collective-permute-start.14 = (bf16[32,2048]{1,0:T(8,128)(2,1)S(1)}, bf16[32,2048]{1,0:T(8,128)(2,1)S(1)}, u32[]{:S(2)}, u32[]{:S(2)}) collective-permute-start(bf16[32,2048]{1,0:T(8,128)(2,1)S(1)} %get-tuple-element.83), channel_id=1, source_target_pairs={{0,1},{1,2},{2,3},{3,0},{4,5},{5,6},{6,7},{7,4},{8,9},{9,10},{10,1... | collective-permute-start | bytes 393224 | tf_op jit(solution)/shard_map/ppermute | solution.py:54
  183.2 16.6 %collective-permute-start.24 = (bf16[128,2048]{1,0:T(8,128)(2,1)S(1)}, bf16[128,2048]{1,0:T(8,128)(2,1)S(1)}, u32[]{:S(2)}, u32[]{:S(2)}) collective-permute-start(bf16[128,2048]{1,0:T(8,128)(2,1)S(1)} %get-tuple-element.234), channel_id=1, source_target_pairs={{0,32},{32,64},{64,96},{96,0},{1,33},{33,65},{65,97},{97,1},{2,34}... | collective-permute-start | bytes 1572872 | tf_op jit(solution)/shard_map/ppermute | solution.py:54
  192.2 18.2 %collective-permute-start.25 = (bf16[128,2048]{1,0:T(8,128)(2,1)S(1)}, bf16[128,2048]{1,0:T(8,128)(2,1)S(1)}, u32[]{:S(2)}, u32[]{:S(2)}) collective-permute-start(bf16[128,2048]{1,0:T(8,128)(2,1)S(1)} %get-tuple-element.234), channel_id=1, source_target_pairs={{0,64},{32,96},{64,0},{96,32},{1,65},{33,97},{65,1},{97,33},{2,66}... | collective-permute-start | bytes 1572872 | tf_op jit(solution)/shard_map/ppermute | solution.py:54
  192.2 19.1 %collective-permute-start.26 = (bf16[128,2048]{1,0:T(8,128)(2,1)S(1)}, bf16[128,2048]{1,0:T(8,128)(2,1)S(1)}, u32[]{:S(2)}, u32[]{:S(2)}) collective-permute-start(bf16[128,2048]{1,0:T(8,128)(2,1)S(1)} %get-tuple-element.234), channel_id=1, source_target_pairs={{0,96},{32,0},{64,32},{96,64},{1,97},{33,1},{65,33},{97,65},{2,98}... | collective-permute-start | bytes 1572872 | tf_op jit(solution)/shard_map/ppermute | solution.py:54
  194.9 17.3 %collective-permute-start.32 = (bf16[512,2176]{1,0:T(8,128)(2,1)}, bf16[512,2176]{1,0:T(8,128)(2,1)}, u32[]{:S(2)}, u32[]{:S(2)}) collective-permute-start(bf16[512,2176]{1,0:T(8,128)(2,1)} %pad_maximum_fusion.tie.spread.y0), channel_id=1, source_target_pairs={{0,4},{4,0},{1,5},{5,1},{2,6},{6,2},{3,7},{7,3},{8,12},{12,8},{9,1... | collective-permute-start | bytes 6684680 | tf_op jit(solution)/shard_map/ppermute | solution.py:54
  230.7 12.9 %collective-permute-start.34 = (bf16[512,2176]{1,0:T(8,128)(2,1)}, bf16[512,2176]{1,0:T(8,128)(2,1)S(1)}, u32[]{:S(2)}, u32[]{:S(2)}) collective-permute-start(bf16[512,2176]{1,0:T(8,128)(2,1)} %get-tuple-element.96), channel_id=1, source_target_pairs={{0,4},{4,0},{1,5},{5,1},{2,6},{6,2},{3,7},{7,3},{8,12},{12,8},{9,1... | collective-permute-start | bytes 6684680 | tf_op jit(solution)/shard_map/ppermute | solution.py:54
  247.9 15.5 %collective-permute-start.35 = (bf16[128,2176]{1,0:T(8,128)(2,1)S(1)}, bf16[128,2176]{1,0:T(8,128)(2,1)S(1)}, u32[]{:S(2)}, u32[]{:S(2)}) collective-permute-start(bf16[128,2176]{1,0:T(8,128)(2,1)S(1)} %get-tuple-element.204), channel_id=1, source_target_pairs={{0,96},{32,0},{64,32},{96,64},{1,97},{33,1},{65,33},{97,65},{2,98}... | collective-permute-start | bytes 1671176 | tf_op jit(solution)/shard_map/ppermute | solution.py:54
  249.1 17.0 %collective-permute-start.36 = (bf16[128,2176]{1,0:T(8,128)(2,1)S(1)}, bf16[128,2176]{1,0:T(8,128)(2,1)S(1)}, u32[]{:S(2)}, u32[]{:S(2)}) collective-permute-start(bf16[128,2176]{1,0:T(8,128)(2,1)S(1)} %get-tuple-element.203), channel_id=1, source_target_pairs={{0,64},{32,96},{64,0},{96,32},{1,65},{33,97},{65,1},{97,33},{2,66}... | collective-permute-start | bytes 1671176 | tf_op jit(solution)/shard_map/ppermute | solution.py:54
  249.1 28.0 %collective-permute-start.37 = (bf16[128,2176]{1,0:T(8,128)(2,1)S(1)}, bf16[128,2176]{1,0:T(8,128)(2,1)S(1)}, u32[]{:S(2)}, u32[]{:S(2)}) collective-permute-start(bf16[128,2176]{1,0:T(8,128)(2,1)S(1)} %get-tuple-element.202), channel_id=1, source_target_pairs={{0,32},{32,64},{64,96},{96,0},{1,33},{33,65},{65,97},{97,1},{2,34}... | collective-permute-start | bytes 1671176 | tf_op jit(solution)/shard_map/ppermute | solution.py:54
  289.9 215.1 %reduce-scatter.5.cloned.1.call-start = ((), (), s32[]{:S(2)}) async-start(), calls=%async_computation.5 | async-start | bytes 6488064 | tf_op jit(solution)/shard_map/reduce_scatter | solution.py:1121
  299.9 25.2 %collective-permute-start.38 = (bf16[128,2048]{1,0:T(8,128)(2,1)S(1)}, bf16[128,2048]{1,0:T(8,128)(2,1)S(1)}, u32[]{:S(2)}, u32[]{:S(2)}) collective-permute-start(bf16[128,2048]{1,0:T(8,128)(2,1)S(1)} %get-tuple-element.98), channel_id=1, source_target_pairs={{0,96},{32,0},{64,32},{96,64},{1,97},{33,1},{65,33},{97,65},{2,98}... | collective-permute-start | bytes 1572872 | tf_op jit(solution)/shard_map/ppermute | solution.py:54
  300.4 24.9 %collective-permute-start.39 = (bf16[128,2048]{1,0:T(8,128)(2,1)S(1)}, bf16[128,2048]{1,0:T(8,128)(2,1)S(1)}, u32[]{:S(2)}, u32[]{:S(2)}) collective-permute-start(bf16[128,2048]{1,0:T(8,128)(2,1)S(1)} %get-tuple-element.99), channel_id=1, source_target_pairs={{0,64},{32,96},{64,0},{96,32},{1,65},{33,97},{65,1},{97,33},{2,66}... | collective-permute-start | bytes 1572872 | tf_op jit(solution)/shard_map/ppermute | solution.py:54
  300.6 26.3 %collective-permute-start.40 = (bf16[128,2048]{1,0:T(8,128)(2,1)S(1)}, bf16[128,2048]{1,0:T(8,128)(2,1)}, u32[]{:S(2)}, u32[]{:S(2)}) collective-permute-start(bf16[128,2048]{1,0:T(8,128)(2,1)S(1)} %get-tuple-element.100), channel_id=1, source_target_pairs={{0,32},{32,64},{64,96},{96,0},{1,33},{33,65},{65,97},{97,1},{2,34}... | collective-permute-start | bytes 1572872 | tf_op jit(solution)/shard_map/ppermute | solution.py:54
  321.6 9.7 %collective-permute-start.48 = (bf16[32,2048]{1,0:T(8,128)(2,1)}, bf16[32,2048]{1,0:T(8,128)(2,1)S(1)}, u32[]{:S(2)}, u32[]{:S(2)}) collective-permute-start(bf16[32,2048]{1,0:T(8,128)(2,1)} %get-tuple-element.102.d0), channel_id=1, source_target_pairs={{0,1},{1,2},{2,3},{3,0},{4,5},{5,6},{6,7},{7,4},{8,9},{9,10},{10,1... | collective-permute-start | bytes 393224 | tf_op jit(solution)/shard_map/ppermute | solution.py:54
  322.2 9.2 %collective-permute-start.49 = (bf16[32,2048]{1,0:T(8,128)(2,1)}, bf16[32,2048]{1,0:T(8,128)(2,1)S(1)}, u32[]{:S(2)}, u32[]{:S(2)}) collective-permute-start(bf16[32,2048]{1,0:T(8,128)(2,1)} %get-tuple-element.102.d0), channel_id=1, source_target_pairs={{0,2},{1,3},{2,0},{3,1},{4,6},{5,7},{6,4},{7,5},{8,10},{9,11},{10,... | collective-permute-start | bytes 393224 | tf_op jit(solution)/shard_map/ppermute | solution.py:54
  329.6 23.8 %collective-permute-start.41 = (bf16[128,2048]{1,0:T(8,128)(2,1)}, bf16[128,2048]{1,0:T(8,128)(2,1)S(1)}, u32[]{:S(2)}, u32[]{:S(2)}) collective-permute-start(bf16[128,2048]{1,0:T(8,128)(2,1)} %out_rows.1.tie), channel_id=1, source_target_pairs={{0,2},{1,3},{2,0},{3,1},{4,6},{5,7},{6,4},{7,5},{8,10},{9,11},{10,... | collective-permute-start | bytes 1572872 | tf_op jit(solution)/shard_map/ppermute | solution.py:54
  347.9 17.9 %collective-permute-start.51 = (bf16[512,640]{1,0:T(8,128)(2,1)}, bf16[512,640]{1,0:T(8,128)(2,1)S(1)}, u32[]{:S(2)}, u32[]{:S(2)}) collective-permute-start(bf16[512,640]{1,0:T(8,128)(2,1)} %get-tuple-element.108), channel_id=1, source_target_pairs={{0,96},{32,0},{64,32},{96,64},{1,97},{33,1},{65,33},{97,65},{2,98}... | collective-permute-start | bytes 1966088 | tf_op jit(solution)/shard_map/ppermute | solution.py:54
  350.7 19.4 %collective-permute-start.52 = (bf16[512,640]{1,0:T(8,128)(2,1)}, bf16[512,640]{1,0:T(8,128)(2,1)S(1)}, u32[]{:S(2)}, u32[]{:S(2)}) collective-permute-start(bf16[512,640]{1,0:T(8,128)(2,1)} %get-tuple-element.109), channel_id=1, source_target_pairs={{0,64},{32,96},{64,0},{96,32},{1,65},{33,97},{65,1},{97,33},{2,66}... | collective-permute-start | bytes 1966088 | tf_op jit(solution)/shard_map/ppermute | solution.py:54
  352.0 29.1 %collective-permute-start.53 = (bf16[512,640]{1,0:T(8,128)(2,1)}, bf16[512,640]{1,0:T(8,128)(2,1)S(1)}, u32[]{:S(2)}, u32[]{:S(2)}) collective-permute-start(bf16[512,640]{1,0:T(8,128)(2,1)} %get-tuple-element.110), channel_id=1, source_target_pairs={{0,32},{32,64},{64,96},{96,0},{1,33},{33,65},{65,97},{97,1},{2,34}... | collective-permute-start | bytes 1966088 | tf_op jit(solution)/shard_map/ppermute | solution.py:54
  353.3 11.1 %collective-permute-start.42 = (bf16[128,2048]{1,0:T(8,128)(2,1)S(1)}, bf16[128,2048]{1,0:T(8,128)(2,1)S(1)}, u32[]{:S(2)}, u32[]{:S(2)}) collective-permute-start(bf16[128,2048]{1,0:T(8,128)(2,1)S(1)} %copy-done.61), channel_id=1, source_target_pairs={{0,1},{1,2},{2,3},{3,0},{4,5},{5,6},{6,7},{7,4},{8,9},{9,10},{10,1... | collective-permute-start | bytes 1572872 | tf_op jit(solution)/shard_map/ppermute | solution.py:54
  353.3 11.1 %collective-permute-start.43 = (bf16[128,2048]{1,0:T(8,128)(2,1)S(1)}, bf16[128,2048]{1,0:T(8,128)(2,1)S(1)}, u32[]{:S(2)}, u32[]{:S(2)}) collective-permute-start(bf16[128,2048]{1,0:T(8,128)(2,1)S(1)} %copy-done.61), channel_id=1, source_target_pairs={{0,3},{1,0},{2,1},{3,2},{4,7},{5,4},{6,5},{7,6},{8,11},{9,8},{10,9... | collective-permute-start | bytes 1572872 | tf_op jit(solution)/shard_map/ppermute | solution.py:54
  398.3 54.9 %collective-permute-start.63 = (bf16[32,2048]{1,0:T(8,128)(2,1)}, bf16[32,2048]{1,0:T(8,128)(2,1)}, u32[]{:S(2)}, u32[]{:S(2)}) collective-permute-start(bf16[32,2048]{1,0:T(8,128)(2,1)} %get-tuple-element.123), channel_id=1, source_target_pairs={{0,1},{1,2},{2,3},{3,0},{4,5},{5,6},{6,7},{7,4},{8,9},{9,10},{10,1... | collective-permute-start | bytes 393224 | tf_op jit(solution)/shard_map/ppermute | solution.py:54
  401.7 9.2 %collective-permute-start.54 = (bf16[128,640]{1,0:T(8,128)(2,1)S(1)}, bf16[128,640]{1,0:T(8,128)(2,1)S(1)}, u32[]{:S(2)}, u32[]{:S(2)}) collective-permute-start(bf16[128,640]{1,0:T(8,128)(2,1)S(1)} %get-tuple-element.217), channel_id=1, source_target_pairs={{0,24},{8,0},{16,8},{24,16},{1,25},{9,1},{17,9},{25,17},{2,26},{10... | collective-permute-start | bytes 491528 | tf_op jit(solution)/shard_map/ppermute | solution.py:54
  404.9 9.5 %collective-permute-start.56 = (bf16[128,640]{1,0:T(8,128)(2,1)S(1)}, bf16[128,640]{1,0:T(8,128)(2,1)S(1)}, u32[]{:S(2)}, u32[]{:S(2)}) collective-permute-start(bf16[128,640]{1,0:T(8,128)(2,1)S(1)} %get-tuple-element.218), channel_id=1, source_target_pairs={{0,8},{8,16},{16,24},{24,0},{1,9},{9,17},{17,25},{25,1},{2,10},{10... | collective-permute-start | bytes 491528 | tf_op jit(solution)/shard_map/ppermute | solution.py:54
  406.6 13.5 %collective-permute-start.44 = (bf16[64,2048]{1,0:T(8,128)(2,1)}, bf16[64,2048]{1,0:T(8,128)(2,1)}, u32[]{:S(2)}, u32[]{:S(2)}) collective-permute-start(bf16[64,2048]{1,0:T(8,128)(2,1)} %dynamic-slice_bitcast_fusion.2), channel_id=1, source_target_pairs={{0,4},{4,0},{1,5},{5,1},{2,6},{6,2},{3,7},{7,3},{8,12},{12,8},{9,1... | collective-permute-start | bytes 786440 | tf_op jit(solution)/shard_map/ppermute | solution.py:54
  419.0 18.8 %collective-permute-start.60 = (bf16[128,1336]{1,0:T(8,128)(2,1)}, bf16[128,1336]{1,0:T(8,128)(2,1)S(1)}, u32[]{:S(2)}, u32[]{:S(2)}) collective-permute-start(bf16[128,1336]{1,0:T(8,128)(2,1)} %get-tuple-element.117), channel_id=1, source_target_pairs={{0,32},{32,64},{64,96},{96,0},{1,33},{33,65},{65,97},{97,1},{2,34}... | collective-permute-start | bytes 1026056 | tf_op jit(solution)/shard_map/ppermute | solution.py:54
  419.4 20.3 %collective-permute-start.61 = (bf16[128,1336]{1,0:T(8,128)(2,1)}, bf16[128,1336]{1,0:T(8,128)(2,1)S(1)}, u32[]{:S(2)}, u32[]{:S(2)}) collective-permute-start(bf16[128,1336]{1,0:T(8,128)(2,1)} %get-tuple-element.118), channel_id=1, source_target_pairs={{0,64},{32,96},{64,0},{96,32},{1,65},{33,97},{65,1},{97,33},{2,66}... | collective-permute-start | bytes 1026056 | tf_op jit(solution)/shard_map/ppermute | solution.py:54
  420.1 21.1 %collective-permute-start.62 = (bf16[128,1336]{1,0:T(8,128)(2,1)}, bf16[128,1336]{1,0:T(8,128)(2,1)S(1)}, u32[]{:S(2)}, u32[]{:S(2)}) collective-permute-start(bf16[128,1336]{1,0:T(8,128)(2,1)} %get-tuple-element.119), channel_id=1, source_target_pairs={{0,96},{32,0},{64,32},{96,64},{1,97},{33,1},{65,33},{97,65},{2,98}... | collective-permute-start | bytes 1026056 | tf_op jit(solution)/shard_map/ppermute | solution.py:54
  423.5 30.6 %collective-permute-start.64 = (bf16[32,2048]{1,0:T(8,128)(2,1)}, bf16[32,2048]{1,0:T(8,128)(2,1)}, u32[]{:S(2)}, u32[]{:S(2)}) collective-permute-start(bf16[32,2048]{1,0:T(8,128)(2,1)} %get-tuple-element.124), channel_id=1, source_target_pairs={{0,2},{1,3},{2,0},{3,1},{4,6},{5,7},{6,4},{7,5},{8,10},{9,11},{10,... | collective-permute-start | bytes 393224 | tf_op jit(solution)/shard_map/ppermute | solution.py:54
  437.8 16.3 %collective-permute-start.65 = (bf16[32,2048]{1,0:T(8,128)(2,1)}, bf16[32,2048]{1,0:T(8,128)(2,1)}, u32[]{:S(2)}, u32[]{:S(2)}) collective-permute-start(bf16[32,2048]{1,0:T(8,128)(2,1)} %get-tuple-element.125), channel_id=1, source_target_pairs={{0,3},{1,0},{2,1},{3,2},{4,7},{5,4},{6,5},{7,6},{8,11},{9,8},{10,9... | collective-permute-start | bytes 393224 | tf_op jit(solution)/shard_map/ppermute | solution.py:54
  449.6 20.3 %collective-permute-start.70 = (bf16[32,640]{1,0:T(8,128)(2,1)S(1)}, bf16[32,640]{1,0:T(8,128)(2,1)S(1)}, u32[]{:S(2)}, u32[]{:S(2)}) collective-permute-start(bf16[32,640]{1,0:T(8,128)(2,1)S(1)} %get-tuple-element.121.d_comp.c0), channel_id=1, source_target_pairs={{0,1},{1,2},{2,3},{3,0},{4,5},{5,6},{6,7},{7,4},{8,9},{9,10},{10,1... | collective-permute-start | bytes 122888 | tf_op jit(solution)/shard_map/ppermute | solution.py:54
  450.3 19.5 %collective-permute-start.71 = (bf16[32,640]{1,0:T(8,128)(2,1)S(1)}, bf16[32,640]{1,0:T(8,128)(2,1)S(1)}, u32[]{:S(2)}, u32[]{:S(2)}) collective-permute-start(bf16[32,640]{1,0:T(8,128)(2,1)S(1)} %get-tuple-element.121.d_comp.c0), channel_id=1, source_target_pairs={{0,2},{1,3},{2,0},{3,1},{4,6},{5,7},{6,4},{7,5},{8,10},{9,11},{10,... | collective-permute-start | bytes 122888 | tf_op jit(solution)/shard_map/ppermute | solution.py:54
  453.2 16.7 %collective-permute-start.72 = (bf16[32,640]{1,0:T(8,128)(2,1)S(1)}, bf16[32,640]{1,0:T(8,128)(2,1)S(1)}, u32[]{:S(2)}, u32[]{:S(2)}) collective-permute-start(bf16[32,640]{1,0:T(8,128)(2,1)S(1)} %get-tuple-element.121.d_comp.c0), channel_id=1, source_target_pairs={{0,3},{1,0},{2,1},{3,2},{4,7},{5,4},{6,5},{7,6},{8,11},{9,8},{10,9... | collective-permute-start | bytes 122888 | tf_op jit(solution)/shard_map/ppermute | solution.py:54
  454.1 10.0 %collective-permute-start.73 = (bf16[4,64,1336]{2,1,0:T(8,128)(2,1)}, bf16[4,64,1336]{2,1,0:T(8,128)(2,1)S(1)}, u32[]{:S(2)}, u32[]{:S(2)}) collective-permute-start(bf16[4,64,1336]{2,1,0:T(8,128)(2,1)} %get-tuple-element.131), channel_id=1, source_target_pairs={{0,4},{4,0},{1,5},{5,1},{2,6},{6,2},{3,7},{7,3},{8,12},{12,8},{9,1... | collective-permute-start | bytes 2052104 | tf_op jit(solution)/shard_map/ppermute | solution.py:54
  463.7 11.8 %collective-permute-start.67 = (bf16[32,2048]{1,0:T(8,128)(2,1)S(1)}, bf16[32,2048]{1,0:T(8,128)(2,1)S(1)}, u32[]{:S(2)}, u32[]{:S(2)}) collective-permute-start(bf16[32,2048]{1,0:T(8,128)(2,1)S(1)} %get-tuple-element.127), channel_id=1, source_target_pairs={{0,2},{1,3},{2,0},{3,1},{4,6},{5,7},{6,4},{7,5},{8,10},{9,11},{10,... | collective-permute-start | bytes 393224 | tf_op jit(solution)/shard_map/ppermute | solution.py:54
  464.2 11.4 %collective-permute-start.68 = (bf16[32,2048]{1,0:T(8,128)(2,1)S(1)}, bf16[32,2048]{1,0:T(8,128)(2,1)S(1)}, u32[]{:S(2)}, u32[]{:S(2)}) collective-permute-start(bf16[32,2048]{1,0:T(8,128)(2,1)S(1)} %get-tuple-element.127), channel_id=1, source_target_pairs={{0,3},{1,0},{2,1},{3,2},{4,7},{5,4},{6,5},{7,6},{8,11},{9,8},{10,9... | collective-permute-start | bytes 393224 | tf_op jit(solution)/shard_map/ppermute | solution.py:54
  477.6 10.0 %collective-permute-start.75 = (bf16[4,64,256]{2,1,0:T(8,128)(2,1)S(1)}, bf16[4,64,256]{2,1,0:T(8,128)(2,1)S(1)}, u32[]{:S(2)}, u32[]{:S(2)}) collective-permute-start(bf16[4,64,256]{2,1,0:T(8,128)(2,1)S(1)} %get-tuple-element.224), channel_id=1, source_target_pairs={{0,32},{32,64},{64,96},{96,0},{1,33},{33,65},{65,97},{97,1},{2,34}... | collective-permute-start | bytes 393224 | tf_op jit(solution)/shard_map/ppermute | solution.py:54
  477.7 9.9 %collective-permute-start.76 = (bf16[4,64,256]{2,1,0:T(8,128)(2,1)S(1)}, bf16[4,64,256]{2,1,0:T(8,128)(2,1)S(1)}, u32[]{:S(2)}, u32[]{:S(2)}) collective-permute-start(bf16[4,64,256]{2,1,0:T(8,128)(2,1)S(1)} %get-tuple-element.226), channel_id=1, source_target_pairs={{0,64},{32,96},{64,0},{96,32},{1,65},{33,97},{65,1},{97,33},{2,66}... | collective-permute-start | bytes 393224 | tf_op jit(solution)/shard_map/ppermute | solution.py:54
  481.0 10.4 %collective-permute-start.69 = (bf16[64,2048]{1,0:T(8,128)(2,1)S(1)}, bf16[64,2048]{1,0:T(8,128)(2,1)S(1)}, u32[]{:S(2)}, u32[]{:S(2)}) collective-permute-start(bf16[64,2048]{1,0:T(8,128)(2,1)S(1)} %dynamic-slice_bitcast_fusion.1), channel_id=1, source_target_pairs={{0,4},{4,0},{1,5},{5,1},{2,6},{6,2},{3,7},{7,3},{8,12},{12,8},{9,1... | collective-permute-start | bytes 786440 | tf_op jit(solution)/shard_map/ppermute | solution.py:54
  (114 other events, 981.9 us)
Sparse Core Ops, SparseCore 0:
  11.1 60.1 all-gather.2
  87.8 63.8 all-gather.4
  290.0 57.9 reduce-scatter.2
  398.3 85.5 reduce-scatter.4
